TPU v7x, 32 devices: a whole 2x2x4 slice. The times are simulated.
32 devices in a mesh: chan: 16 (over z, x, core), win: 2 (over y).
Axes of the slice: x: 2, y: 2, z: 4, core: 2. Of those that a mesh axis runs over, the one named last changes fastest.
Arguments:
- records: float32 [64, 16, 8192], P('chan', 'win'), may hold values from -80 to 80, as said below
- positions: int32 [64], replicated, may hold values from 0 to 7843, as said below
Outputs:
- stacks: float32 [4, 64, 4, 2, 4096], P(None, 'chan', None, None, 'win')
Inputs may be any that keep to these rules, and one draw needn't show every extreme that they name: `positions`: positions rise along the channels by 62 to 187 metres from one channel to the next; the first is 0. `records`: records of different channels and windows differ in scale.
All inputs are finite; a program needn't handle non-finite values.
Results may differ from a plain program's by a relative error of at most 0.004.
Values may be sent and summed in bfloat16 or wider, within the bound.
No kernel may reach another device: no remote copies, remote signals or barrier semaphores. Data moves between devices by JAX's collectives and lax.ppermute only.
A program may use at most 128 MiB of HBM per device.

v0:
```python
import functools
import math

import jax
import jax.numpy as jnp
from jax import lax
from jax.experimental import pallas as pl
from jax.experimental.pallas import tpu as pltpu
from jax.sharding import PartitionSpec as P

BINS = 4096
BAND = 128
ROUNDS = 4
REACH = 2000
LANES = 128
band_epsilon = 1e-06
VMEM = pl.BlockSpec(memory_space=pltpu.VMEM)
SMEM = pl.BlockSpec(memory_space=pltpu.SMEM)
HBM = pl.BlockSpec(memory_space=pltpu.HBM)
PARAMS = pltpu.CompilerParams(vmem_limit_bytes=40 * 1024 * 1024)


def cost(microseconds):
    return pl.CostEstimate(flops=int(microseconds * 1.1e9), bytes_accessed=0, transcendentals=0)


def split3(value):
    hi = value.astype(jnp.bfloat16)
    rest = value - hi.astype(jnp.float32)
    mid = rest.astype(jnp.bfloat16)
    lo = (rest - mid.astype(jnp.float32)).astype(jnp.bfloat16)
    return hi, mid, lo


def real_dft(values):
    n = len(values)
    if n == 2:
        return [(values[0] + values[1], None), (values[0] - values[1], None)]
    even, odd = real_dft(values[0::2]), real_dft(values[1::2])
    out = [None] * (n // 2 + 1)
    for k in range(n // 4 + 1):
        (er, ei), (dr, di) = even[k], odd[k]
        if k == 0:
            out[0] = (er + dr, None)
            out[n // 2] = (er - dr, None)
        elif 4 * k == n:
            out[k] = (er, -dr)
        else:
            c, s = math.cos(2.0 * math.pi * k / n), math.sin(2.0 * math.pi * k / n)
            tr = dr * c + di * s
            ti = di * c - dr * s
            out[k] = (er + tr, ei + ti)
            out[n // 2 - k] = (er - tr, ti - ei)
    return out


def spectra_channel(parts, chan, x, tw_ref, l2_ref, t_ref, outs):
    first = len(x)
    wins = x[0].shape[0]
    bands = BINS // BAND // parts
    terms = real_dft(x)
    for k in range(first):
        re, im = terms[min(k, first - k)]
        rows = pl.ds(k * wins, wins)
        cos, sin = tw_ref[0, pl.ds(k, 1), :], tw_ref[1, pl.ds(k, 1), :]
        if im is None:
            t_ref[chan, 0, rows, :] = re * cos
            t_ref[chan, 1, rows, :] = -(re * sin)
        elif 2 * k <= first:
            t_ref[chan, 0, rows, :] = re * cos + im * sin
            t_ref[chan, 1, rows, :] = im * cos - re * sin
        else:
            t_ref[chan, 0, rows, :] = re * cos - im * sin
            t_ref[chan, 1, rows, :] = -(im * cos + re * sin)
    rhs = []
    for win in range(wins):
        at = pl.ds(win, first, stride=wins)
        row = jnp.concatenate([t_ref[chan, 0, at, :], t_ref[chan, 1, at, :]], axis=1)
        hi, mid, lo = split3(row)
        rhs.append(jnp.concatenate([hi, mid, lo, hi, mid, hi], axis=1))
    spec = lax.dot_general(
        l2_ref[...],
        jnp.concatenate(rhs, axis=0),
        (((1,), (1,)), ((), ())),
        preferred_element_type=jnp.float32,
    )
    left = lax.broadcasted_iota(jnp.int32, (bands, LANES), 1) < first
    pairs = wins // 2
    tiles = [
        spec[:, i * LANES : (i + 1) * LANES].reshape(parts, 4, bands, LANES) for i in range(pairs)
    ]
    powers = []
    for tile in tiles:
        square = tile * tile
        power = square[:, 0] + square[:, 1] + square[:, 2] + square[:, 3]
        powers.append(power.reshape(parts * bands, LANES))
    row = lax.rem(lax.broadcasted_iota(jnp.int32, (3 * LANES, LANES), 0), LANES)
    lane = lax.broadcasted_iota(jnp.int32, (3 * LANES, LANES), 1)
    ones = ((row < first) == (lane < first)).astype(jnp.bfloat16)
    total = jnp.dot(
        jnp.concatenate(split3(jnp.concatenate(powers, axis=0)), axis=1),
        ones,
        preferred_element_type=jnp.float32,
    )
    scales = lax.rsqrt(total * (1.0 / BAND) + band_epsilon).reshape(pairs, parts, bands, LANES)
    for pair in range(pairs):
        for s in range(parts):
            scale = scales[pair, s]
            for imag in range(2):
                even = tiles[pair][s, 2 * imag] * scale
                odd = tiles[pair][s, 2 * imag + 1] * scale
                one = jnp.where(left, even, pltpu.roll(odd, first, 1)).astype(jnp.bfloat16)
                two = jnp.where(left, pltpu.roll(even, first, 1), odd).astype(jnp.bfloat16)
                at = pl.ds(imag * bands, bands)
                for out_ref, row in outs[s]:
                    out_ref[row, 2 * pair, at, :] = one
                    out_ref[row, 2 * pair + 1, at, :] = two


def turn_table(index, period):
    index = lax.rem(index, period)
    quarter = period // 4
    turn = lax.div(index + quarter // 2, quarter)
    angle = (index - turn * quarter).astype(jnp.float32) * (2.0 * math.pi / period)
    square = angle * angle

    def series(first):
        value = jnp.full_like(angle, 0.0)
        for power in range(10 + first, first - 1, -2):
            value = value * square + (-1) ** (power // 2) / math.factorial(power)
        return value

    cos, sin = series(0), series(1) * angle
    swap = lax.rem(turn, 2) == 1
    minus_cos = (turn == 1) | (turn == 2)
    minus_sin = (turn == 2) | (turn == 3)
    cos, sin = jnp.where(swap, sin, cos), jnp.where(swap, cos, sin)
    return jnp.where(minus_cos, -cos, cos), jnp.where(minus_sin, -sin, sin)


def tables_kernel(parts, samples, tw_ref, l2_ref):
    first = samples // LANES
    bands = BINS // BAND // parts
    me = lax.axis_index("win")
    k1 = lax.broadcasted_iota(jnp.int32, (first, LANES), 0)
    q = lax.broadcasted_iota(jnp.int32, (first, LANES), 1)
    tw_ref[0], tw_ref[1] = turn_table(k1 * q, samples)
    band = lax.broadcasted_iota(jnp.int32, (bands, LANES), 0)
    q = lax.broadcasted_iota(jnp.int32, (bands, LANES), 1)
    for s in range(parts):
        part = lax.rem(me + s, parts)
        tables = [turn_table((2 * (part * bands + band) + odd) * q, LANES) for odd in range(2)]
        rows = [jnp.concatenate([cos, sin], axis=1) for cos, sin in tables]
        rows += [jnp.concatenate([-sin, cos], axis=1) for cos, sin in tables]
        hi, mid, lo = split3(jnp.concatenate(rows, axis=0))
        table = jnp.concatenate([hi, hi, hi, mid, mid, lo], axis=1)
        l2_ref[pl.ds(s * 4 * bands, 4 * bands), :] = table


def spectra_kernel(parts, x_ref, tw_ref, l2_ref, *refs):
    low, high, whole, t_ref = (
        refs[:parts], refs[parts : 2 * parts], refs[2 * parts : 3 * parts - 1], refs[-1]
    )
    chans, first = x_ref.shape[:2]
    half = low[0].shape[0]
    for chan in range(chans):
        x = [x_ref[chan, p] for p in range(first)]
        chunk, row = (low, chan) if chan < half else (high, chan - half)
        targets = [[(out, row)] for out in chunk]
        for s in range(1, parts):
            targets[s].append((whole[s - 1], chan))
        spectra_channel(parts, chan, x, tw_ref, l2_ref, t_ref, targets)


def whitened_spectra(records, parts):
    chans, wins, samples = records.shape
    first = samples // LANES
    rows = 2 * (BINS // BAND // parts)
    x = records.reshape(chans, wins, first, LANES).transpose(0, 2, 1, 3)
    half = chans // 2

    def chunk(count):
        return jax.ShapeDtypeStruct((count, wins, rows, LANES), jnp.bfloat16)

    tables = pl.pallas_call(
        functools.partial(tables_kernel, parts, samples),
        out_specs=[VMEM] * 2,
        out_shape=[
            jax.ShapeDtypeStruct((2, first, LANES), jnp.float32),
            jax.ShapeDtypeStruct((2 * rows * parts, 12 * LANES), jnp.bfloat16),
        ],
        compiler_params=PARAMS,
        cost_estimate=cost(1),
        name="tables",
    )()
    out = pl.pallas_call(
        functools.partial(spectra_kernel, parts),
        in_specs=[VMEM] * 3,
        out_specs=[VMEM] * (3 * parts - 1),
        out_shape=[chunk(half)] * parts + [chunk(chans - half)] * parts + [chunk(chans)] * (parts - 1),
        scratch_shapes=[pltpu.VMEM((chans, 2, first * wins, LANES), jnp.float32)],
        compiler_params=PARAMS,
        cost_estimate=cost(4),
        name="spectra",
    )(x, *tables)
    return out[:parts], out[parts : 2 * parts], out[2 * parts :]


def cross_unit(mine, theirs, acc):
    rows = mine[0][0].shape[1]
    bands = rows // 2
    wins = mine[0][0].shape[0]
    per_step = 4 if wins % 4 == 0 else 1

    def planes(ref, win):
        return [ref[win, pl.ds(i * bands, bands), :].astype(jnp.float32) for i in range(2)]

    for own, their in zip(mine, theirs):

        def step(index, acc, own=own, their=their):
            acc = list(acc)
            for i in range(per_step):
                win = index * per_step + i
                ours = [planes(ref, win) for ref in own]
                for c, ref in enumerate(their):
                    cr, ci = planes(ref, win)
                    for a, (ar, ai) in enumerate(ours):
                        at = 2 * (a * len(their) + c)
                        acc[at] = acc[at] + ar * cr + ai * ci
                        acc[at + 1] = acc[at + 1] + ai * cr - ar * ci
            return tuple(acc)

        acc = lax.fori_loop(0, wins // per_step, step, acc)
    return acc


def cross_kernel(layout, jobs, inv_root, *refs):
    groups, at = {}, 0
    for name, count in layout:
        groups[name] = refs[at : at + count]
        at += count
    pos_ref, out_ref, buffer, sems = groups["pos"][0], groups["out"][0], groups["buffer"][0], groups["sems"][0]
    chans = out_ref.shape[1]
    me = lax.axis_index("chan")
    odd = lax.rem(me, 2)
    rounds = {"one": 2 * odd, "mid": 1, "two": 2 - 2 * odd, "far": 3}
    last = pos_ref.shape[0] - 1
    bands = buffer.shape[-2] // 2
    half = chans // 2
    own_refs = groups["mine"]

    def own_view(piece, a):
        if piece == 0:
            return own_refs[a // half].at[a % half]
        return own_refs[piece + 1].at[a]

    copies = []
    for index, (source, side, pieces, acc_in, acc_out) in enumerate(jobs):
        rnd = rounds[source]
        for a_start in range(0, chans, 2):
            a_list = list(range(a_start, min(a_start + 2, chans)))
            mine = [[own_view(piece, a) for a in a_list] for piece, _ in pieces]
            theirs = [
                [groups[name][ref_index].at[row + c] for c in range(half)]
                for _, (name, ref_index, row) in pieces
            ]
            count = 2 * len(a_list) * half
            if acc_in is None:
                acc = tuple(jnp.zeros((bands, LANES), jnp.float32) for _ in range(count))
            else:
                ref = groups["acc_in"][acc_in]
                acc = tuple(
                    ref[a, c, pl.ds(i * bands, bands), :]
                    for a in a_list for c in range(half) for i in range(2)
                )
            acc = cross_unit(mine, theirs, acc)
            for ai, a in enumerate(a_list):
                pos_a = pos_ref[me * chans + a]
                for c in range(half):
                    at = 2 * (ai * half + c)
                    if acc_out is not None:
                        for i in range(2):
                            groups["acc_out"][acc_out][a, c, pl.ds(i * bands, bands), :] = acc[at + i]
                        continue
                    other = (me + rnd + 1) * chans + side * half + c
                    pos_c = pos_ref[lax.min(other, last)]
                    gain = jnp.where(pos_c - pos_a <= REACH, inv_root, 0.0).astype(jnp.float32)
                    for i in range(2):
                        buffer[index, a, c, pl.ds(i, bands, stride=2), :] = acc[at + i] * gain
        if acc_out is None:
            copy = pltpu.make_async_copy(
                buffer.at[index], out_ref.at[rnd, :, pl.ds(side * half, half)], sems.at[index]
            )
            copy.start()
            copies.append(copy)
    for copy in copies:
        copy.wait()


def cross_call(name, jobs, inv_root, positions, mine, sources, acc_in, acc_count, out_before):
    chans = mine[0].shape[0] + mine[1].shape[0]
    rows = mine[0].shape[2]
    half = chans // 2
    layout = [("pos", 1), ("mine", len(mine))]
    operands = [positions, *mine]
    for key, arrays in sources.items():
        layout.append((key, len(arrays)))
        operands += arrays
    layout.append(("acc_in", len(acc_in)))
    operands += acc_in
    specs = [SMEM] + [VMEM] * (len(operands) - 1)
    aliases = {}
    if out_before is not None:
        layout.append(("before", 1))
        aliases = {len(operands): 0}
        operands.append(out_before)
        specs.append(HBM)
    layout += [("out", 1), ("acc_out", acc_count), ("buffer", 1), ("sems", 1)]
    acc = jax.ShapeDtypeStruct((chans, half, rows, LANES), jnp.float32)
    return pl.pallas_call(
        functools.partial(cross_kernel, layout, jobs, inv_root),
        in_specs=specs,
        out_specs=[HBM] + [VMEM] * acc_count,
        out_shape=[jax.ShapeDtypeStruct((ROUNDS, chans, chans, rows, LANES), jnp.float32)]
        + [acc] * acc_count,
        scratch_shapes=[
            pltpu.VMEM((len(jobs), chans, half, rows, LANES), jnp.float32),
            pltpu.SemaphoreType.DMA((len(jobs),)),
        ],
        input_output_aliases=aliases,
        compiler_params=PARAMS,
        cost_estimate=cost(0.3 * sum(len(job[2]) for job in jobs)),
        name=name,
    )(*operands)


def choose_body(bit, triples, out_ref):
    yes = lax.rem(lax.div(lax.axis_index("chan"), bit), 2) == 1
    start = 0
    for own_ref, row, far_ref in triples:
        rows = far_ref.shape[0]

        @pl.when(yes)
        def _(own_ref=own_ref, row=row, rows=rows, start=start):
            out_ref[pl.ds(start, rows)] = own_ref[pl.ds(row, rows)]

        @pl.when(jnp.logical_not(yes))
        def _(far_ref=far_ref, rows=rows, start=start):
            out_ref[pl.ds(start, rows)] = far_ref[...]

        start += rows


def choose(bit, pairs):
    rows = [row for _, row, _ in pairs]

    def kernel(*refs):
        triples = [(refs[2 * i], row, refs[2 * i + 1]) for i, row in enumerate(rows)]
        choose_body(bit, triples, refs[-1])

    operands = [array for own, _, far in pairs for array in (own, far)]
    shape = (sum(far.shape[0] for _, _, far in pairs),) + pairs[0][2].shape[1:]
    return pl.pallas_call(
        kernel,
        in_specs=[VMEM] * len(operands),
        out_specs=VMEM,
        out_shape=jax.ShapeDtypeStruct(shape, jnp.bfloat16),
        compiler_params=PARAMS,
        cost_estimate=cost(0.1),
        name="choose",
    )(*operands)


def shards(records, positions):
    parts = lax.axis_size("win")
    blocks = lax.axis_size("chan")
    chans, wins, _ = records.shape
    half = chans // 2
    low, high, whole = whitened_spectra(records, parts)
    turn = [[(i, (i + s) % parts) for i in range(parts)] for s in range(parts)]
    up = [
        [
            (b * parts + i, (b - 4) * parts + j)
            for b in range(4, blocks)
            for i, j in turn[s]
        ]
        for s in range(parts)
    ]
    swap2 = [(i, i ^ 2) for i in range(blocks)]
    swap1 = [(i, i ^ 1) for i in range(blocks)]
    keys = [(s, h) for s in range(parts) for h in range(2)]
    far = {}
    for at, (s, h) in enumerate(keys):
        payload = (low, high)[h][s]
        if at >= 2:
            far[keys[at - 2]], payload = lax.optimization_barrier((far[keys[at - 2]], payload))
        far[s, h] = lax.ppermute(payload, ("chan", "win"), up[s])
    others = [lax.ppermute(whole[s - 1], "win", turn[s]) for s in range(1, parts)]

    def own(s, h):
        return ((low, high)[h][0], 0) if s == 0 else (others[s - 1], h * half)

    mid, one, two = {}, [], {}
    for s in range(parts):
        for h in range(2):
            mid[s, h] = lax.ppermute(choose(2, [(*own(s, h), far[s, h])]), "chan", swap2)
            if (s, h) != keys[-1]:
                two[s, h] = lax.ppermute(mid[s, h], "chan", swap1)
        pairs = [(*own(s, h), far[s, h]) for h in range(2)]
        one.append(lax.ppermute(choose(1, pairs), "chan", swap1))

    mine = [low[0], high[0], *others]
    inv_root = 1.0 / math.sqrt(parts * wins)
    last = parts - 1
    names = {"far": far, "mid": mid, "two": two}
    jobs = []
    for name in ("far", "mid", "two"):
        for h in range(2):
            open_job = h == 1 and name != "far"
            pieces = [
                (s, (name, keys.index((s, h)), 0)) for s in range(parts) if not (open_job and s == last)
            ]
            jobs.append((name, h, pieces, None, {"mid": 0, "two": 1}[name] if open_job else None))
    for h in range(2):
        jobs.append(("one", h, [(s, ("one", s, h * half)) for s in range(parts)], None, None))
    sources = {"far": [far[k] for k in keys], "one": one}
    sources |= {name: [names[name][k] for k in keys[:-1]] for name in ("mid", "two")}
    out, acc_mid, acc_two = cross_call(
        "cross_most", jobs, inv_root, positions, mine, sources, [], 2, None
    )
    mid[keys[-1]], acc_mid = lax.optimization_barrier((mid[keys[-1]], acc_mid))
    two[keys[-1]] = lax.ppermute(mid[keys[-1]], "chan", swap1)
    for name, acc in (("mid", acc_mid), ("two", acc_two)):
        job = (name, 1, [(last, (name, 0, 0))], 0, None)
        (out,) = cross_call(
            "cross_" + name, [job], inv_root, positions, mine,
            {name: [names[name][last, 1]]}, [acc], 0, out,
        )
    bands = out.shape[3] // 2
    out = out.reshape(ROUNDS, chans, chans, bands, 2, LANES).transpose(0, 1, 2, 4, 3, 5)
    return out.reshape(ROUNDS, chans, chans, 2, bands * LANES)


def solution(mesh):
    return jax.shard_map(
        shards,
        mesh=mesh,
        in_specs=(P("chan", "win", None), P()),
        out_specs=P(None, "chan", None, None, "win"),
        check_vma=False,
    )
```

profile of v0, /device:TPU:0, one launch (start us, length us, event | category | flops | bytes accessed | tf_op | source)
XLA Modules:
  0.0 41.6 jit_solution(11057485864444197529)
XLA Ops:
  0.0 0.0 copy-start.1
  0.0 0.2 tables.1
  0.2 1.1 %copy-done.1 = f32[4,8,8192]{2,1,0:T(8,128)S(1)} copy-done((f32[4,8,8192]{2,1,0:T(8,128)S(1)}, f32[4,8,8192]{2,1,0:T(8,128)}, u32[]{:S(2)}) %copy-start.1) | copy-done | bytes 1048600
  1.2 3.3 %spectra.1 = (bf16[2,8,32,128]{3,2,1,0:T(8,128)(2,1)S(1)}, bf16[2,8,32,128]{3,2,1,0:T(8,128)(2,1)S(1)}, bf16[2,8,32,128]{3,2,1,0:T(8,128)(2,1)S(1)}, bf16[2,8,32...) custom-call(f32[4,64,8,128]{3,2,1,0:T(8,128)S(1)} %bitcast.8, f32[2,64,128]{2,1,0:T(8,128)S(1)} %get-tuple-element.21.tw_ref, ...), custom_call_target="tpu_custom_call" | custom-call | flops 4400000000 | tf_op jit(solution)/shard_map/spectra/pallas_call | solution.py:196
  4.6 1.3 %collective-permute-start.4 = (bf16[2,8,32,128]{3,2,1,0:T(8,128)(2,1)S(1)}, bf16[2,8,32,128]{3,2,1,0:T(8,128)(2,1)S(1)}, u32[]{:S(2)}, u32[]{:S(2)}) collective-permute-start(bf16[2,8,32,128]{3,2,1,0:T(8,128)(2,1)S(1)} %get-tuple-element.23.refs_0_.refs_1_), channel_id=1, source_target_pairs={{8,0},{9,1},{10,2},{11,3},{12,4},{13,5},{14,6},{15,7},{16,8},{17,9... | collective-permute-start | bytes 393224 | tf_op jit(solution)/shard_map/ppermute | solution.py:397
  5.9 1.3 %collective-permute-start.1 = (bf16[2,8,32,128]{3,2,1,0:T(8,128)(2,1)S(1)}, bf16[2,8,32,128]{3,2,1,0:T(8,128)(2,1)S(1)}, u32[]{:S(2)}, u32[]{:S(2)}) collective-permute-start(bf16[2,8,32,128]{3,2,1,0:T(8,128)(2,1)S(1)} %get-tuple-element.24.refs_2_.refs_0_), channel_id=1, source_target_pairs={{8,0},{9,1},{10,2},{11,3},{12,4},{13,5},{14,6},{15,7},{16,8},{17,9... | collective-permute-start | bytes 393224 | tf_op jit(solution)/shard_map/ppermute | solution.py:397
  7.2 3.0 %collective-permute-start = (bf16[4,8,32,128]{3,2,1,0:T(8,128)(2,1)S(1)}, bf16[4,8,32,128]{3,2,1,0:T(8,128)(2,1)S(1)}, u32[]{:S(2)}, u32[]{:S(2)}) collective-permute-start(bf16[4,8,32,128]{3,2,1,0:T(8,128)(2,1)S(1)} %get-tuple-element.25), channel_id=1, source_target_pairs={{0,1},{1,0},{2,3},{3,2},{4,5},{5,4},{6,7},{7,6},{8,9},{9,8},{10,11... | collective-permute-start | bytes 786440 | tf_op jit(solution)/shard_map/ppermute | solution.py:398
  10.2 3.6 %collective-permute-done.4.refs_1_.refs_4_ = bf16[2,8,32,128]{3,2,1,0:T(8,128)(2,1)S(1)} collective-permute-done((bf16[2,8,32,128]{3,2,1,0:T(8,128)(2,1)S(1)}, bf16[2,8,32,128]{3,2,1,0:T(8,128)(2,1)S(1)}, u32[]{:S(2)}, u32[]{:S(2)}) %collective-permute-start.4) | collective-permute-done | bytes 131104 | tf_op jit(solution)/shard_map/ppermute | solution.py:397
  13.8 2.0 %collective-permute-done.1.refs_3_.refs_1_.refs_5_ = bf16[2,8,32,128]{3,2,1,0:T(8,128)(2,1)S(1)} collective-permute-done((bf16[2,8,32,128]{3,2,1,0:T(8,128)(2,1)S(1)}, bf16[2,8,32,128]{3,2,1,0:T(8,128)(2,1)S(1)}, u32[]{:S(2)}, u32[]{:S(2)}) %collective-permute-start.1) | collective-permute-done | bytes 131104 | tf_op jit(solution)/shard_map/ppermute | solution.py:397
  15.8 1.3 %collective-permute-start.5 = (bf16[2,8,32,128]{3,2,1,0:T(8,128)(2,1)S(1)}, bf16[2,8,32,128]{3,2,1,0:T(8,128)(2,1)S(1)}, u32[]{:S(2)}, u32[]{:S(2)}) collective-permute-start(bf16[2,8,32,128]{3,2,1,0:T(8,128)(2,1)S(1)} %get-tuple-element.31), channel_id=1, source_target_pairs={{8,1},{9,0},{10,3},{11,2},{12,5},{13,4},{14,7},{15,6},{16,9},{17,8... | collective-permute-start | bytes 393224 | tf_op jit(solution)/shard_map/ppermute | solution.py:397
  17.1 1.3 %collective-permute-start.2 = (bf16[2,8,32,128]{3,2,1,0:T(8,128)(2,1)S(1)}, bf16[2,8,32,128]{3,2,1,0:T(8,128)(2,1)S(1)}, u32[]{:S(2)}, u32[]{:S(2)}) collective-permute-start(bf16[2,8,32,128]{3,2,1,0:T(8,128)(2,1)S(1)} %get-tuple-element.27), channel_id=1, source_target_pairs={{8,1},{9,0},{10,3},{11,2},{12,5},{13,4},{14,7},{15,6},{16,9},{17,8... | collective-permute-start | bytes 393224 | tf_op jit(solution)/shard_map/ppermute | solution.py:397
  18.4 0.1 collective-permute-start.6
  18.6 1.7 %collective-permute-start.8 = (bf16[2,8,32,128]{3,2,1,0:T(8,128)(2,1)S(1)}, bf16[2,8,32,128]{3,2,1,0:T(8,128)(2,1)S(1)}, u32[]{:S(2)}, u32[]{:S(2)}) collective-permute-start(bf16[2,8,32,128]{3,2,1,0:T(8,128)(2,1)S(1)} %choose.9), channel_id=1, source_target_pairs={{0,4},{2,6},{4,0},{6,2},{8,12},{10,14},{12,8},{14,10},{16,20},{18,... | collective-permute-start | bytes 393224 | tf_op jit(solution)/shard_map/ppermute | solution.py:406
  20.3 4.4 %collective-permute-done.5.refs_1_.refs_6_ = bf16[2,8,32,128]{3,2,1,0:T(8,128)(2,1)S(1)} collective-permute-done((bf16[2,8,32,128]{3,2,1,0:T(8,128)(2,1)S(1)}, bf16[2,8,32,128]{3,2,1,0:T(8,128)(2,1)S(1)}, u32[]{:S(2)}, u32[]{:S(2)}) %collective-permute-start.5) | collective-permute-done | bytes 131104 | tf_op jit(solution)/shard_map/ppermute | solution.py:397
  24.6 1.7 %collective-permute-start.9 = (bf16[2,8,32,128]{3,2,1,0:T(8,128)(2,1)S(1)}, bf16[2,8,32,128]{3,2,1,0:T(8,128)(2,1)S(1)}, u32[]{:S(2)}, u32[]{:S(2)}) collective-permute-start(bf16[2,8,32,128]{3,2,1,0:T(8,128)(2,1)S(1)} %choose.10), channel_id=1, source_target_pairs={{0,4},{2,6},{4,0},{6,2},{8,12},{10,14},{12,8},{14,10},{16,20},{18,... | collective-permute-start | bytes 393224 | tf_op jit(solution)/shard_map/ppermute | solution.py:406
  26.4 0.0 collective-permute-done.2.refs_1_.refs_3_.refs_7_
  26.4 0.0 collective-permute-done.refs_0_.refs_2_.refs_3_
  26.4 0.1 collective-permute-start.7
  26.5 0.0 copy-start
  26.5 1.7 %collective-permute-start.10 = (bf16[2,8,32,128]{3,2,1,0:T(8,128)(2,1)S(1)}, bf16[2,8,32,128]{3,2,1,0:T(8,128)(2,1)S(1)}, u32[]{:S(2)}, u32[]{:S(2)}) collective-permute-start(bf16[2,8,32,128]{3,2,1,0:T(8,128)(2,1)S(1)} %choose.11), channel_id=1, source_target_pairs={{0,4},{2,6},{4,0},{6,2},{8,12},{10,14},{12,8},{14,10},{16,20},{18,... | collective-permute-start | bytes 393224 | tf_op jit(solution)/shard_map/ppermute | solution.py:406
  28.2 0.0 collective-permute-done.8.refs_10_
  28.2 0.2 collective-permute-start.11
  28.4 1.2 %collective-permute-done.9.refs_11_ = bf16[2,8,32,128]{3,2,1,0:T(8,128)(2,1)S(1)} collective-permute-done((bf16[2,8,32,128]{3,2,1,0:T(8,128)(2,1)S(1)}, bf16[2,8,32,128]{3,2,1,0:T(8,128)(2,1)S(1)}, u32[]{:S(2)}, u32[]{:S(2)}) %collective-permute-start.9) | collective-permute-done | bytes 131104 | tf_op jit(solution)/shard_map/ppermute | solution.py:406
  29.6 0.0 collective-permute-start.12
  29.6 2.8 %collective-permute-done.10.refs_12_ = bf16[2,8,32,128]{3,2,1,0:T(8,128)(2,1)S(1)} collective-permute-done((bf16[2,8,32,128]{3,2,1,0:T(8,128)(2,1)S(1)}, bf16[2,8,32,128]{3,2,1,0:T(8,128)(2,1)S(1)}, u32[]{:S(2)}, u32[]{:S(2)}) %collective-permute-start.10) | collective-permute-done | bytes 131104 | tf_op jit(solution)/shard_map/ppermute | solution.py:406
  32.5 0.0 collective-permute-start.13
  32.5 0.0 collective-permute-done.6.refs_8_
  32.5 1.7 %collective-permute-start.3 = (bf16[2,8,32,128]{3,2,1,0:T(8,128)(2,1)S(1)}, bf16[2,8,32,128]{3,2,1,0:T(8,128)(2,1)S(1)}, u32[]{:S(2)}, u32[]{:S(2)}) collective-permute-start(bf16[2,8,32,128]{3,2,1,0:T(8,128)(2,1)S(1)} %choose.6), channel_id=1, source_target_pairs={{0,4},{2,6},{4,0},{6,2},{8,12},{10,14},{12,8},{14,10},{16,20},{18,... | collective-permute-start | bytes 393224 | tf_op jit(solution)/shard_map/ppermute | solution.py:406
  34.2 0.0 collective-permute-done.11.refs_13_
  34.2 0.0 collective-permute-done.12.refs_14_
  34.2 0.0 collective-permute-done.7.refs_9_
  34.2 0.0 collective-permute-done.13.refs_15_
  34.3 0.0 copy-done
  34.3 4.2 %cross_most.1 = (f32[4,4,4,32,128]{4,3,2,1,0:T(8,128)}, f32[4,2,32,128]{3,2,1,0:T(8,128)S(1)}, f32[4,2,32,128]{3,2,1,0:T(8,128)S(1)}) custom-call(s32[64]{0:T(128)S(1)} %copy-done, bf16[2,8,32,128]{3,2,1,0:T(8,128)(2,1)S(1)} %get-tuple-element.23.refs_0_.refs_1_, bf16[2,8,32,128]{3,2,1,0:T(8,128)(2,1)S(1)} %get-tuple-element.24.refs_2_.refs_0_, ...), custom_call_target="tpu_custom_call" | custom-call | flops 4620000256 | tf_op jit(solution)/shard_map/cross_most/pallas_call | solution.py:320
  38.4 0.0 collective-permute-done.3.refs_4_
  38.5 0.3 collective-permute-start.14
  38.7 1.4 %cross_mid.1.refs_6_ = f32[4,4,4,32,128]{4,3,2,1,0:T(8,128)} custom-call(s32[64]{0:T(128)S(1)} %copy-done, bf16[2,8,32,128]{3,2,1,0:T(8,128)(2,1)S(1)} %get-tuple-element.23.refs_0_.refs_1_, bf16[2,8,32,128]{3,2,1,0:T(8,128)(2,1)S(1)} %get-tuple-element.24.refs_2_.refs_0_, ...), custom_call_target="tpu_custom_call", output_to_operand_aliasing={{}: (6, {})} | custom-call | flops 330000000 | tf_op jit(solution)/shard_map/cross_mid/pallas_call | solution.py:320
  40.2 0.0 collective-permute-done.14.refs_4_
  40.2 1.4 %cross_two.1 = f32[4,4,4,32,128]{4,3,2,1,0:T(8,128)} custom-call(s32[64]{0:T(128)S(1)} %copy-done, bf16[2,8,32,128]{3,2,1,0:T(8,128)(2,1)S(1)} %get-tuple-element.23.refs_0_.refs_1_, bf16[2,8,32,128]{3,2,1,0:T(8,128)(2,1)S(1)} %get-tuple-element.24.refs_2_.refs_0_, ...), custom_call_target="tpu_custom_call", output_to_operand_aliasing={{}: (6, {})} | custom-call | flops 330000000 | tf_op jit(solution)/shard_map/cross_two/pallas_call | solution.py:320
  (6 shorter events, 0.1 us)
Async XLA Ops:
  0.0 1.2 %copy-start.1 = (f32[4,8,8192]{2,1,0:T(8,128)S(1)}, f32[4,8,8192]{2,1,0:T(8,128)}, u32[]{:S(2)}) copy-start(f32[4,8,8192]{2,1,0:T(8,128)} %param.2) | copy-start | bytes 3145732
  4.6 9.3 %collective-permute-start.4 = (bf16[2,8,32,128]{3,2,1,0:T(8,128)(2,1)S(1)}, bf16[2,8,32,128]{3,2,1,0:T(8,128)(2,1)S(1)}, u32[]{:S(2)}, u32[]{:S(2)}) collective-permute-start(bf16[2,8,32,128]{3,2,1,0:T(8,128)(2,1)S(1)} %get-tuple-element.23.refs_0_.refs_1_), channel_id=1, source_target_pairs={{8,0},{9,1},{10,2},{11,3},{12,4},{13,5},{14,6},{15,7},{16,8},{17,9... | collective-permute-start | bytes 393224 | tf_op jit(solution)/shard_map/ppermute | solution.py:397
  5.9 9.9 %collective-permute-start.1 = (bf16[2,8,32,128]{3,2,1,0:T(8,128)(2,1)S(1)}, bf16[2,8,32,128]{3,2,1,0:T(8,128)(2,1)S(1)}, u32[]{:S(2)}, u32[]{:S(2)}) collective-permute-start(bf16[2,8,32,128]{3,2,1,0:T(8,128)(2,1)S(1)} %get-tuple-element.24.refs_2_.refs_0_), channel_id=1, source_target_pairs={{8,0},{9,1},{10,2},{11,3},{12,4},{13,5},{14,6},{15,7},{16,8},{17,9... | collective-permute-start | bytes 393224 | tf_op jit(solution)/shard_map/ppermute | solution.py:397
  7.2 19.2 %collective-permute-start = (bf16[4,8,32,128]{3,2,1,0:T(8,128)(2,1)S(1)}, bf16[4,8,32,128]{3,2,1,0:T(8,128)(2,1)S(1)}, u32[]{:S(2)}, u32[]{:S(2)}) collective-permute-start(bf16[4,8,32,128]{3,2,1,0:T(8,128)(2,1)S(1)} %get-tuple-element.25), channel_id=1, source_target_pairs={{0,1},{1,0},{2,3},{3,2},{4,5},{5,4},{6,7},{7,6},{8,9},{9,8},{10,11... | collective-permute-start | bytes 786440 | tf_op jit(solution)/shard_map/ppermute | solution.py:398
  15.8 8.8 %collective-permute-start.5 = (bf16[2,8,32,128]{3,2,1,0:T(8,128)(2,1)S(1)}, bf16[2,8,32,128]{3,2,1,0:T(8,128)(2,1)S(1)}, u32[]{:S(2)}, u32[]{:S(2)}) collective-permute-start(bf16[2,8,32,128]{3,2,1,0:T(8,128)(2,1)S(1)} %get-tuple-element.31), channel_id=1, source_target_pairs={{8,1},{9,0},{10,3},{11,2},{12,5},{13,4},{14,7},{15,6},{16,9},{17,8... | collective-permute-start | bytes 393224 | tf_op jit(solution)/shard_map/ppermute | solution.py:397
  17.1 9.3 %collective-permute-start.2 = (bf16[2,8,32,128]{3,2,1,0:T(8,128)(2,1)S(1)}, bf16[2,8,32,128]{3,2,1,0:T(8,128)(2,1)S(1)}, u32[]{:S(2)}, u32[]{:S(2)}) collective-permute-start(bf16[2,8,32,128]{3,2,1,0:T(8,128)(2,1)S(1)} %get-tuple-element.27), channel_id=1, source_target_pairs={{8,1},{9,0},{10,3},{11,2},{12,5},{13,4},{14,7},{15,6},{16,9},{17,8... | collective-permute-start | bytes 393224 | tf_op jit(solution)/shard_map/ppermute | solution.py:397
  18.4 14.0 %collective-permute-start.6 = (bf16[4,8,32,128]{3,2,1,0:T(8,128)(2,1)S(1)}, bf16[4,8,32,128]{3,2,1,0:T(8,128)(2,1)S(1)}, u32[]{:S(2)}, u32[]{:S(2)}) collective-permute-start(bf16[4,8,32,128]{3,2,1,0:T(8,128)(2,1)S(1)} %choose.7), channel_id=1, source_target_pairs={{0,2},{2,0},{4,6},{6,4},{8,10},{10,8},{12,14},{14,12},{16,18},{18,... | collective-permute-start | bytes 786440 | tf_op jit(solution)/shard_map/ppermute | solution.py:410
  18.6 9.7 %collective-permute-start.8 = (bf16[2,8,32,128]{3,2,1,0:T(8,128)(2,1)S(1)}, bf16[2,8,32,128]{3,2,1,0:T(8,128)(2,1)S(1)}, u32[]{:S(2)}, u32[]{:S(2)}) collective-permute-start(bf16[2,8,32,128]{3,2,1,0:T(8,128)(2,1)S(1)} %choose.9), channel_id=1, source_target_pairs={{0,4},{2,6},{4,0},{6,2},{8,12},{10,14},{12,8},{14,10},{16,20},{18,... | collective-permute-start | bytes 393224 | tf_op jit(solution)/shard_map/ppermute | solution.py:406
  24.6 5.0 %collective-permute-start.9 = (bf16[2,8,32,128]{3,2,1,0:T(8,128)(2,1)S(1)}, bf16[2,8,32,128]{3,2,1,0:T(8,128)(2,1)S(1)}, u32[]{:S(2)}, u32[]{:S(2)}) collective-permute-start(bf16[2,8,32,128]{3,2,1,0:T(8,128)(2,1)S(1)} %choose.10), channel_id=1, source_target_pairs={{0,4},{2,6},{4,0},{6,2},{8,12},{10,14},{12,8},{14,10},{16,20},{18,... | collective-permute-start | bytes 393224 | tf_op jit(solution)/shard_map/ppermute | solution.py:406
  26.4 7.8 %collective-permute-start.7 = (bf16[4,8,32,128]{3,2,1,0:T(8,128)(2,1)S(1)}, bf16[4,8,32,128]{3,2,1,0:T(8,128)(2,1)S(1)}, u32[]{:S(2)}, u32[]{:S(2)}) collective-permute-start(bf16[4,8,32,128]{3,2,1,0:T(8,128)(2,1)S(1)} %choose.8), channel_id=1, source_target_pairs={{0,2},{2,0},{4,6},{6,4},{8,10},{10,8},{12,14},{14,12},{16,18},{18,... | collective-permute-start | bytes 786440 | tf_op jit(solution)/shard_map/ppermute | solution.py:410
  26.5 7.7 %copy-start = (s32[64]{0:T(128)S(1)}, s32[64]{0:T(128)}, u32[]{:S(2)}) copy-start(s32[64]{0:T(128)} %refs_0_.5) | copy-start | bytes 772
  26.5 5.9 %collective-permute-start.10 = (bf16[2,8,32,128]{3,2,1,0:T(8,128)(2,1)S(1)}, bf16[2,8,32,128]{3,2,1,0:T(8,128)(2,1)S(1)}, u32[]{:S(2)}, u32[]{:S(2)}) collective-permute-start(bf16[2,8,32,128]{3,2,1,0:T(8,128)(2,1)S(1)} %choose.11), channel_id=1, source_target_pairs={{0,4},{2,6},{4,0},{6,2},{8,12},{10,14},{12,8},{14,10},{16,20},{18,... | collective-permute-start | bytes 393224 | tf_op jit(solution)/shard_map/ppermute | solution.py:406
  28.2 6.0 %collective-permute-start.11 = (bf16[2,8,32,128]{3,2,1,0:T(8,128)(2,1)S(1)}, bf16[2,8,32,128]{3,2,1,0:T(8,128)(2,1)S(1)}, u32[]{:S(2)}, u32[]{:S(2)}) collective-permute-start(bf16[2,8,32,128]{3,2,1,0:T(8,128)(2,1)S(1)} %collective-permute-done.8.refs_10_), channel_id=1, source_target_pairs={{0,2},{2,0},{4,6},{6,4},{8,10},{10,8},{12,14},{14,12},{16,18},{18,... | collective-permute-start | bytes 393224 | tf_op jit(solution)/shard_map/ppermute | solution.py:408
  29.6 4.6 %collective-permute-start.12 = (bf16[2,8,32,128]{3,2,1,0:T(8,128)(2,1)S(1)}, bf16[2,8,32,128]{3,2,1,0:T(8,128)(2,1)S(1)}, u32[]{:S(2)}, u32[]{:S(2)}) collective-permute-start(bf16[2,8,32,128]{3,2,1,0:T(8,128)(2,1)S(1)} %collective-permute-done.9.refs_11_), channel_id=1, source_target_pairs={{0,2},{2,0},{4,6},{6,4},{8,10},{10,8},{12,14},{14,12},{16,18},{18,... | collective-permute-start | bytes 393224 | tf_op jit(solution)/shard_map/ppermute | solution.py:408
  32.5 1.8 %collective-permute-start.13 = (bf16[2,8,32,128]{3,2,1,0:T(8,128)(2,1)S(1)}, bf16[2,8,32,128]{3,2,1,0:T(8,128)(2,1)S(1)}, u32[]{:S(2)}, u32[]{:S(2)}) collective-permute-start(bf16[2,8,32,128]{3,2,1,0:T(8,128)(2,1)S(1)} %collective-permute-done.10.refs_12_), channel_id=1, source_target_pairs={{0,2},{2,0},{4,6},{6,4},{8,10},{10,8},{12,14},{14,12},{16,18},{18,... | collective-permute-start | bytes 393224 | tf_op jit(solution)/shard_map/ppermute | solution.py:408
  32.5 6.0 %collective-permute-start.3 = (bf16[2,8,32,128]{3,2,1,0:T(8,128)(2,1)S(1)}, bf16[2,8,32,128]{3,2,1,0:T(8,128)(2,1)S(1)}, u32[]{:S(2)}, u32[]{:S(2)}) collective-permute-start(bf16[2,8,32,128]{3,2,1,0:T(8,128)(2,1)S(1)} %choose.6), channel_id=1, source_target_pairs={{0,4},{2,6},{4,0},{6,2},{8,12},{10,14},{12,8},{14,10},{16,20},{18,... | collective-permute-start | bytes 393224 | tf_op jit(solution)/shard_map/ppermute | solution.py:406
  38.5 1.7 %collective-permute-start.14 = (bf16[2,8,32,128]{3,2,1,0:T(8,128)(2,1)S(1)}, bf16[2,8,32,128]{3,2,1,0:T(8,128)(2,1)S(1)}, u32[]{:S(2)}, u32[]{:S(2)}) collective-permute-start(bf16[2,8,32,128]{3,2,1,0:T(8,128)(2,1)S(1)} %collective-permute-done.3.refs_4_), channel_id=1, source_target_pairs={{0,2},{2,0},{4,6},{6,4},{8,10},{10,8},{12,14},{14,12},{16,18},{18,... | collective-permute-start | bytes 393224 | tf_op jit(solution)/shard_map/ppermute | solution.py:432
where the time goes:
time: 41.8 us; the launch traced here: 41.6 us
  starting transfers between devices  15.7 us (38%)
  waiting for transfers between devices  14 us (33%)
  Pallas kernels  10.7 us (26%)
  local copies, waits for them, and re-layouts  1.07 us (3%)
    ppermute x4, waiting for transfers between devices, shards(): far[s, h] = lax.ppermute(payload, ('chan', 'win'), up[s])  9.97 us
    pallas_call x3, Pallas kernels, cross_call(): pl.pallas_call(functools.partial(cross_kernel, layout, jobs, inv_root), i...  7.01 us
    ppermute x4, starting transfers between devices, shards(): lax.ppermute(choose(2, [(*own(s, h), far[s, h])]), 'chan', swap2)  6.87 us
    ppermute x4, starting transfers between devices, shards(): far[s, h] = lax.ppermute(payload, ('chan', 'win'), up[s])  5.16 us
    ppermute x4, waiting for transfers between devices, shards(): lax.ppermute(choose(2, [(*own(s, h), far[s, h])]), 'chan', swap2)  4.06 us
    pallas_call x1, Pallas kernels, whitened_spectra(): pl.pallas_call(functools.partial(spectra_kernel, parts), in_specs=[VMEM]...  3.34 us
    ppermute x1, starting transfers between devices, shards(): lax.ppermute(whole[s - 1], 'win', turn[s])  3.03 us
    unnamed x4, local copies, waits for them, and re-layouts  1.07 us
  transfers between devices with their start and end apart: 15, of which 5 were waited for; matrix products, arithmetic and copies ran while one was open for 0% of the time, Pallas kernels for 14%

commit v1 on v0

v1 whole, which is shorter than its diff:
```python
import functools
import math

import jax
import jax.numpy as jnp
from jax import lax
from jax.experimental import pallas as pl
from jax.experimental.pallas import tpu as pltpu
from jax.sharding import PartitionSpec as P

BINS = 4096
BAND = 128
ROUNDS = 4
REACH = 2000
LANES = 128
band_epsilon = 1e-06
VMEM = pl.BlockSpec(memory_space=pltpu.VMEM)
SMEM = pl.BlockSpec(memory_space=pltpu.SMEM)
HBM = pl.BlockSpec(memory_space=pltpu.HBM)
PARAMS = pltpu.CompilerParams(vmem_limit_bytes=40 * 1024 * 1024)


def cost(microseconds):
    return pl.CostEstimate(flops=int(microseconds * 1.1e9), bytes_accessed=0, transcendentals=0)


def split3(value):
    hi = value.astype(jnp.bfloat16)
    rest = value - hi.astype(jnp.float32)
    mid = rest.astype(jnp.bfloat16)
    lo = (rest - mid.astype(jnp.float32)).astype(jnp.bfloat16)
    return hi, mid, lo


def real_dft(values):
    n = len(values)
    if n == 2:
        return [(values[0] + values[1], None), (values[0] - values[1], None)]
    even, odd = real_dft(values[0::2]), real_dft(values[1::2])
    out = [None] * (n // 2 + 1)
    for k in range(n // 4 + 1):
        (er, ei), (dr, di) = even[k], odd[k]
        if k == 0:
            out[0] = (er + dr, None)
            out[n // 2] = (er - dr, None)
        elif 4 * k == n:
            out[k] = (er, -dr)
        else:
            c, s = math.cos(2.0 * math.pi * k / n), math.sin(2.0 * math.pi * k / n)
            tr = dr * c + di * s
            ti = di * c - dr * s
            out[k] = (er + tr, ei + ti)
            out[n // 2 - k] = (er - tr, ti - ei)
    return out


def spectra_channel(parts, chan, x, tw_ref, l2_ref, t_ref, outs):
    first = len(x)
    wins = x[0].shape[0]
    bands = BINS // BAND // parts
    terms = real_dft(x)
    for k in range(first):
        re, im = terms[min(k, first - k)]
        rows = pl.ds(k * wins, wins)
        cos, sin = tw_ref[0, pl.ds(k, 1), :], tw_ref[1, pl.ds(k, 1), :]
        if im is None:
            t_ref[chan, 0, rows, :] = re * cos
            t_ref[chan, 1, rows, :] = -(re * sin)
        elif 2 * k <= first:
            t_ref[chan, 0, rows, :] = re * cos + im * sin
            t_ref[chan, 1, rows, :] = im * cos - re * sin
        else:
            t_ref[chan, 0, rows, :] = re * cos - im * sin
            t_ref[chan, 1, rows, :] = -(im * cos + re * sin)
    rhs = []
    for win in range(wins):
        at = pl.ds(win, first, stride=wins)
        row = jnp.concatenate([t_ref[chan, 0, at, :], t_ref[chan, 1, at, :]], axis=1)
        hi, mid, lo = split3(row)
        rhs.append(jnp.concatenate([hi, mid, lo, hi, mid, hi], axis=1))
    spec = lax.dot_general(
        l2_ref[...],
        jnp.concatenate(rhs, axis=0),
        (((1,), (1,)), ((), ())),
        preferred_element_type=jnp.float32,
    )
    left = lax.broadcasted_iota(jnp.int32, (bands, LANES), 1) < first
    pairs = wins // 2
    tiles = [
        spec[:, i * LANES : (i + 1) * LANES].reshape(parts, 4, bands, LANES) for i in range(pairs)
    ]
    powers = []
    for tile in tiles:
        square = tile * tile
        power = square[:, 0] + square[:, 1] + square[:, 2] + square[:, 3]
        powers.append(power.reshape(parts * bands, LANES))
    row = lax.rem(lax.broadcasted_iota(jnp.int32, (3 * LANES, LANES), 0), LANES)
    lane = lax.broadcasted_iota(jnp.int32, (3 * LANES, LANES), 1)
    ones = ((row < first) == (lane < first)).astype(jnp.bfloat16)
    total = jnp.dot(
        jnp.concatenate(split3(jnp.concatenate(powers, axis=0)), axis=1),
        ones,
        preferred_element_type=jnp.float32,
    )
    scales = lax.rsqrt(total * (1.0 / BAND) + band_epsilon).reshape(pairs, parts, bands, LANES)
    for pair in range(pairs):
        for s in range(parts):
            scale = scales[pair, s]
            for imag in range(2):
                even = tiles[pair][s, 2 * imag] * scale
                odd = tiles[pair][s, 2 * imag + 1] * scale
                one = jnp.where(left, even, pltpu.roll(odd, first, 1)).astype(jnp.bfloat16)
                two = jnp.where(left, pltpu.roll(even, first, 1), odd).astype(jnp.bfloat16)
                at = pl.ds(imag * bands, bands)
                outs[s][chan, 2 * pair, at, :] = one
                outs[s][chan, 2 * pair + 1, at, :] = two


def turn_table(index, period):
    index = lax.rem(index, period)
    quarter = period // 4
    turn = lax.div(index + quarter // 2, quarter)
    angle = (index - turn * quarter).astype(jnp.float32) * (2.0 * math.pi / period)
    square = angle * angle

    def series(first):
        value = jnp.full_like(angle, 0.0)
        for power in range(10 + first, first - 1, -2):
            value = value * square + (-1) ** (power // 2) / math.factorial(power)
        return value

    cos, sin = series(0), series(1) * angle
    swap = lax.rem(turn, 2) == 1
    minus_cos = (turn == 1) | (turn == 2)
    minus_sin = (turn == 2) | (turn == 3)
    cos, sin = jnp.where(swap, sin, cos), jnp.where(swap, cos, sin)
    return jnp.where(minus_cos, -cos, cos), jnp.where(minus_sin, -sin, sin)


def tables_kernel(parts, samples, tw_ref, l2_ref):
    first = samples // LANES
    bands = BINS // BAND // parts
    me = lax.axis_index("win")
    k1 = lax.broadcasted_iota(jnp.int32, (first, LANES), 0)
    q = lax.broadcasted_iota(jnp.int32, (first, LANES), 1)
    tw_ref[0], tw_ref[1] = turn_table(k1 * q, samples)
    band = lax.broadcasted_iota(jnp.int32, (bands, LANES), 0)
    q = lax.broadcasted_iota(jnp.int32, (bands, LANES), 1)
    for s in range(parts):
        part = lax.rem(me + s, parts)
        tables = [turn_table((2 * (part * bands + band) + odd) * q, LANES) for odd in range(2)]
        rows = [jnp.concatenate([cos, sin], axis=1) for cos, sin in tables]
        rows += [jnp.concatenate([-sin, cos], axis=1) for cos, sin in tables]
        hi, mid, lo = split3(jnp.concatenate(rows, axis=0))
        table = jnp.concatenate([hi, hi, hi, mid, mid, lo], axis=1)
        l2_ref[pl.ds(s * 4 * bands, 4 * bands), :] = table


def spectra_kernel(parts, x_ref, tw_ref, l2_ref, *refs):
    outs, t_ref = refs[:-1], refs[-1]
    chans, first = x_ref.shape[:2]
    for chan in range(chans):
        x = [x_ref[chan, p] for p in range(first)]
        spectra_channel(parts, chan, x, tw_ref, l2_ref, t_ref, outs)


def whitened_spectra(records, parts):
    chans, wins, samples = records.shape
    first = samples // LANES
    rows = 2 * (BINS // BAND // parts)
    x = records.reshape(chans, wins, first, LANES).transpose(0, 2, 1, 3)
    tables = pl.pallas_call(
        functools.partial(tables_kernel, parts, samples),
        out_specs=[VMEM] * 2,
        out_shape=[
            jax.ShapeDtypeStruct((2, first, LANES), jnp.float32),
            jax.ShapeDtypeStruct((2 * rows * parts, 12 * LANES), jnp.bfloat16),
        ],
        compiler_params=PARAMS,
        cost_estimate=cost(1),
        name="tables",
    )()
    return pl.pallas_call(
        functools.partial(spectra_kernel, parts),
        in_specs=[VMEM] * 3,
        out_specs=[VMEM] * parts,
        out_shape=[jax.ShapeDtypeStruct((chans, wins, rows, LANES), jnp.bfloat16)] * parts,
        scratch_shapes=[pltpu.VMEM((chans, 2, first * wins, LANES), jnp.float32)],
        compiler_params=PARAMS,
        cost_estimate=cost(4),
        name="spectra",
    )(x, *tables)


def cross_unit(mine, theirs, acc):
    rows = mine[0][0].shape[1]
    bands = rows // 2
    wins = mine[0][0].shape[0]
    per_step = 4 if wins % 4 == 0 else 1

    def planes(ref, win):
        return [ref[win, pl.ds(i * bands, bands), :].astype(jnp.float32) for i in range(2)]

    for own, their in zip(mine, theirs):

        def step(index, acc, own=own, their=their):
            acc = list(acc)
            for i in range(per_step):
                win = index * per_step + i
                ours = [planes(ref, win) for ref in own]
                for c, ref in enumerate(their):
                    cr, ci = planes(ref, win)
                    for a, (ar, ai) in enumerate(ours):
                        at = 2 * (a * len(their) + c)
                        acc[at] = acc[at] + ar * cr + ai * ci
                        acc[at + 1] = acc[at + 1] + ai * cr - ar * ci
            return tuple(acc)

        acc = lax.fori_loop(0, wins // per_step, step, acc)
    return acc


def cross_kernel(layout, jobs, inv_root, *refs):
    groups, at = {}, 0
    for name, count in layout:
        groups[name] = refs[at : at + count]
        at += count
    (pos_ref,) = groups["pos"]
    mine = groups["mine"]
    chans, _, rows, _ = mine[0].shape
    bands = rows // 2
    me = lax.axis_index("chan")
    odd = lax.rem(me, 2)
    rounds = {"one": 2 * odd, "mid": 1, "two": 2 - 2 * odd, "far": 3}
    last = pos_ref.shape[0] - 1
    step = 2
    copies = []

    def send(source, ref, a_start, count):
        (out_ref,), (sems,) = groups["out"], groups["sems"]
        part = pl.ds(a_start, count)
        copy = pltpu.make_async_copy(
            ref.at[part], out_ref.at[rounds[source], part], sems.at[len(copies)]
        )
        copy.start()
        copies.append(copy)

    for source, ref in zip(("far", "mid", "one"), groups["done"]):
        send(source, ref, 0, chans)
    for source, pieces, acc_in, final, to in jobs:
        rnd = rounds[source]
        to_ref = groups["buffer"][0] if to is None else groups["acc_out"][to]
        for a_start in range(0, chans, step):
            a_list = range(a_start, min(a_start + step, chans))
            for c_start in range(0, chans, step):
                c_list = range(c_start, min(c_start + step, chans))
                ours = [[mine[piece].at[a] for a in a_list] for piece, _ in pieces]
                theirs = [[groups[source][ref].at[c] for c in c_list] for _, ref in pieces]
                order = [(a, c, i) for a in a_list for c in c_list for i in range(2)]
                if acc_in is None:
                    acc = tuple(jnp.zeros((bands, LANES), jnp.float32) for _ in order)
                else:
                    ref = groups["acc_in"][acc_in]
                    acc = tuple(ref[a, c, pl.ds(i * bands, bands), :] for a, c, i in order)
                acc = cross_unit(ours, theirs, acc)
                for (a, c, i), value in zip(order, acc):
                    if not final:
                        to_ref[a, c, pl.ds(i * bands, bands), :] = value
                        continue
                    pos_c = pos_ref[lax.min((me + rnd + 1) * chans + c, last)]
                    near = pos_c - pos_ref[me * chans + a] <= REACH
                    gain = jnp.where(near, inv_root, 0.0).astype(jnp.float32)
                    to_ref[a, c, pl.ds(i, bands, stride=2), :] = value * gain
            if to is None:
                send(source, to_ref, a_start, len(a_list))
    for copy in copies:
        copy.wait()


def cross_call(name, jobs, inv_root, positions, mine, sources, acc_in=(), done=()):
    chans, _, rows, _ = mine[0].shape
    groups = [("pos", [positions]), ("mine", mine), *sources.items()]
    groups += [("acc_in", acc_in), ("done", done)]
    operands = [array for _, arrays in groups for array in arrays]
    layout = [(key, len(arrays)) for key, arrays in groups]
    sums = jax.ShapeDtypeStruct((chans, chans, rows, LANES), jnp.float32)
    whole = jax.ShapeDtypeStruct((ROUNDS,) + sums.shape, jnp.float32)
    acc_count = sum(job[4] is not None for job in jobs)
    ends = 1 - acc_count // len(jobs)
    layout += [("out", ends), ("acc_out", acc_count), ("buffer", ends), ("sems", ends)]
    scratch = [pltpu.VMEM(sums.shape, jnp.float32), pltpu.SemaphoreType.DMA((chans + len(done),))]
    return pl.pallas_call(
        functools.partial(cross_kernel, layout, jobs, inv_root),
        in_specs=[SMEM] + [VMEM] * (len(operands) - 1),
        out_specs=[HBM] * ends + [VMEM] * acc_count,
        out_shape=[whole] * ends + [sums] * acc_count,
        scratch_shapes=scratch * ends,
        compiler_params=PARAMS,
        cost_estimate=cost(0.6 * sum(len(job[1]) for job in jobs)),
        name=name,
    )(*operands)


def choose(bit, own, far):
    def kernel(own_ref, far_ref, out_ref):
        yes = lax.rem(lax.div(lax.axis_index("chan"), bit), 2) == 1

        @pl.when(yes)
        def _():
            out_ref[...] = own_ref[...]

        @pl.when(jnp.logical_not(yes))
        def _():
            out_ref[...] = far_ref[...]

    return pl.pallas_call(
        kernel,
        in_specs=[VMEM] * 2,
        out_specs=VMEM,
        out_shape=jax.ShapeDtypeStruct(far.shape, far.dtype),
        compiler_params=PARAMS,
        cost_estimate=cost(0.1),
        name="choose",
    )(own, far)


def after(value, *others):
    return lax.optimization_barrier((value, *others))[0]


def shards(records, positions):
    parts = lax.axis_size("win")
    blocks = lax.axis_size("chan")
    wins = records.shape[1]
    spectra = whitened_spectra(records, parts)
    up = [(b, b - 4) for b in range(4, blocks)]
    swap2 = [(b, b ^ 2) for b in range(blocks)]
    swap1 = [(b, b ^ 1) for b in range(blocks)]
    mine = [spectra[0]]
    for s in range(1, parts):
        mine.append(lax.ppermute(spectra[s], "win", [(i, (i + s) % parts) for i in range(parts)]))
    far = [lax.ppermute(own, "chan", up) for own in mine]
    last = parts - 1
    early = range(last)
    inv_root = 1.0 / math.sqrt(parts * wins)
    call = functools.partial(cross_call, inv_root=inv_root, positions=positions, mine=mine)

    (acc_far,) = call(
        "cross_far", [("far", [(s, s) for s in early], None, False, 0)], sources={"far": far[:-1]}
    )
    far[last] = after(far[last], acc_far)
    mid, one, two = [], [], []
    for s in range(parts):
        mid.append(lax.ppermute(choose(2, mine[s], far[s]), "chan", swap2))
        one.append(lax.ppermute(choose(1, mine[s], far[s]), "chan", swap1))
        if s < last:
            two.append(lax.ppermute(mid[s], "chan", swap1))
    done_far, acc_mid, acc_one = call(
        "cross_most",
        [
            ("far", [(last, 0)], 0, True, 0),
            ("mid", [(s, s) for s in early], None, False, 1),
            ("one", [(s, s) for s in early], None, False, 2),
        ],
        sources={"far": far[last:], "mid": mid[:last], "one": one[:last]},
        acc_in=[acc_far],
    )
    mid[last] = after(mid[last], acc_mid)
    two.append(lax.ppermute(mid[last], "chan", swap1))
    done_mid, done_one, acc_two = call(
        "cross_next",
        [
            ("mid", [(last, 0)], 0, True, 0),
            ("one", [(last, 0)], 1, True, 1),
            ("two", [(s, s) for s in early], None, False, 2),
        ],
        sources={"mid": mid[last:], "one": one[last:], "two": two[:last]},
        acc_in=[acc_mid, acc_one],
    )
    two[last] = after(two[last], acc_two)
    (out,) = call(
        "cross_last", [("two", [(last, 0)], 0, True, None)], sources={"two": two[last:]},
        acc_in=[acc_two], done=[done_far, done_mid, done_one],
    )
    chans, bands = out.shape[1], out.shape[3] // 2
    out = out.reshape(ROUNDS, chans, chans, bands, 2, LANES).transpose(0, 1, 2, 4, 3, 5)
    return out.reshape(ROUNDS, chans, chans, 2, bands * LANES)


def solution(mesh):
    return jax.shard_map(
        shards,
        mesh=mesh,
        in_specs=(P("chan", "win", None), P()),
        out_specs=P(None, "chan", None, None, "win"),
        check_vma=False,
    )
```

time: 41.8 us -> 33.8 us (0.81)
  starting transfers between devices: 15.7 us -> 9.22 us
  Pallas kernels: 10.7 us -> 9.84 us
  waiting for transfers between devices: 14 us -> 13.3 us
    ppermute x15 -> x9, starting transfers between devices: 15.7 us -> 9.22 us  [the longest x1 3.03 us: shards(): lax.ppermute(spectra[s], 'win', [(i, (i + s) % parts) for i in range(part...]
    ppermute x15 -> x9, waiting for transfers between devices: 14 us -> 13.3 us  [the longest x2 5.45 us: shards(): far = [lax.ppermute(own, 'chan', up) for own in mine]]
    pallas_call x3 -> x4, Pallas kernels: 7.01 us -> 6.28 us  [cross_call(): pl.pallas_call(functools.partial(cross_kernel, layout, jobs, inv_root), i...]
  transfers between devices with their start and end apart: 15 -> 9, of which waited for: 5 -> 4; matrix products, arithmetic and copies ran while one was open for 0% -> 0% of each run, Pallas kernels for 14% -> 14%
where the time goes in v1:
time: 33.8 us; the launch traced here: 33.6 us
  waiting for transfers between devices  13.3 us (39%)
  Pallas kernels  9.84 us (29%)
  starting transfers between devices  9.22 us (27%)
  local copies, waits for them, and re-layouts  1.07 us (3%)
    pallas_call x4, Pallas kernels, cross_call(): pl.pallas_call(functools.partial(cross_kernel, layout, jobs, inv_root), i...  6.28 us
    ppermute x2, waiting for transfers between devices, shards(): far = [lax.ppermute(own, 'chan', up) for own in mine]  5.45 us
    ppermute x1, waiting for transfers between devices, shards(): lax.ppermute(spectra[s], 'win', [(i, (i + s) % parts) for i in range(part...  5.03 us
    pallas_call x1, Pallas kernels, whitened_spectra(): pl.pallas_call(functools.partial(spectra_kernel, parts), in_specs=[VMEM]...  3.34 us
    ppermute x1, starting transfers between devices, shards(): lax.ppermute(spectra[s], 'win', [(i, (i + s) % parts) for i in range(part...  3.03 us
    ppermute x2, starting transfers between devices, shards(): mid.append(lax.ppermute(choose(2, mine[s], far[s]), 'chan', swap2))  3 us
    ppermute x2, waiting for transfers between devices, shards(): mid.append(lax.ppermute(choose(2, mine[s], far[s]), 'chan', swap2))  2.8 us
    ppermute x2, starting transfers between devices, shards(): far = [lax.ppermute(own, 'chan', up) for own in mine]  2.56 us
  transfers between devices with their start and end apart: 9, of which 4 were waited for; matrix products, arithmetic and copies ran while one was open for 0% of the time, Pallas kernels for 14%

profile of v1, /device:TPU:0, one launch (start us, length us, event | category | flops | bytes accessed | tf_op | source)
XLA Modules:
  0.0 33.6 jit_solution(11517702266805705957)
XLA Ops:
  0.0 0.0 copy-start.1
  0.0 0.2 tables.1
  0.2 1.1 %copy-done.1 = f32[4,8,8192]{2,1,0:T(8,128)S(1)} copy-done((f32[4,8,8192]{2,1,0:T(8,128)S(1)}, f32[4,8,8192]{2,1,0:T(8,128)}, u32[]{:S(2)}) %copy-start.1) | copy-done | bytes 1048600
  1.2 3.3 %spectra.1 = (bf16[4,8,32,128]{3,2,1,0:T(8,128)(2,1)S(1)}, bf16[4,8,32,128]{3,2,1,0:T(8,128)(2,1)S(1)}) custom-call(f32[4,64,8,128]{3,2,1,0:T(8,128)S(1)} %bitcast.8, f32[2,64,128]{2,1,0:T(8,128)S(1)} %get-tuple-element.18.tw_ref, bf16[128,1536]{1,0:T(8,128)(2,1)S(1)} %get-tuple-element.19.l2_ref), custom_call_target="tpu_custom_call" | custom-call | flops 4400000000 | tf_op jit(solution)/shard_map/spectra/pallas_call | solution.py:183
  4.6 3.0 %collective-permute-start = (bf16[4,8,32,128]{3,2,1,0:T(8,128)(2,1)S(1)}, bf16[4,8,32,128]{3,2,1,0:T(8,128)(2,1)S(1)}, u32[]{:S(2)}, u32[]{:S(2)}) collective-permute-start(bf16[4,8,32,128]{3,2,1,0:T(8,128)(2,1)S(1)} %get-tuple-element.21), channel_id=1, source_target_pairs={{0,1},{1,0},{2,3},{3,2},{4,5},{5,4},{6,7},{7,6},{8,9},{9,8},{10,11... | collective-permute-start | bytes 786440 | tf_op jit(solution)/shard_map/ppermute | solution.py:341
  7.6 1.3 %collective-permute-start.2 = (bf16[4,8,32,128]{3,2,1,0:T(8,128)(2,1)S(1)}, bf16[4,8,32,128]{3,2,1,0:T(8,128)(2,1)S(1)}, u32[]{:S(2)}, u32[]{:S(2)}) collective-permute-start(bf16[4,8,32,128]{3,2,1,0:T(8,128)(2,1)S(1)} %get-tuple-element.20.refs_1_.own_ref), channel_id=1, source_target_pairs={{8,0},{10,2},{12,4},{14,6},{16,8},{18,10},{20,12},{22,14},{24,16},... | collective-permute-start | bytes 786440 | tf_op jit(solution)/shard_map/ppermute | solution.py:342
  8.9 5.0 %collective-permute-done.refs_2_.own_ref = bf16[4,8,32,128]{3,2,1,0:T(8,128)(2,1)S(1)} collective-permute-done((bf16[4,8,32,128]{3,2,1,0:T(8,128)(2,1)S(1)}, bf16[4,8,32,128]{3,2,1,0:T(8,128)(2,1)S(1)}, u32[]{:S(2)}, u32[]{:S(2)}) %collective-permute-start) | collective-permute-done | bytes 262176 | tf_op jit(solution)/shard_map/ppermute | solution.py:341
  13.9 1.3 %collective-permute-start.1 = (bf16[4,8,32,128]{3,2,1,0:T(8,128)(2,1)S(1)}, bf16[4,8,32,128]{3,2,1,0:T(8,128)(2,1)S(1)}, u32[]{:S(2)}, u32[]{:S(2)}) collective-permute-start(bf16[4,8,32,128]{3,2,1,0:T(8,128)(2,1)S(1)} %collective-permute-done.refs_2_.own_ref), channel_id=1, source_target_pairs={{8,0},{10,2},{12,4},{14,6},{16,8},{18,10},{20,12},{22,14},{24,16},... | collective-permute-start | bytes 786440 | tf_op jit(solution)/shard_map/ppermute | solution.py:342
  15.2 2.1 %collective-permute-done.2.refs_3_.far_ref = bf16[4,8,32,128]{3,2,1,0:T(8,128)(2,1)S(1)} collective-permute-done((bf16[4,8,32,128]{3,2,1,0:T(8,128)(2,1)S(1)}, bf16[4,8,32,128]{3,2,1,0:T(8,128)(2,1)S(1)}, u32[]{:S(2)}, u32[]{:S(2)}) %collective-permute-start.2) | collective-permute-done | bytes 262176 | tf_op jit(solution)/shard_map/ppermute | solution.py:342
  17.3 0.0 copy-start
  17.3 1.6 %collective-permute-start.4 = (bf16[4,8,32,128]{3,2,1,0:T(8,128)(2,1)S(1)}, bf16[4,8,32,128]{3,2,1,0:T(8,128)(2,1)S(1)}, u32[]{:S(2)}, u32[]{:S(2)}) collective-permute-start(bf16[4,8,32,128]{3,2,1,0:T(8,128)(2,1)S(1)} %choose.5), channel_id=1, source_target_pairs={{0,4},{2,6},{4,0},{6,2},{8,12},{10,14},{12,8},{14,10},{16,20},{18,... | collective-permute-start | bytes 786440 | tf_op jit(solution)/shard_map/ppermute | solution.py:354
  18.9 0.1 collective-permute-start.5
  19.0 0.0 copy-done
  19.0 0.9 %cross_far.1.refs_6_ = f32[4,4,32,128]{3,2,1,0:T(8,128)S(1)} custom-call(s32[64]{0:T(128)S(1)} %copy-done, bf16[4,8,32,128]{3,2,1,0:T(8,128)(2,1)S(1)} %get-tuple-element.20.refs_1_.own_ref, bf16[4,8,32,128]{3,2,1,0:T(8,128)(2,1)S(1)} %collective-permute-done.refs_2_.own_ref, bf16[4,8,32,128]{3,2,1,0:T(8,128)(2,1)S(1)} %collective-permute-done.2.refs_3_.far_ref), custom_call_target="tpu_custom_call" | custom-call | flops 660000000 | tf_op jit(solution)/shard_map/cross_far/pallas_call | solution.py:292
  19.9 3.4 %collective-permute-done.1.far_ref.refs_3_ = bf16[4,8,32,128]{3,2,1,0:T(8,128)(2,1)S(1)} collective-permute-done((bf16[4,8,32,128]{3,2,1,0:T(8,128)(2,1)S(1)}, bf16[4,8,32,128]{3,2,1,0:T(8,128)(2,1)S(1)}, u32[]{:S(2)}, u32[]{:S(2)}) %collective-permute-start.1) | collective-permute-done | bytes 262176 | tf_op jit(solution)/shard_map/ppermute | solution.py:342
  23.3 1.4 %collective-permute-start.3 = (bf16[4,8,32,128]{3,2,1,0:T(8,128)(2,1)S(1)}, bf16[4,8,32,128]{3,2,1,0:T(8,128)(2,1)S(1)}, u32[]{:S(2)}, u32[]{:S(2)}) collective-permute-start(bf16[4,8,32,128]{3,2,1,0:T(8,128)(2,1)S(1)} %choose.4), channel_id=1, source_target_pairs={{0,4},{2,6},{4,0},{6,2},{8,12},{10,14},{12,8},{14,10},{16,20},{18,... | collective-permute-start | bytes 786440 | tf_op jit(solution)/shard_map/ppermute | solution.py:354
  24.8 0.1 collective-permute-start.7
  24.9 0.0 collective-permute-done.4.refs_4_
  24.9 0.5 %collective-permute-start.8 = (bf16[4,8,32,128]{3,2,1,0:T(8,128)(2,1)S(1)}, bf16[4,8,32,128]{3,2,1,0:T(8,128)(2,1)S(1)}, u32[]{:S(2)}, u32[]{:S(2)}) collective-permute-start(bf16[4,8,32,128]{3,2,1,0:T(8,128)(2,1)S(1)} %collective-permute-done.4.refs_4_), channel_id=1, source_target_pairs={{0,2},{2,0},{4,6},{6,4},{8,10},{10,8},{12,14},{14,12},{16,18},{18,... | collective-permute-start | bytes 786440 | tf_op jit(solution)/shard_map/ppermute | solution.py:357
  25.4 0.0 collective-permute-done.5.refs_5_
  25.4 1.8 %cross_most.1 = (f32[4,4,32,128]{3,2,1,0:T(8,128)S(1)}, f32[4,4,32,128]{3,2,1,0:T(8,128)S(1)}, f32[4,4,32,128]{3,2,1,0:T(8,128)S(1)}) custom-call(s32[64]{0:T(128)S(1)} %copy-done, bf16[4,8,32,128]{3,2,1,0:T(8,128)(2,1)S(1)} %get-tuple-element.20.refs_1_.own_ref, bf16[4,8,32,128]{3,2,1,0:T(8,128)(2,1)S(1)} %collective-permute-done.refs_2_.own_ref, ...), custom_call_target="tpu_custom_call" | custom-call | flops 1980000000 | tf_op jit(solution)/shard_map/cross_most/pallas_call | solution.py:292
  27.2 2.8 %collective-permute-done.3.refs_3_ = bf16[4,8,32,128]{3,2,1,0:T(8,128)(2,1)S(1)} collective-permute-done((bf16[4,8,32,128]{3,2,1,0:T(8,128)(2,1)S(1)}, bf16[4,8,32,128]{3,2,1,0:T(8,128)(2,1)S(1)}, u32[]{:S(2)}, u32[]{:S(2)}) %collective-permute-start.3) | collective-permute-done | bytes 262176 | tf_op jit(solution)/shard_map/ppermute | solution.py:354
  30.0 0.0 collective-permute-start.6
  30.0 0.0 collective-permute-done.7.refs_4_
  30.0 0.0 collective-permute-done.8.refs_5_
  30.0 1.8 %cross_next.1 = (f32[4,4,32,128]{3,2,1,0:T(8,128)S(1)}, f32[4,4,32,128]{3,2,1,0:T(8,128)S(1)}, f32[4,4,32,128]{3,2,1,0:T(8,128)S(1)}) custom-call(s32[64]{0:T(128)S(1)} %copy-done, bf16[4,8,32,128]{3,2,1,0:T(8,128)(2,1)S(1)} %get-tuple-element.20.refs_1_.own_ref, bf16[4,8,32,128]{3,2,1,0:T(8,128)(2,1)S(1)} %collective-permute-done.refs_2_.own_ref, ...), custom_call_target="tpu_custom_call" | custom-call | flops 1980000000 | tf_op jit(solution)/shard_map/cross_next/pallas_call | solution.py:292
  31.8 0.0 collective-permute-done.6.refs_3_
  31.8 1.7 %cross_last.1 = f32[4,4,4,32,128]{4,3,2,1,0:T(8,128)} custom-call(s32[64]{0:T(128)S(1)} %copy-done, bf16[4,8,32,128]{3,2,1,0:T(8,128)(2,1)S(1)} %get-tuple-element.20.refs_1_.own_ref, bf16[4,8,32,128]{3,2,1,0:T(8,128)(2,1)S(1)} %collective-permute-done.refs_2_.own_ref, bf16[4,8,32,128]{3,2,1,0:T(8,128)(2,1)S(1)} %collective-permute-done.6.refs_3_, ...), custom_call_target="tpu_custom_call" | custom-call | flops 660000000 | tf_op jit(solution)/shard_map/cross_last/pallas_call | solution.py:292
  (4 shorter events, 0.1 us)
Async XLA Ops:
  0.0 1.2 %copy-start.1 = (f32[4,8,8192]{2,1,0:T(8,128)S(1)}, f32[4,8,8192]{2,1,0:T(8,128)}, u32[]{:S(2)}) copy-start(f32[4,8,8192]{2,1,0:T(8,128)} %param.2) | copy-start | bytes 3145732
  4.6 9.3 %collective-permute-start = (bf16[4,8,32,128]{3,2,1,0:T(8,128)(2,1)S(1)}, bf16[4,8,32,128]{3,2,1,0:T(8,128)(2,1)S(1)}, u32[]{:S(2)}, u32[]{:S(2)}) collective-permute-start(bf16[4,8,32,128]{3,2,1,0:T(8,128)(2,1)S(1)} %get-tuple-element.21), channel_id=1, source_target_pairs={{0,1},{1,0},{2,3},{3,2},{4,5},{5,4},{6,7},{7,6},{8,9},{9,8},{10,11... | collective-permute-start | bytes 786440 | tf_op jit(solution)/shard_map/ppermute | solution.py:341
  7.6 9.7 %collective-permute-start.2 = (bf16[4,8,32,128]{3,2,1,0:T(8,128)(2,1)S(1)}, bf16[4,8,32,128]{3,2,1,0:T(8,128)(2,1)S(1)}, u32[]{:S(2)}, u32[]{:S(2)}) collective-permute-start(bf16[4,8,32,128]{3,2,1,0:T(8,128)(2,1)S(1)} %get-tuple-element.20.refs_1_.own_ref), channel_id=1, source_target_pairs={{8,0},{10,2},{12,4},{14,6},{16,8},{18,10},{20,12},{22,14},{24,16},... | collective-permute-start | bytes 786440 | tf_op jit(solution)/shard_map/ppermute | solution.py:342
  13.9 9.4 %collective-permute-start.1 = (bf16[4,8,32,128]{3,2,1,0:T(8,128)(2,1)S(1)}, bf16[4,8,32,128]{3,2,1,0:T(8,128)(2,1)S(1)}, u32[]{:S(2)}, u32[]{:S(2)}) collective-permute-start(bf16[4,8,32,128]{3,2,1,0:T(8,128)(2,1)S(1)} %collective-permute-done.refs_2_.own_ref), channel_id=1, source_target_pairs={{8,0},{10,2},{12,4},{14,6},{16,8},{18,10},{20,12},{22,14},{24,16},... | collective-permute-start | bytes 786440 | tf_op jit(solution)/shard_map/ppermute | solution.py:342
  17.3 1.7 %copy-start = (s32[64]{0:T(128)S(1)}, s32[64]{0:T(128)}, u32[]{:S(2)}) copy-start(s32[64]{0:T(128)} %refs_0_.7) | copy-start | bytes 772
  17.3 7.6 %collective-permute-start.4 = (bf16[4,8,32,128]{3,2,1,0:T(8,128)(2,1)S(1)}, bf16[4,8,32,128]{3,2,1,0:T(8,128)(2,1)S(1)}, u32[]{:S(2)}, u32[]{:S(2)}) collective-permute-start(bf16[4,8,32,128]{3,2,1,0:T(8,128)(2,1)S(1)} %choose.5), channel_id=1, source_target_pairs={{0,4},{2,6},{4,0},{6,2},{8,12},{10,14},{12,8},{14,10},{16,20},{18,... | collective-permute-start | bytes 786440 | tf_op jit(solution)/shard_map/ppermute | solution.py:354
  18.9 6.5 %collective-permute-start.5 = (bf16[4,8,32,128]{3,2,1,0:T(8,128)(2,1)S(1)}, bf16[4,8,32,128]{3,2,1,0:T(8,128)(2,1)S(1)}, u32[]{:S(2)}, u32[]{:S(2)}) collective-permute-start(bf16[4,8,32,128]{3,2,1,0:T(8,128)(2,1)S(1)} %choose.6), channel_id=1, source_target_pairs={{0,2},{2,0},{4,6},{6,4},{8,10},{10,8},{12,14},{14,12},{16,18},{18,... | collective-permute-start | bytes 786440 | tf_op jit(solution)/shard_map/ppermute | solution.py:355
  23.3 6.6 %collective-permute-start.3 = (bf16[4,8,32,128]{3,2,1,0:T(8,128)(2,1)S(1)}, bf16[4,8,32,128]{3,2,1,0:T(8,128)(2,1)S(1)}, u32[]{:S(2)}, u32[]{:S(2)}) collective-permute-start(bf16[4,8,32,128]{3,2,1,0:T(8,128)(2,1)S(1)} %choose.4), channel_id=1, source_target_pairs={{0,4},{2,6},{4,0},{6,2},{8,12},{10,14},{12,8},{14,10},{16,20},{18,... | collective-permute-start | bytes 786440 | tf_op jit(solution)/shard_map/ppermute | solution.py:354
  24.8 5.2 %collective-permute-start.7 = (bf16[4,8,32,128]{3,2,1,0:T(8,128)(2,1)S(1)}, bf16[4,8,32,128]{3,2,1,0:T(8,128)(2,1)S(1)}, u32[]{:S(2)}, u32[]{:S(2)}) collective-permute-start(bf16[4,8,32,128]{3,2,1,0:T(8,128)(2,1)S(1)} %choose.7), channel_id=1, source_target_pairs={{0,2},{2,0},{4,6},{6,4},{8,10},{10,8},{12,14},{14,12},{16,18},{18,... | collective-permute-start | bytes 786440 | tf_op jit(solution)/shard_map/ppermute | solution.py:355
  24.9 5.1 %collective-permute-start.8 = (bf16[4,8,32,128]{3,2,1,0:T(8,128)(2,1)S(1)}, bf16[4,8,32,128]{3,2,1,0:T(8,128)(2,1)S(1)}, u32[]{:S(2)}, u32[]{:S(2)}) collective-permute-start(bf16[4,8,32,128]{3,2,1,0:T(8,128)(2,1)S(1)} %collective-permute-done.4.refs_4_), channel_id=1, source_target_pairs={{0,2},{2,0},{4,6},{6,4},{8,10},{10,8},{12,14},{14,12},{16,18},{18,... | collective-permute-start | bytes 786440 | tf_op jit(solution)/shard_map/ppermute | solution.py:357
  30.0 1.9 %collective-permute-start.6 = (bf16[4,8,32,128]{3,2,1,0:T(8,128)(2,1)S(1)}, bf16[4,8,32,128]{3,2,1,0:T(8,128)(2,1)S(1)}, u32[]{:S(2)}, u32[]{:S(2)}) collective-permute-start(bf16[4,8,32,128]{3,2,1,0:T(8,128)(2,1)S(1)} %collective-permute-done.3.refs_3_), channel_id=1, source_target_pairs={{0,2},{2,0},{4,6},{6,4},{8,10},{10,8},{12,14},{14,12},{16,18},{18,... | collective-permute-start | bytes 786440 | tf_op jit(solution)/shard_map/ppermute | solution.py:369

commit v2 on v1

--- a/solution.py
+++ b/solution.py
@@ -137,6 +137,29 @@
     return jnp.where(minus_cos, -cos, cos), jnp.where(minus_sin, -sin, sin)
 
 
+def gains_kernel(chans, inv_root, pos_ref, gain_ref):
+    block = lax.axis_index("chan")
+    last = pos_ref.shape[0] - 1
+    for row in range(ROUNDS * chans * chans):
+        rnd, a, c = row // (chans * chans), row // chans % chans, row % chans
+        pos_c = pos_ref[lax.min((block + rnd + 1) * chans + c, last)]
+        near = pos_c - pos_ref[block * chans + a] <= REACH
+        gain = jnp.where(near, inv_root, 0.0).astype(jnp.float32)
+        gain_ref[pl.ds(row, 1), :] = jnp.full((1, LANES), gain)
+
+
+def stack_gains(positions, chans, windows):
+    return pl.pallas_call(
+        functools.partial(gains_kernel, chans, 1.0 / math.sqrt(windows)),
+        in_specs=[SMEM],
+        out_specs=VMEM,
+        out_shape=jax.ShapeDtypeStruct((ROUNDS * chans * chans, LANES), jnp.float32),
+        compiler_params=PARAMS,
+        cost_estimate=cost(0.5),
+        name="gains",
+    )(positions)
+
+
 def tables_kernel(parts, samples, tw_ref, l2_ref):
     first = samples // LANES
     bands = BINS // BAND // parts
@@ -196,7 +219,7 @@
     rows = mine[0][0].shape[1]
     bands = rows // 2
     wins = mine[0][0].shape[0]
-    per_step = 4 if wins % 4 == 0 else 1
+    per_step = wins if wins <= 8 else 1
 
     def planes(ref, win):
         return [ref[win, pl.ds(i * bands, bands), :].astype(jnp.float32) for i in range(2)]
@@ -220,19 +243,17 @@
     return acc
 
 
-def cross_kernel(layout, jobs, inv_root, *refs):
+def cross_kernel(layout, jobs, *refs):
     groups, at = {}, 0
     for name, count in layout:
         groups[name] = refs[at : at + count]
         at += count
-    (pos_ref,) = groups["pos"]
+    (gain_ref,) = groups["gains"]
     mine = groups["mine"]
     chans, _, rows, _ = mine[0].shape
     bands = rows // 2
-    me = lax.axis_index("chan")
-    odd = lax.rem(me, 2)
+    odd = lax.rem(lax.axis_index("chan"), 2)
     rounds = {"one": 2 * odd, "mid": 1, "two": 2 - 2 * odd, "far": 3}
-    last = pos_ref.shape[0] - 1
     step = 2
     copies = []
 
@@ -267,9 +288,7 @@
                     if not final:
                         to_ref[a, c, pl.ds(i * bands, bands), :] = value
                         continue
-                    pos_c = pos_ref[lax.min((me + rnd + 1) * chans + c, last)]
-                    near = pos_c - pos_ref[me * chans + a] <= REACH
-                    gain = jnp.where(near, inv_root, 0.0).astype(jnp.float32)
+                    gain = gain_ref[pl.ds((rnd * chans + a) * chans + c, 1), :]
                     to_ref[a, c, pl.ds(i, bands, stride=2), :] = value * gain
             if to is None:
                 send(source, to_ref, a_start, len(a_list))
@@ -277,10 +296,11 @@
         copy.wait()
 
 
-def cross_call(name, jobs, inv_root, positions, mine, sources, acc_in=(), done=()):
+def cross_call(name, jobs, gains, mine, sources, acc_in=(), done=()):
     chans, _, rows, _ = mine[0].shape
-    groups = [("pos", [positions]), ("mine", mine), *sources.items()]
+    groups = [("gains", [gains]), ("mine", mine), *sources.items()]
     groups += [("acc_in", acc_in), ("done", done)]
+    groups = [(key, list(arrays)) for key, arrays in groups]
     operands = [array for _, arrays in groups for array in arrays]
     layout = [(key, len(arrays)) for key, arrays in groups]
     sums = jax.ShapeDtypeStruct((chans, chans, rows, LANES), jnp.float32)
@@ -290,8 +310,8 @@
     layout += [("out", ends), ("acc_out", acc_count), ("buffer", ends), ("sems", ends)]
     scratch = [pltpu.VMEM(sums.shape, jnp.float32), pltpu.SemaphoreType.DMA((chans + len(done),))]
     return pl.pallas_call(
-        functools.partial(cross_kernel, layout, jobs, inv_root),
-        in_specs=[SMEM] + [VMEM] * (len(operands) - 1),
+        functools.partial(cross_kernel, layout, jobs),
+        in_specs=[VMEM] * len(operands),
         out_specs=[HBM] * ends + [VMEM] * acc_count,
         out_shape=[whole] * ends + [sums] * acc_count,
         scratch_shapes=scratch * ends,
@@ -331,7 +351,7 @@
 def shards(records, positions):
     parts = lax.axis_size("win")
     blocks = lax.axis_size("chan")
-    wins = records.shape[1]
+    chans, wins, _ = records.shape
     spectra = whitened_spectra(records, parts)
     up = [(b, b - 4) for b in range(4, blocks)]
     swap2 = [(b, b ^ 2) for b in range(blocks)]
@@ -342,8 +362,8 @@
     far = [lax.ppermute(own, "chan", up) for own in mine]
     last = parts - 1
     early = range(last)
-    inv_root = 1.0 / math.sqrt(parts * wins)
-    call = functools.partial(cross_call, inv_root=inv_root, positions=positions, mine=mine)
+    gains = stack_gains(after(positions, far[0]), chans, parts * wins)
+    call = functools.partial(cross_call, gains=gains, mine=mine)
 
     (acc_far,) = call(
         "cross_far", [("far", [(s, s) for s in early], None, False, 0)], sources={"far": far[:-1]}
@@ -382,7 +402,7 @@
         "cross_last", [("two", [(last, 0)], 0, True, None)], sources={"two": two[last:]},
         acc_in=[acc_two], done=[done_far, done_mid, done_one],
     )
-    chans, bands = out.shape[1], out.shape[3] // 2
+    bands = out.shape[3] // 2
     out = out.reshape(ROUNDS, chans, chans, bands, 2, LANES).transpose(0, 1, 2, 4, 3, 5)
     return out.reshape(ROUNDS, chans, chans, 2, bands * LANES)
 

time: 33.8 us -> 32.8 us (0.970)
  Pallas kernels: 9.84 us -> 7.33 us
  waiting for transfers between devices: 13.3 us -> 14.8 us
    pallas_call x4 -> x5, Pallas kernels: 6.28 us -> 3.77 us  [the longest x4 3.09 us: cross_call(): pl.pallas_call(functools.partial(cross_kernel, layout, jobs), in_specs=[V...]
    ppermute x2, waiting for transfers between devices: 2.8 us -> 3.77 us  [shards(): mid.append(lax.ppermute(choose(2, mine[s], far[s]), 'chan', swap2))]
    ppermute x1, waiting for transfers between devices: 0.01 us -> 0.58 us  [shards(): two.append(lax.ppermute(mid[last], 'chan', swap1))]
  transfers between devices with their start and end apart: 9 -> 9, of which waited for: 4 -> 5; matrix products, arithmetic and copies ran while one was open for 0% -> 0% of each run, Pallas kernels for 14% -> 8%
where the time goes in v2:
time: 32.8 us; the launch traced here: 32.6 us
  waiting for transfers between devices  14.8 us (45%)
  starting transfers between devices  9.22 us (28%)
  Pallas kernels  7.33 us (22%)
  local copies, waits for them, and re-layouts  1.07 us (3%)
    ppermute x2, waiting for transfers between devices, shards(): far = [lax.ppermute(own, 'chan', up) for own in mine]  5.45 us
    ppermute x1, waiting for transfers between devices, shards(): lax.ppermute(spectra[s], 'win', [(i, (i + s) % parts) for i in range(part...  5.03 us
    ppermute x2, waiting for transfers between devices, shards(): mid.append(lax.ppermute(choose(2, mine[s], far[s]), 'chan', swap2))  3.77 us
    pallas_call x1, Pallas kernels, whitened_spectra(): pl.pallas_call(functools.partial(spectra_kernel, parts), in_specs=[VMEM]...  3.34 us
    pallas_call x4, Pallas kernels, cross_call(): pl.pallas_call(functools.partial(cross_kernel, layout, jobs), in_specs=[V...  3.09 us
    ppermute x1, starting transfers between devices, shards(): lax.ppermute(spectra[s], 'win', [(i, (i + s) % parts) for i in range(part...  3.03 us
    ppermute x2, starting transfers between devices, shards(): mid.append(lax.ppermute(choose(2, mine[s], far[s]), 'chan', swap2))  3 us
    ppermute x2, starting transfers between devices, shards(): far = [lax.ppermute(own, 'chan', up) for own in mine]  2.56 us
  transfers between devices with their start and end apart: 9, of which 5 were waited for; matrix products, arithmetic and copies ran while one was open for 0% of the time, Pallas kernels for 8%

profile of v2, /device:TPU:0, one launch (start us, length us, event | category | flops | bytes accessed | tf_op | source)
XLA Modules:
  0.0 32.6 jit_solution(4308393111099151333)
XLA Ops:
  0.0 0.0 copy-start
  0.0 0.2 tables.1
  0.2 1.1 %copy-done = f32[4,8,8192]{2,1,0:T(8,128)S(1)} copy-done((f32[4,8,8192]{2,1,0:T(8,128)S(1)}, f32[4,8,8192]{2,1,0:T(8,128)}, u32[]{:S(2)}) %copy-start) | copy-done | bytes 1048600
  1.2 3.3 %spectra.1 = (bf16[4,8,32,128]{3,2,1,0:T(8,128)(2,1)S(1)}, bf16[4,8,32,128]{3,2,1,0:T(8,128)(2,1)S(1)}) custom-call(f32[4,64,8,128]{3,2,1,0:T(8,128)S(1)} %bitcast.8, f32[2,64,128]{2,1,0:T(8,128)S(1)} %get-tuple-element.19.tw_ref, bf16[128,1536]{1,0:T(8,128)(2,1)S(1)} %get-tuple-element.20.l2_ref), custom_call_target="tpu_custom_call" | custom-call | flops 4400000000 | tf_op jit(solution)/shard_map/spectra/pallas_call | solution.py:206
  4.6 3.0 %collective-permute-start.1 = (bf16[4,8,32,128]{3,2,1,0:T(8,128)(2,1)S(1)}, bf16[4,8,32,128]{3,2,1,0:T(8,128)(2,1)S(1)}, u32[]{:S(2)}, u32[]{:S(2)}) collective-permute-start(bf16[4,8,32,128]{3,2,1,0:T(8,128)(2,1)S(1)} %get-tuple-element.23), channel_id=1, source_target_pairs={{0,1},{1,0},{2,3},{3,2},{4,5},{5,4},{6,7},{7,6},{8,9},{9,8},{10,11... | collective-permute-start | bytes 786440 | tf_op jit(solution)/shard_map/ppermute | solution.py:361
  7.6 1.3 %collective-permute-start = (bf16[4,8,32,128]{3,2,1,0:T(8,128)(2,1)S(1)}, bf16[4,8,32,128]{3,2,1,0:T(8,128)(2,1)S(1)}, u32[]{:S(2)}, u32[]{:S(2)}) collective-permute-start(bf16[4,8,32,128]{3,2,1,0:T(8,128)(2,1)S(1)} %get-tuple-element.21.refs_1_.own_ref), channel_id=1, source_target_pairs={{8,0},{10,2},{12,4},{14,6},{16,8},{18,10},{20,12},{22,14},{24,16},... | collective-permute-start | bytes 786440 | tf_op jit(solution)/shard_map/ppermute | solution.py:362
  8.9 5.0 %collective-permute-done.1.refs_2_.own_ref = bf16[4,8,32,128]{3,2,1,0:T(8,128)(2,1)S(1)} collective-permute-done((bf16[4,8,32,128]{3,2,1,0:T(8,128)(2,1)S(1)}, bf16[4,8,32,128]{3,2,1,0:T(8,128)(2,1)S(1)}, u32[]{:S(2)}, u32[]{:S(2)}) %collective-permute-start.1) | collective-permute-done | bytes 262176 | tf_op jit(solution)/shard_map/ppermute | solution.py:361
  13.9 1.3 %collective-permute-start.2 = (bf16[4,8,32,128]{3,2,1,0:T(8,128)(2,1)S(1)}, bf16[4,8,32,128]{3,2,1,0:T(8,128)(2,1)S(1)}, u32[]{:S(2)}, u32[]{:S(2)}) collective-permute-start(bf16[4,8,32,128]{3,2,1,0:T(8,128)(2,1)S(1)} %collective-permute-done.1.refs_2_.own_ref), channel_id=1, source_target_pairs={{8,0},{10,2},{12,4},{14,6},{16,8},{18,10},{20,12},{22,14},{24,16},... | collective-permute-start | bytes 786440 | tf_op jit(solution)/shard_map/ppermute | solution.py:362
  15.2 2.1 %collective-permute-done.refs_3_.far_ref = bf16[4,8,32,128]{3,2,1,0:T(8,128)(2,1)S(1)} collective-permute-done((bf16[4,8,32,128]{3,2,1,0:T(8,128)(2,1)S(1)}, bf16[4,8,32,128]{3,2,1,0:T(8,128)(2,1)S(1)}, u32[]{:S(2)}, u32[]{:S(2)}) %collective-permute-start) | collective-permute-done | bytes 262176 | tf_op jit(solution)/shard_map/ppermute | solution.py:362
  17.3 0.0 copy-start.1
  17.3 1.6 %collective-permute-start.4 = (bf16[4,8,32,128]{3,2,1,0:T(8,128)(2,1)S(1)}, bf16[4,8,32,128]{3,2,1,0:T(8,128)(2,1)S(1)}, u32[]{:S(2)}, u32[]{:S(2)}) collective-permute-start(bf16[4,8,32,128]{3,2,1,0:T(8,128)(2,1)S(1)} %choose.5), channel_id=1, source_target_pairs={{0,4},{2,6},{4,0},{6,2},{8,12},{10,14},{12,8},{14,10},{16,20},{18,... | collective-permute-start | bytes 786440 | tf_op jit(solution)/shard_map/ppermute | solution.py:374
  18.9 0.1 collective-permute-start.5
  19.0 0.0 copy-done.1
  19.0 0.7 %gains.1.refs_0_ = f32[64,128]{1,0:T(8,128)S(1)} custom-call(s32[64]{0:T(128)S(1)} %copy-done.1), custom_call_target="tpu_custom_call" | custom-call | flops 550000000 | tf_op jit(solution)/shard_map/gains/pallas_call | solution.py:152
  19.6 0.2 cross_far.1.refs_6_
  19.9 3.4 %collective-permute-done.2.far_ref.refs_3_ = bf16[4,8,32,128]{3,2,1,0:T(8,128)(2,1)S(1)} collective-permute-done((bf16[4,8,32,128]{3,2,1,0:T(8,128)(2,1)S(1)}, bf16[4,8,32,128]{3,2,1,0:T(8,128)(2,1)S(1)}, u32[]{:S(2)}, u32[]{:S(2)}) %collective-permute-start.2) | collective-permute-done | bytes 262176 | tf_op jit(solution)/shard_map/ppermute | solution.py:362
  23.3 1.4 %collective-permute-start.3 = (bf16[4,8,32,128]{3,2,1,0:T(8,128)(2,1)S(1)}, bf16[4,8,32,128]{3,2,1,0:T(8,128)(2,1)S(1)}, u32[]{:S(2)}, u32[]{:S(2)}) collective-permute-start(bf16[4,8,32,128]{3,2,1,0:T(8,128)(2,1)S(1)} %choose.4), channel_id=1, source_target_pairs={{0,4},{2,6},{4,0},{6,2},{8,12},{10,14},{12,8},{14,10},{16,20},{18,... | collective-permute-start | bytes 786440 | tf_op jit(solution)/shard_map/ppermute | solution.py:374
  24.8 0.1 collective-permute-start.7
  24.9 0.0 collective-permute-done.4.refs_4_
  24.9 0.5 %collective-permute-start.8 = (bf16[4,8,32,128]{3,2,1,0:T(8,128)(2,1)S(1)}, bf16[4,8,32,128]{3,2,1,0:T(8,128)(2,1)S(1)}, u32[]{:S(2)}, u32[]{:S(2)}) collective-permute-start(bf16[4,8,32,128]{3,2,1,0:T(8,128)(2,1)S(1)} %collective-permute-done.4.refs_4_), channel_id=1, source_target_pairs={{0,2},{2,0},{4,6},{6,4},{8,10},{10,8},{12,14},{14,12},{16,18},{18,... | collective-permute-start | bytes 786440 | tf_op jit(solution)/shard_map/ppermute | solution.py:377
  25.4 0.0 collective-permute-done.5.refs_5_
  25.4 0.8 %cross_most.1 = (f32[4,4,32,128]{3,2,1,0:T(8,128)S(1)}, f32[4,4,32,128]{3,2,1,0:T(8,128)S(1)}, f32[4,4,32,128]{3,2,1,0:T(8,128)S(1)}) custom-call(f32[64,128]{1,0:T(8,128)S(1)} %gains.1.refs_0_, bf16[4,8,32,128]{3,2,1,0:T(8,128)(2,1)S(1)} %get-tuple-element.21.refs_1_.own_ref, bf16[4,8,32,128]{3,2,1,0:T(8,128)(2,1)S(1)} %collective-permute-done.1.refs_2_.own_ref, ...), custom_call_target="tpu_custom_call" | custom-call | flops 1980000000 | tf_op jit(solution)/shard_map/cross_most/pallas_call | solution.py:312
  26.2 3.8 %collective-permute-done.3.refs_3_ = bf16[4,8,32,128]{3,2,1,0:T(8,128)(2,1)S(1)} collective-permute-done((bf16[4,8,32,128]{3,2,1,0:T(8,128)(2,1)S(1)}, bf16[4,8,32,128]{3,2,1,0:T(8,128)(2,1)S(1)}, u32[]{:S(2)}, u32[]{:S(2)}) %collective-permute-start.3) | collective-permute-done | bytes 262176 | tf_op jit(solution)/shard_map/ppermute | solution.py:374
  30.0 0.0 collective-permute-start.6
  30.0 0.0 collective-permute-done.7.refs_4_
  30.0 0.0 collective-permute-done.8.refs_5_
  30.0 0.9 %cross_next.1 = (f32[4,4,32,128]{3,2,1,0:T(8,128)S(1)}, f32[4,4,32,128]{3,2,1,0:T(8,128)S(1)}, f32[4,4,32,128]{3,2,1,0:T(8,128)S(1)}) custom-call(f32[64,128]{1,0:T(8,128)S(1)} %gains.1.refs_0_, bf16[4,8,32,128]{3,2,1,0:T(8,128)(2,1)S(1)} %get-tuple-element.21.refs_1_.own_ref, bf16[4,8,32,128]{3,2,1,0:T(8,128)(2,1)S(1)} %collective-permute-done.1.refs_2_.own_ref, ...), custom_call_target="tpu_custom_call" | custom-call | flops 1980000000 | tf_op jit(solution)/shard_map/cross_next/pallas_call | solution.py:312
  30.9 0.6 %collective-permute-done.6.refs_3_ = bf16[4,8,32,128]{3,2,1,0:T(8,128)(2,1)S(1)} collective-permute-done((bf16[4,8,32,128]{3,2,1,0:T(8,128)(2,1)S(1)}, bf16[4,8,32,128]{3,2,1,0:T(8,128)(2,1)S(1)}, u32[]{:S(2)}, u32[]{:S(2)}) %collective-permute-start.6) | collective-permute-done | bytes 262176 | tf_op jit(solution)/shard_map/ppermute | solution.py:389
  31.5 1.1 %cross_last.1 = f32[4,4,4,32,128]{4,3,2,1,0:T(8,128)} custom-call(f32[64,128]{1,0:T(8,128)S(1)} %gains.1.refs_0_, bf16[4,8,32,128]{3,2,1,0:T(8,128)(2,1)S(1)} %get-tuple-element.21.refs_1_.own_ref, bf16[4,8,32,128]{3,2,1,0:T(8,128)(2,1)S(1)} %collective-permute-done.1.refs_2_.own_ref, bf16[4,8,32,128]{3,2,1,0:T(8,128)(2,1)S(1)} %collective-permute-done.6.refs_3_, ...), custom_call_target="tpu_custom_call" | custom-call | flops 660000000 | tf_op jit(solution)/shard_map/cross_last/pallas_call | solution.py:312
  (4 shorter events, 0.1 us)
Async XLA Ops:
  0.0 1.2 %copy-start = (f32[4,8,8192]{2,1,0:T(8,128)S(1)}, f32[4,8,8192]{2,1,0:T(8,128)}, u32[]{:S(2)}) copy-start(f32[4,8,8192]{2,1,0:T(8,128)} %param.2) | copy-start | bytes 3145732
  4.6 9.3 %collective-permute-start.1 = (bf16[4,8,32,128]{3,2,1,0:T(8,128)(2,1)S(1)}, bf16[4,8,32,128]{3,2,1,0:T(8,128)(2,1)S(1)}, u32[]{:S(2)}, u32[]{:S(2)}) collective-permute-start(bf16[4,8,32,128]{3,2,1,0:T(8,128)(2,1)S(1)} %get-tuple-element.23), channel_id=1, source_target_pairs={{0,1},{1,0},{2,3},{3,2},{4,5},{5,4},{6,7},{7,6},{8,9},{9,8},{10,11... | collective-permute-start | bytes 786440 | tf_op jit(solution)/shard_map/ppermute | solution.py:361
  7.6 9.7 %collective-permute-start = (bf16[4,8,32,128]{3,2,1,0:T(8,128)(2,1)S(1)}, bf16[4,8,32,128]{3,2,1,0:T(8,128)(2,1)S(1)}, u32[]{:S(2)}, u32[]{:S(2)}) collective-permute-start(bf16[4,8,32,128]{3,2,1,0:T(8,128)(2,1)S(1)} %get-tuple-element.21.refs_1_.own_ref), channel_id=1, source_target_pairs={{8,0},{10,2},{12,4},{14,6},{16,8},{18,10},{20,12},{22,14},{24,16},... | collective-permute-start | bytes 786440 | tf_op jit(solution)/shard_map/ppermute | solution.py:362
  13.9 9.4 %collective-permute-start.2 = (bf16[4,8,32,128]{3,2,1,0:T(8,128)(2,1)S(1)}, bf16[4,8,32,128]{3,2,1,0:T(8,128)(2,1)S(1)}, u32[]{:S(2)}, u32[]{:S(2)}) collective-permute-start(bf16[4,8,32,128]{3,2,1,0:T(8,128)(2,1)S(1)} %collective-permute-done.1.refs_2_.own_ref), channel_id=1, source_target_pairs={{8,0},{10,2},{12,4},{14,6},{16,8},{18,10},{20,12},{22,14},{24,16},... | collective-permute-start | bytes 786440 | tf_op jit(solution)/shard_map/ppermute | solution.py:362
  17.3 1.7 %copy-start.1 = (s32[64]{0:T(128)S(1)}, s32[64]{0:T(128)}, u32[]{:S(2)}) copy-start(s32[64]{0:T(128)} %pos_ref) | copy-start | bytes 772
  17.3 7.6 %collective-permute-start.4 = (bf16[4,8,32,128]{3,2,1,0:T(8,128)(2,1)S(1)}, bf16[4,8,32,128]{3,2,1,0:T(8,128)(2,1)S(1)}, u32[]{:S(2)}, u32[]{:S(2)}) collective-permute-start(bf16[4,8,32,128]{3,2,1,0:T(8,128)(2,1)S(1)} %choose.5), channel_id=1, source_target_pairs={{0,4},{2,6},{4,0},{6,2},{8,12},{10,14},{12,8},{14,10},{16,20},{18,... | collective-permute-start | bytes 786440 | tf_op jit(solution)/shard_map/ppermute | solution.py:374
  18.9 6.5 %collective-permute-start.5 = (bf16[4,8,32,128]{3,2,1,0:T(8,128)(2,1)S(1)}, bf16[4,8,32,128]{3,2,1,0:T(8,128)(2,1)S(1)}, u32[]{:S(2)}, u32[]{:S(2)}) collective-permute-start(bf16[4,8,32,128]{3,2,1,0:T(8,128)(2,1)S(1)} %choose.6), channel_id=1, source_target_pairs={{0,2},{2,0},{4,6},{6,4},{8,10},{10,8},{12,14},{14,12},{16,18},{18,... | collective-permute-start | bytes 786440 | tf_op jit(solution)/shard_map/ppermute | solution.py:375
  23.3 6.6 %collective-permute-start.3 = (bf16[4,8,32,128]{3,2,1,0:T(8,128)(2,1)S(1)}, bf16[4,8,32,128]{3,2,1,0:T(8,128)(2,1)S(1)}, u32[]{:S(2)}, u32[]{:S(2)}) collective-permute-start(bf16[4,8,32,128]{3,2,1,0:T(8,128)(2,1)S(1)} %choose.4), channel_id=1, source_target_pairs={{0,4},{2,6},{4,0},{6,2},{8,12},{10,14},{12,8},{14,10},{16,20},{18,... | collective-permute-start | bytes 786440 | tf_op jit(solution)/shard_map/ppermute | solution.py:374
  24.8 5.2 %collective-permute-start.7 = (bf16[4,8,32,128]{3,2,1,0:T(8,128)(2,1)S(1)}, bf16[4,8,32,128]{3,2,1,0:T(8,128)(2,1)S(1)}, u32[]{:S(2)}, u32[]{:S(2)}) collective-permute-start(bf16[4,8,32,128]{3,2,1,0:T(8,128)(2,1)S(1)} %choose.7), channel_id=1, source_target_pairs={{0,2},{2,0},{4,6},{6,4},{8,10},{10,8},{12,14},{14,12},{16,18},{18,... | collective-permute-start | bytes 786440 | tf_op jit(solution)/shard_map/ppermute | solution.py:375
  24.9 5.1 %collective-permute-start.8 = (bf16[4,8,32,128]{3,2,1,0:T(8,128)(2,1)S(1)}, bf16[4,8,32,128]{3,2,1,0:T(8,128)(2,1)S(1)}, u32[]{:S(2)}, u32[]{:S(2)}) collective-permute-start(bf16[4,8,32,128]{3,2,1,0:T(8,128)(2,1)S(1)} %collective-permute-done.4.refs_4_), channel_id=1, source_target_pairs={{0,2},{2,0},{4,6},{6,4},{8,10},{10,8},{12,14},{14,12},{16,18},{18,... | collective-permute-start | bytes 786440 | tf_op jit(solution)/shard_map/ppermute | solution.py:377
  30.0 1.5 %collective-permute-start.6 = (bf16[4,8,32,128]{3,2,1,0:T(8,128)(2,1)S(1)}, bf16[4,8,32,128]{3,2,1,0:T(8,128)(2,1)S(1)}, u32[]{:S(2)}, u32[]{:S(2)}) collective-permute-start(bf16[4,8,32,128]{3,2,1,0:T(8,128)(2,1)S(1)} %collective-permute-done.3.refs_3_), channel_id=1, source_target_pairs={{0,2},{2,0},{4,6},{6,4},{8,10},{10,8},{12,14},{14,12},{16,18},{18,... | collective-permute-start | bytes 786440 | tf_op jit(solution)/shard_map/ppermute | solution.py:389

commit v3 on v2

--- a/solution.py
+++ b/solution.py
@@ -371,7 +371,10 @@
     far[last] = after(far[last], acc_far)
     mid, one, two = [], [], []
     for s in range(parts):
-        mid.append(lax.ppermute(choose(2, mine[s], far[s]), "chan", swap2))
+        if s < last:
+            mid.append(lax.ppermute(choose(2, mine[s], far[s]), "chan", swap2))
+        else:
+            mid.append(lax.ppermute(mine[s], "chan", [(b, b - 2) for b in range(2, blocks)]))
         one.append(lax.ppermute(choose(1, mine[s], far[s]), "chan", swap1))
         if s < last:
             two.append(lax.ppermute(mid[s], "chan", swap1))

time: 32.8 us -> 32.8 us (level)
    ppermute x2 -> x1, waiting for transfers between devices: 3.77 us -> 5.48 us  [shards(): mid.append(lax.ppermute(choose(2, mine[s], far[s]), 'chan', swap2))]
    ppermute x2 -> x1, starting transfers between devices: 3 us -> 1.56 us  [shards(): mid.append(lax.ppermute(choose(2, mine[s], far[s]), 'chan', swap2))]
    ppermute x2, waiting for transfers between devices: 5.45 us -> 4.15 us  [shards(): far = [lax.ppermute(own, 'chan', up) for own in mine]]
    ppermute x0 -> x1, starting transfers between devices: none -> 1.29 us  [shards(): lax.ppermute(mine[s], 'chan', [(b, b - 2) for b in range(2, blocks)])]
    ppermute x1, starting transfers between devices: 0.49 us -> 0.01 us  [shards(): two.append(lax.ppermute(mid[s], 'chan', swap1))]
    ppermute x1, waiting for transfers between devices: 0.58 us -> 0.11 us  [shards(): two.append(lax.ppermute(mid[last], 'chan', swap1))]
    ppermute x1, starting transfers between devices: 0.01 us -> 0.46 us  [shards(): two.append(lax.ppermute(mid[last], 'chan', swap1))]
  transfers between devices with their start and end apart: 9 -> 9, of which waited for: 5 -> 7; matrix products, arithmetic and copies ran while one was open for 0% -> 0% of each run, Pallas kernels for 8% -> 8%
where the time goes in v3:
time: 32.8 us; the launch traced here: 32.5 us
  waiting for transfers between devices  15 us (46%)
  starting transfers between devices  9.05 us (28%)
  Pallas kernels  7.31 us (22%)
  local copies, waits for them, and re-layouts  1.07 us (3%)
    ppermute x1, waiting for transfers between devices, shards(): mid.append(lax.ppermute(choose(2, mine[s], far[s]), 'chan', swap2))  5.48 us
    ppermute x1, waiting for transfers between devices, shards(): lax.ppermute(spectra[s], 'win', [(i, (i + s) % parts) for i in range(part...  5.03 us
    ppermute x2, waiting for transfers between devices, shards(): far = [lax.ppermute(own, 'chan', up) for own in mine]  4.15 us
    pallas_call x1, Pallas kernels, whitened_spectra(): pl.pallas_call(functools.partial(spectra_kernel, parts), in_specs=[VMEM]...  3.34 us
    pallas_call x4, Pallas kernels, cross_call(): pl.pallas_call(functools.partial(cross_kernel, layout, jobs), in_specs=[V...  3.09 us
    ppermute x1, starting transfers between devices, shards(): lax.ppermute(spectra[s], 'win', [(i, (i + s) % parts) for i in range(part...  3.03 us
    ppermute x2, starting transfers between devices, shards(): far = [lax.ppermute(own, 'chan', up) for own in mine]  2.56 us
    ppermute x1, starting transfers between devices, shards(): mid.append(lax.ppermute(choose(2, mine[s], far[s]), 'chan', swap2))  1.56 us
  transfers between devices with their start and end apart: 9, of which 7 were waited for; matrix products, arithmetic and copies ran while one was open for 0% of the time, Pallas kernels for 8%

profile of v3, /device:TPU:0, one launch (start us, length us, event | category | flops | bytes accessed | tf_op | source)
XLA Modules:
  0.0 32.5 jit_solution(5062208698480888555)
XLA Ops:
  0.0 0.0 copy-start
  0.0 0.2 tables.1
  0.2 1.1 %copy-done = f32[4,8,8192]{2,1,0:T(8,128)S(1)} copy-done((f32[4,8,8192]{2,1,0:T(8,128)S(1)}, f32[4,8,8192]{2,1,0:T(8,128)}, u32[]{:S(2)}) %copy-start) | copy-done | bytes 1048600
  1.2 3.3 %spectra.1 = (bf16[4,8,32,128]{3,2,1,0:T(8,128)(2,1)S(1)}, bf16[4,8,32,128]{3,2,1,0:T(8,128)(2,1)S(1)}) custom-call(f32[4,64,8,128]{3,2,1,0:T(8,128)S(1)} %bitcast.8, f32[2,64,128]{2,1,0:T(8,128)S(1)} %get-tuple-element.19.tw_ref, bf16[128,1536]{1,0:T(8,128)(2,1)S(1)} %get-tuple-element.20.l2_ref), custom_call_target="tpu_custom_call" | custom-call | flops 4400000000 | tf_op jit(solution)/shard_map/spectra/pallas_call | solution.py:206
  4.6 3.0 %collective-permute-start.1 = (bf16[4,8,32,128]{3,2,1,0:T(8,128)(2,1)S(1)}, bf16[4,8,32,128]{3,2,1,0:T(8,128)(2,1)S(1)}, u32[]{:S(2)}, u32[]{:S(2)}) collective-permute-start(bf16[4,8,32,128]{3,2,1,0:T(8,128)(2,1)S(1)} %get-tuple-element.23), channel_id=1, source_target_pairs={{0,1},{1,0},{2,3},{3,2},{4,5},{5,4},{6,7},{7,6},{8,9},{9,8},{10,11... | collective-permute-start | bytes 786440 | tf_op jit(solution)/shard_map/ppermute | solution.py:361
  7.6 1.3 %collective-permute-start = (bf16[4,8,32,128]{3,2,1,0:T(8,128)(2,1)S(1)}, bf16[4,8,32,128]{3,2,1,0:T(8,128)(2,1)S(1)}, u32[]{:S(2)}, u32[]{:S(2)}) collective-permute-start(bf16[4,8,32,128]{3,2,1,0:T(8,128)(2,1)S(1)} %get-tuple-element.21.refs_1_.own_ref), channel_id=1, source_target_pairs={{8,0},{10,2},{12,4},{14,6},{16,8},{18,10},{20,12},{22,14},{24,16},... | collective-permute-start | bytes 786440 | tf_op jit(solution)/shard_map/ppermute | solution.py:362
  8.9 5.0 %collective-permute-done.1.refs_2_.own_ref = bf16[4,8,32,128]{3,2,1,0:T(8,128)(2,1)S(1)} collective-permute-done((bf16[4,8,32,128]{3,2,1,0:T(8,128)(2,1)S(1)}, bf16[4,8,32,128]{3,2,1,0:T(8,128)(2,1)S(1)}, u32[]{:S(2)}, u32[]{:S(2)}) %collective-permute-start.1) | collective-permute-done | bytes 262176 | tf_op jit(solution)/shard_map/ppermute | solution.py:361
  13.9 1.3 %collective-permute-start.3 = (bf16[4,8,32,128]{3,2,1,0:T(8,128)(2,1)S(1)}, bf16[4,8,32,128]{3,2,1,0:T(8,128)(2,1)S(1)}, u32[]{:S(2)}, u32[]{:S(2)}) collective-permute-start(bf16[4,8,32,128]{3,2,1,0:T(8,128)(2,1)S(1)} %collective-permute-done.1.refs_2_.own_ref), channel_id=1, source_target_pairs={{8,0},{10,2},{12,4},{14,6},{16,8},{18,10},{20,12},{22,14},{24,16},... | collective-permute-start | bytes 786440 | tf_op jit(solution)/shard_map/ppermute | solution.py:362
  15.2 2.1 %collective-permute-done.refs_3_.far_ref = bf16[4,8,32,128]{3,2,1,0:T(8,128)(2,1)S(1)} collective-permute-done((bf16[4,8,32,128]{3,2,1,0:T(8,128)(2,1)S(1)}, bf16[4,8,32,128]{3,2,1,0:T(8,128)(2,1)S(1)}, u32[]{:S(2)}, u32[]{:S(2)}) %collective-permute-start) | collective-permute-done | bytes 262176 | tf_op jit(solution)/shard_map/ppermute | solution.py:362
  17.3 0.0 copy-start.1
  17.3 1.6 %collective-permute-start.4 = (bf16[4,8,32,128]{3,2,1,0:T(8,128)(2,1)S(1)}, bf16[4,8,32,128]{3,2,1,0:T(8,128)(2,1)S(1)}, u32[]{:S(2)}, u32[]{:S(2)}) collective-permute-start(bf16[4,8,32,128]{3,2,1,0:T(8,128)(2,1)S(1)} %choose.3), channel_id=1, source_target_pairs={{0,4},{2,6},{4,0},{6,2},{8,12},{10,14},{12,8},{14,10},{16,20},{18,... | collective-permute-start | bytes 786440 | tf_op jit(solution)/shard_map/ppermute | solution.py:375
  18.9 0.1 collective-permute-start.5
  19.0 1.3 %collective-permute-start.2 = (bf16[4,8,32,128]{3,2,1,0:T(8,128)(2,1)S(1)}, bf16[4,8,32,128]{3,2,1,0:T(8,128)(2,1)S(1)}, u32[]{:S(2)}, u32[]{:S(2)}) collective-permute-start(bf16[4,8,32,128]{3,2,1,0:T(8,128)(2,1)S(1)} %collective-permute-done.1.refs_2_.own_ref), channel_id=1, source_target_pairs={{4,0},{6,2},{8,4},{10,6},{12,8},{14,10},{16,12},{18,14},{20,16},{2... | collective-permute-start | bytes 786440 | tf_op jit(solution)/shard_map/ppermute | solution.py:377
  20.3 0.0 copy-done.1
  20.3 0.7 %gains.1.refs_0_ = f32[64,128]{1,0:T(8,128)S(1)} custom-call(s32[64]{0:T(128)S(1)} %copy-done.1), custom_call_target="tpu_custom_call" | custom-call | flops 550000000 | tf_op jit(solution)/shard_map/gains/pallas_call | solution.py:152
  20.9 0.2 cross_far.1.refs_6_
  21.2 2.1 %collective-permute-done.3.refs_3_.far_ref = bf16[4,8,32,128]{3,2,1,0:T(8,128)(2,1)S(1)} collective-permute-done((bf16[4,8,32,128]{3,2,1,0:T(8,128)(2,1)S(1)}, bf16[4,8,32,128]{3,2,1,0:T(8,128)(2,1)S(1)}, u32[]{:S(2)}, u32[]{:S(2)}) %collective-permute-start.3) | collective-permute-done | bytes 262176 | tf_op jit(solution)/shard_map/ppermute | solution.py:362
  23.3 0.1 collective-permute-start.7
  23.4 5.5 %collective-permute-done.4.refs_4_ = bf16[4,8,32,128]{3,2,1,0:T(8,128)(2,1)S(1)} collective-permute-done((bf16[4,8,32,128]{3,2,1,0:T(8,128)(2,1)S(1)}, bf16[4,8,32,128]{3,2,1,0:T(8,128)(2,1)S(1)}, u32[]{:S(2)}, u32[]{:S(2)}) %collective-permute-start.4) | collective-permute-done | bytes 262176 | tf_op jit(solution)/shard_map/ppermute | solution.py:375
  28.9 0.0 collective-permute-start.8
  28.9 0.0 collective-permute-done.5.refs_5_
  28.9 0.8 %cross_most.1 = (f32[4,4,32,128]{3,2,1,0:T(8,128)S(1)}, f32[4,4,32,128]{3,2,1,0:T(8,128)S(1)}, f32[4,4,32,128]{3,2,1,0:T(8,128)S(1)}) custom-call(f32[64,128]{1,0:T(8,128)S(1)} %gains.1.refs_0_, bf16[4,8,32,128]{3,2,1,0:T(8,128)(2,1)S(1)} %get-tuple-element.21.refs_1_.own_ref, bf16[4,8,32,128]{3,2,1,0:T(8,128)(2,1)S(1)} %collective-permute-done.1.refs_2_.own_ref, ...), custom_call_target="tpu_custom_call" | custom-call | flops 1980000000 | tf_op jit(solution)/shard_map/cross_most/pallas_call | solution.py:312
  29.7 0.1 collective-permute-done.2.refs_3_
  29.8 0.5 %collective-permute-start.6 = (bf16[4,8,32,128]{3,2,1,0:T(8,128)(2,1)S(1)}, bf16[4,8,32,128]{3,2,1,0:T(8,128)(2,1)S(1)}, u32[]{:S(2)}, u32[]{:S(2)}) collective-permute-start(bf16[4,8,32,128]{3,2,1,0:T(8,128)(2,1)S(1)} %collective-permute-done.2.refs_3_), channel_id=1, source_target_pairs={{0,2},{2,0},{4,6},{6,4},{8,10},{10,8},{12,14},{14,12},{16,18},{18,... | collective-permute-start | bytes 786440 | tf_op jit(solution)/shard_map/ppermute | solution.py:392
  30.3 0.0 collective-permute-done.7.refs_4_
  30.3 0.1 collective-permute-done.8.refs_5_
  30.4 0.9 %cross_next.1 = (f32[4,4,32,128]{3,2,1,0:T(8,128)S(1)}, f32[4,4,32,128]{3,2,1,0:T(8,128)S(1)}, f32[4,4,32,128]{3,2,1,0:T(8,128)S(1)}) custom-call(f32[64,128]{1,0:T(8,128)S(1)} %gains.1.refs_0_, bf16[4,8,32,128]{3,2,1,0:T(8,128)(2,1)S(1)} %get-tuple-element.21.refs_1_.own_ref, bf16[4,8,32,128]{3,2,1,0:T(8,128)(2,1)S(1)} %collective-permute-done.1.refs_2_.own_ref, ...), custom_call_target="tpu_custom_call" | custom-call | flops 1980000000 | tf_op jit(solution)/shard_map/cross_next/pallas_call | solution.py:312
  31.4 0.1 collective-permute-done.6.refs_3_
  31.5 1.1 %cross_last.1 = f32[4,4,4,32,128]{4,3,2,1,0:T(8,128)} custom-call(f32[64,128]{1,0:T(8,128)S(1)} %gains.1.refs_0_, bf16[4,8,32,128]{3,2,1,0:T(8,128)(2,1)S(1)} %get-tuple-element.21.refs_1_.own_ref, bf16[4,8,32,128]{3,2,1,0:T(8,128)(2,1)S(1)} %collective-permute-done.1.refs_2_.own_ref, bf16[4,8,32,128]{3,2,1,0:T(8,128)(2,1)S(1)} %collective-permute-done.6.refs_3_, ...), custom_call_target="tpu_custom_call" | custom-call | flops 660000000 | tf_op jit(solution)/shard_map/cross_last/pallas_call | solution.py:312
  (3 shorter events, 0.1 us)
Async XLA Ops:
  0.0 1.2 %copy-start = (f32[4,8,8192]{2,1,0:T(8,128)S(1)}, f32[4,8,8192]{2,1,0:T(8,128)}, u32[]{:S(2)}) copy-start(f32[4,8,8192]{2,1,0:T(8,128)} %param.2) | copy-start | bytes 3145732
  4.6 9.3 %collective-permute-start.1 = (bf16[4,8,32,128]{3,2,1,0:T(8,128)(2,1)S(1)}, bf16[4,8,32,128]{3,2,1,0:T(8,128)(2,1)S(1)}, u32[]{:S(2)}, u32[]{:S(2)}) collective-permute-start(bf16[4,8,32,128]{3,2,1,0:T(8,128)(2,1)S(1)} %get-tuple-element.23), channel_id=1, source_target_pairs={{0,1},{1,0},{2,3},{3,2},{4,5},{5,4},{6,7},{7,6},{8,9},{9,8},{10,11... | collective-permute-start | bytes 786440 | tf_op jit(solution)/shard_map/ppermute | solution.py:361
  7.6 9.7 %collective-permute-start = (bf16[4,8,32,128]{3,2,1,0:T(8,128)(2,1)S(1)}, bf16[4,8,32,128]{3,2,1,0:T(8,128)(2,1)S(1)}, u32[]{:S(2)}, u32[]{:S(2)}) collective-permute-start(bf16[4,8,32,128]{3,2,1,0:T(8,128)(2,1)S(1)} %get-tuple-element.21.refs_1_.own_ref), channel_id=1, source_target_pairs={{8,0},{10,2},{12,4},{14,6},{16,8},{18,10},{20,12},{22,14},{24,16},... | collective-permute-start | bytes 786440 | tf_op jit(solution)/shard_map/ppermute | solution.py:362
  13.9 9.4 %collective-permute-start.3 = (bf16[4,8,32,128]{3,2,1,0:T(8,128)(2,1)S(1)}, bf16[4,8,32,128]{3,2,1,0:T(8,128)(2,1)S(1)}, u32[]{:S(2)}, u32[]{:S(2)}) collective-permute-start(bf16[4,8,32,128]{3,2,1,0:T(8,128)(2,1)S(1)} %collective-permute-done.1.refs_2_.own_ref), channel_id=1, source_target_pairs={{8,0},{10,2},{12,4},{14,6},{16,8},{18,10},{20,12},{22,14},{24,16},... | collective-permute-start | bytes 786440 | tf_op jit(solution)/shard_map/ppermute | solution.py:362
  17.3 3.0 %copy-start.1 = (s32[64]{0:T(128)S(1)}, s32[64]{0:T(128)}, u32[]{:S(2)}) copy-start(s32[64]{0:T(128)} %pos_ref) | copy-start | bytes 772
  17.3 11.6 %collective-permute-start.4 = (bf16[4,8,32,128]{3,2,1,0:T(8,128)(2,1)S(1)}, bf16[4,8,32,128]{3,2,1,0:T(8,128)(2,1)S(1)}, u32[]{:S(2)}, u32[]{:S(2)}) collective-permute-start(bf16[4,8,32,128]{3,2,1,0:T(8,128)(2,1)S(1)} %choose.3), channel_id=1, source_target_pairs={{0,4},{2,6},{4,0},{6,2},{8,12},{10,14},{12,8},{14,10},{16,20},{18,... | collective-permute-start | bytes 786440 | tf_op jit(solution)/shard_map/ppermute | solution.py:375
  18.9 10.0 %collective-permute-start.5 = (bf16[4,8,32,128]{3,2,1,0:T(8,128)(2,1)S(1)}, bf16[4,8,32,128]{3,2,1,0:T(8,128)(2,1)S(1)}, u32[]{:S(2)}, u32[]{:S(2)}) collective-permute-start(bf16[4,8,32,128]{3,2,1,0:T(8,128)(2,1)S(1)} %choose.4), channel_id=1, source_target_pairs={{0,2},{2,0},{4,6},{6,4},{8,10},{10,8},{12,14},{14,12},{16,18},{18,... | collective-permute-start | bytes 786440 | tf_op jit(solution)/shard_map/ppermute | solution.py:378
  19.0 10.9 %collective-permute-start.2 = (bf16[4,8,32,128]{3,2,1,0:T(8,128)(2,1)S(1)}, bf16[4,8,32,128]{3,2,1,0:T(8,128)(2,1)S(1)}, u32[]{:S(2)}, u32[]{:S(2)}) collective-permute-start(bf16[4,8,32,128]{3,2,1,0:T(8,128)(2,1)S(1)} %collective-permute-done.1.refs_2_.own_ref), channel_id=1, source_target_pairs={{4,0},{6,2},{8,4},{10,6},{12,8},{14,10},{16,12},{18,14},{20,16},{2... | collective-permute-start | bytes 786440 | tf_op jit(solution)/shard_map/ppermute | solution.py:377
  23.3 7.0 %collective-permute-start.7 = (bf16[4,8,32,128]{3,2,1,0:T(8,128)(2,1)S(1)}, bf16[4,8,32,128]{3,2,1,0:T(8,128)(2,1)S(1)}, u32[]{:S(2)}, u32[]{:S(2)}) collective-permute-start(bf16[4,8,32,128]{3,2,1,0:T(8,128)(2,1)S(1)} %choose.5), channel_id=1, source_target_pairs={{0,2},{2,0},{4,6},{6,4},{8,10},{10,8},{12,14},{14,12},{16,18},{18,... | collective-permute-start | bytes 786440 | tf_op jit(solution)/shard_map/ppermute | solution.py:378
  28.9 1.5 %collective-permute-start.8 = (bf16[4,8,32,128]{3,2,1,0:T(8,128)(2,1)S(1)}, bf16[4,8,32,128]{3,2,1,0:T(8,128)(2,1)S(1)}, u32[]{:S(2)}, u32[]{:S(2)}) collective-permute-start(bf16[4,8,32,128]{3,2,1,0:T(8,128)(2,1)S(1)} %collective-permute-done.4.refs_4_), channel_id=1, source_target_pairs={{0,2},{2,0},{4,6},{6,4},{8,10},{10,8},{12,14},{14,12},{16,18},{18,... | collective-permute-start | bytes 786440 | tf_op jit(solution)/shard_map/ppermute | solution.py:380
  29.8 1.6 %collective-permute-start.6 = (bf16[4,8,32,128]{3,2,1,0:T(8,128)(2,1)S(1)}, bf16[4,8,32,128]{3,2,1,0:T(8,128)(2,1)S(1)}, u32[]{:S(2)}, u32[]{:S(2)}) collective-permute-start(bf16[4,8,32,128]{3,2,1,0:T(8,128)(2,1)S(1)} %collective-permute-done.2.refs_3_), channel_id=1, source_target_pairs={{0,2},{2,0},{4,6},{6,4},{8,10},{10,8},{12,14},{14,12},{16,18},{18,... | collective-permute-start | bytes 786440 | tf_op jit(solution)/shard_map/ppermute | solution.py:392

commit v4 on v2

--- a/solution.py
+++ b/solution.py
@@ -54,61 +54,51 @@
     return out
 
 
-def spectra_channel(parts, chan, x, tw_ref, l2_ref, t_ref, outs):
+def spectra_channel(parts, chan, x, tables, t_ref, outs):
+    tw_ref, main_ref, side_ref, bands_ref, pick_ref = tables
     first = len(x)
     wins = x[0].shape[0]
     bands = BINS // BAND // parts
     terms = real_dft(x)
+    rows = []
     for k in range(first):
         re, im = terms[min(k, first - k)]
-        rows = pl.ds(k * wins, wins)
         cos, sin = tw_ref[0, pl.ds(k, 1), :], tw_ref[1, pl.ds(k, 1), :]
         if im is None:
-            t_ref[chan, 0, rows, :] = re * cos
-            t_ref[chan, 1, rows, :] = -(re * sin)
+            row = [re * cos, -(re * sin)]
         elif 2 * k <= first:
-            t_ref[chan, 0, rows, :] = re * cos + im * sin
-            t_ref[chan, 1, rows, :] = im * cos - re * sin
+            row = [re * cos + im * sin, im * cos - re * sin]
         else:
-            t_ref[chan, 0, rows, :] = re * cos - im * sin
-            t_ref[chan, 1, rows, :] = -(im * cos + re * sin)
-    rhs = []
-    for win in range(wins):
-        at = pl.ds(win, first, stride=wins)
-        row = jnp.concatenate([t_ref[chan, 0, at, :], t_ref[chan, 1, at, :]], axis=1)
-        hi, mid, lo = split3(row)
-        rhs.append(jnp.concatenate([hi, mid, lo, hi, mid, hi], axis=1))
-    spec = lax.dot_general(
-        l2_ref[...],
-        jnp.concatenate(rhs, axis=0),
-        (((1,), (1,)), ((), ())),
+            row = [re * cos - im * sin, -(im * cos + re * sin)]
+        rows.append(jnp.concatenate(row, axis=1))
+    hi, mid, lo = split3(jnp.concatenate(rows, axis=0))
+    main = jnp.dot(
+        jnp.concatenate([hi, mid], axis=1), main_ref[...], preferred_element_type=jnp.float32
+    )
+    side = jnp.dot(
+        jnp.concatenate([hi, lo], axis=1), side_ref[...], preferred_element_type=jnp.float32
+    )
+    spec = (main[:, :LANES] + main[:, LANES:] + side).reshape(first, wins, LANES)
+    total = jnp.dot(
+        jnp.concatenate(split3(jnp.sum(spec * spec, axis=0)), axis=1),
+        bands_ref[...],
         preferred_element_type=jnp.float32,
     )
+    scale = lax.rsqrt(total * (1.0 / BAND) + band_epsilon)
+    t_ref[chan] = (spec * scale).reshape(first * wins, LANES)
+    white = jnp.concatenate(
+        [t_ref[chan, pl.ds(win, first, stride=wins), :].astype(jnp.bfloat16) for win in range(wins)],
+        axis=0,
+    )
+    spread = lax.dot_general(
+        pick_ref[...], white, (((1,), (1,)), ((), ())), preferred_element_type=jnp.float32
+    )
     left = lax.broadcasted_iota(jnp.int32, (bands, LANES), 1) < first
-    pairs = wins // 2
-    tiles = [
-        spec[:, i * LANES : (i + 1) * LANES].reshape(parts, 4, bands, LANES) for i in range(pairs)
-    ]
-    powers = []
-    for tile in tiles:
-        square = tile * tile
-        power = square[:, 0] + square[:, 1] + square[:, 2] + square[:, 3]
-        powers.append(power.reshape(parts * bands, LANES))
-    row = lax.rem(lax.broadcasted_iota(jnp.int32, (3 * LANES, LANES), 0), LANES)
-    lane = lax.broadcasted_iota(jnp.int32, (3 * LANES, LANES), 1)
-    ones = ((row < first) == (lane < first)).astype(jnp.bfloat16)
-    total = jnp.dot(
-        jnp.concatenate(split3(jnp.concatenate(powers, axis=0)), axis=1),
-        ones,
-        preferred_element_type=jnp.float32,
-    )
-    scales = lax.rsqrt(total * (1.0 / BAND) + band_epsilon).reshape(pairs, parts, bands, LANES)
-    for pair in range(pairs):
+    for pair in range(wins // 2):
+        tile = spread[:, pair * LANES : (pair + 1) * LANES].reshape(parts, 2, 2, bands, LANES)
         for s in range(parts):
-            scale = scales[pair, s]
             for imag in range(2):
-                even = tiles[pair][s, 2 * imag] * scale
-                odd = tiles[pair][s, 2 * imag + 1] * scale
+                even, odd = tile[s, imag, 0], tile[s, imag, 1]
                 one = jnp.where(left, even, pltpu.roll(odd, first, 1)).astype(jnp.bfloat16)
                 two = jnp.where(left, pltpu.roll(even, first, 1), odd).astype(jnp.bfloat16)
                 at = pl.ds(imag * bands, bands)
@@ -160,31 +150,38 @@
     )(positions)
 
 
-def tables_kernel(parts, samples, tw_ref, l2_ref):
+def tables_kernel(parts, samples, tw_ref, main_ref, side_ref, bands_ref, pick_ref):
     first = samples // LANES
     bands = BINS // BAND // parts
     me = lax.axis_index("win")
     k1 = lax.broadcasted_iota(jnp.int32, (first, LANES), 0)
     q = lax.broadcasted_iota(jnp.int32, (first, LANES), 1)
     tw_ref[0], tw_ref[1] = turn_table(k1 * q, samples)
-    band = lax.broadcasted_iota(jnp.int32, (bands, LANES), 0)
-    q = lax.broadcasted_iota(jnp.int32, (bands, LANES), 1)
-    for s in range(parts):
-        part = lax.rem(me + s, parts)
-        tables = [turn_table((2 * (part * bands + band) + odd) * q, LANES) for odd in range(2)]
-        rows = [jnp.concatenate([cos, sin], axis=1) for cos, sin in tables]
-        rows += [jnp.concatenate([-sin, cos], axis=1) for cos, sin in tables]
-        hi, mid, lo = split3(jnp.concatenate(rows, axis=0))
-        table = jnp.concatenate([hi, hi, hi, mid, mid, lo], axis=1)
-        l2_ref[pl.ds(s * 4 * bands, 4 * bands), :] = table
-
-
-def spectra_kernel(parts, x_ref, tw_ref, l2_ref, *refs):
-    outs, t_ref = refs[:-1], refs[-1]
+    row = lax.broadcasted_iota(jnp.int32, (LANES, LANES), 0)
+    lane = lax.broadcasted_iota(jnp.int32, (LANES, LANES), 1)
+    real = lane < first
+    m = lax.rem(lane, first)
+    cos, sin = turn_table(row * m, LANES)
+    table = jnp.concatenate([jnp.where(real, cos, -sin), jnp.where(real, sin, cos)], axis=0)
+    hi, mid, lo = split3(table)
+    wide = jnp.concatenate([hi, mid], axis=1)
+    main_ref[...] = jnp.concatenate([wide, wide], axis=0)
+    side_ref[...] = jnp.concatenate([lo, hi], axis=0)
+    same = lax.div(lax.rem(row, first), 2) == lax.div(m, 2)
+    bands_ref[...] = jnp.concatenate([same.astype(jnp.float32)] * 3, axis=0).astype(jnp.bfloat16)
+    part = lax.rem(me + lax.div(row, 4 * bands), parts)
+    imag = lax.rem(lax.div(row, 2 * bands), 2)
+    odd = lax.rem(lax.div(row, bands), 2)
+    source = imag * first + 2 * (part * bands + lax.rem(row, bands)) + odd
+    pick_ref[...] = (lane == source).astype(jnp.float32).astype(jnp.bfloat16)
+
+
+def spectra_kernel(parts, x_ref, *refs):
+    tables, outs, t_ref = refs[:5], refs[5:-1], refs[-1]
     chans, first = x_ref.shape[:2]
     for chan in range(chans):
         x = [x_ref[chan, p] for p in range(first)]
-        spectra_channel(parts, chan, x, tw_ref, l2_ref, t_ref, outs)
+        spectra_channel(parts, chan, x, tables, t_ref, outs)
 
 
 def whitened_spectra(records, parts):
@@ -194,10 +191,13 @@
     x = records.reshape(chans, wins, first, LANES).transpose(0, 2, 1, 3)
     tables = pl.pallas_call(
         functools.partial(tables_kernel, parts, samples),
-        out_specs=[VMEM] * 2,
+        out_specs=[VMEM] * 5,
         out_shape=[
             jax.ShapeDtypeStruct((2, first, LANES), jnp.float32),
-            jax.ShapeDtypeStruct((2 * rows * parts, 12 * LANES), jnp.bfloat16),
+            jax.ShapeDtypeStruct((4 * LANES, 2 * LANES), jnp.bfloat16),
+            jax.ShapeDtypeStruct((4 * LANES, LANES), jnp.bfloat16),
+            jax.ShapeDtypeStruct((3 * LANES, LANES), jnp.bfloat16),
+            jax.ShapeDtypeStruct((LANES, LANES), jnp.bfloat16),
         ],
         compiler_params=PARAMS,
         cost_estimate=cost(1),
@@ -205,10 +205,10 @@
     )()
     return pl.pallas_call(
         functools.partial(spectra_kernel, parts),
-        in_specs=[VMEM] * 3,
+        in_specs=[VMEM] * 6,
         out_specs=[VMEM] * parts,
         out_shape=[jax.ShapeDtypeStruct((chans, wins, rows, LANES), jnp.bfloat16)] * parts,
-        scratch_shapes=[pltpu.VMEM((chans, 2, first * wins, LANES), jnp.float32)],
+        scratch_shapes=[pltpu.VMEM((chans, first * wins, LANES), jnp.float32)],
         compiler_params=PARAMS,
         cost_estimate=cost(4),
         name="spectra",

time: 32.8 us -> 32.4 us (0.988)
  transfers between devices with their start and end apart: 9 -> 9, of which waited for: 5 -> 5; matrix products, arithmetic and copies ran while one was open for 0% -> 0% of each run, Pallas kernels for 8% -> 9%
where the time goes in v4:
time: 32.4 us; the launch traced here: 32.2 us
  waiting for transfers between devices  14.8 us (46%)
  starting transfers between devices  9.25 us (29%)
  Pallas kernels  7.15 us (22%)
  local copies, waits for them, and re-layouts  0.93 us (3%)
    ppermute x2, waiting for transfers between devices, shards(): far = [lax.ppermute(own, 'chan', up) for own in mine]  5.43 us
    ppermute x1, waiting for transfers between devices, shards(): lax.ppermute(spectra[s], 'win', [(i, (i + s) % parts) for i in range(part...  5.02 us
    ppermute x2, waiting for transfers between devices, shards(): mid.append(lax.ppermute(choose(2, mine[s], far[s]), 'chan', swap2))  3.75 us
    pallas_call x4, Pallas kernels, cross_call(): pl.pallas_call(functools.partial(cross_kernel, layout, jobs), in_specs=[V...  3.09 us
    ppermute x1, starting transfers between devices, shards(): lax.ppermute(spectra[s], 'win', [(i, (i + s) % parts) for i in range(part...  3.03 us
    ppermute x2, starting transfers between devices, shards(): mid.append(lax.ppermute(choose(2, mine[s], far[s]), 'chan', swap2))  3.02 us
    pallas_call x1, Pallas kernels, whitened_spectra(): pl.pallas_call(functools.partial(spectra_kernel, parts), in_specs=[VMEM]...  3.01 us
    ppermute x2, starting transfers between devices, shards(): far = [lax.ppermute(own, 'chan', up) for own in mine]  2.56 us
  transfers between devices with their start and end apart: 9, of which 5 were waited for; matrix products, arithmetic and copies ran while one was open for 0% of the time, Pallas kernels for 9%

profile of v4, /device:TPU:0, one launch (start us, length us, event | category | flops | bytes accessed | tf_op | source)
XLA Modules:
  0.0 32.2 jit_solution(1406021205019181721)
XLA Ops:
  0.0 0.0 copy-start
  0.0 0.3 tables.1
  0.3 0.9 %copy-done = f32[4,8,8192]{2,1,0:T(8,128)S(1)} copy-done((f32[4,8,8192]{2,1,0:T(8,128)S(1)}, f32[4,8,8192]{2,1,0:T(8,128)}, u32[]{:S(2)}) %copy-start) | copy-done | bytes 1048600
  1.2 3.0 %spectra.1 = (bf16[4,8,32,128]{3,2,1,0:T(8,128)(2,1)S(1)}, bf16[4,8,32,128]{3,2,1,0:T(8,128)(2,1)S(1)}) custom-call(f32[4,64,8,128]{3,2,1,0:T(8,128)S(1)} %bitcast.8, f32[2,64,128]{2,1,0:T(8,128)S(1)} %get-tuple-element.22.refs_0_, bf16[512,256]{1,0:T(8,128)(2,1)S(1)} %get-tuple-element.23.refs_1_, bf16[512,128]{1,0:T(8,128)(2,1)S(1)} %get-tuple-element.24.refs_2_, ...), custom_call_target="tpu_custom_call" | custom-call | flops 4400000000 | tf_op jit(solution)/shard_map/spectra/pallas_call | solution.py:206
  4.2 3.0 %collective-permute-start.1 = (bf16[4,8,32,128]{3,2,1,0:T(8,128)(2,1)S(1)}, bf16[4,8,32,128]{3,2,1,0:T(8,128)(2,1)S(1)}, u32[]{:S(2)}, u32[]{:S(2)}) collective-permute-start(bf16[4,8,32,128]{3,2,1,0:T(8,128)(2,1)S(1)} %get-tuple-element.29), channel_id=1, source_target_pairs={{0,1},{1,0},{2,3},{3,2},{4,5},{5,4},{6,7},{7,6},{8,9},{9,8},{10,11... | collective-permute-start | bytes 786440 | tf_op jit(solution)/shard_map/ppermute | solution.py:361
  7.3 1.3 %collective-permute-start = (bf16[4,8,32,128]{3,2,1,0:T(8,128)(2,1)S(1)}, bf16[4,8,32,128]{3,2,1,0:T(8,128)(2,1)S(1)}, u32[]{:S(2)}, u32[]{:S(2)}) collective-permute-start(bf16[4,8,32,128]{3,2,1,0:T(8,128)(2,1)S(1)} %get-tuple-element.27.refs_1_.own_ref), channel_id=1, source_target_pairs={{8,0},{10,2},{12,4},{14,6},{16,8},{18,10},{20,12},{22,14},{24,16},... | collective-permute-start | bytes 786440 | tf_op jit(solution)/shard_map/ppermute | solution.py:362
  8.6 5.0 %collective-permute-done.1.refs_2_.own_ref = bf16[4,8,32,128]{3,2,1,0:T(8,128)(2,1)S(1)} collective-permute-done((bf16[4,8,32,128]{3,2,1,0:T(8,128)(2,1)S(1)}, bf16[4,8,32,128]{3,2,1,0:T(8,128)(2,1)S(1)}, u32[]{:S(2)}, u32[]{:S(2)}) %collective-permute-start.1) | collective-permute-done | bytes 262176 | tf_op jit(solution)/shard_map/ppermute | solution.py:361
  13.6 1.3 %collective-permute-start.2 = (bf16[4,8,32,128]{3,2,1,0:T(8,128)(2,1)S(1)}, bf16[4,8,32,128]{3,2,1,0:T(8,128)(2,1)S(1)}, u32[]{:S(2)}, u32[]{:S(2)}) collective-permute-start(bf16[4,8,32,128]{3,2,1,0:T(8,128)(2,1)S(1)} %collective-permute-done.1.refs_2_.own_ref), channel_id=1, source_target_pairs={{8,0},{10,2},{12,4},{14,6},{16,8},{18,10},{20,12},{22,14},{24,16},... | collective-permute-start | bytes 786440 | tf_op jit(solution)/shard_map/ppermute | solution.py:362
  14.9 2.1 %collective-permute-done.refs_3_.far_ref = bf16[4,8,32,128]{3,2,1,0:T(8,128)(2,1)S(1)} collective-permute-done((bf16[4,8,32,128]{3,2,1,0:T(8,128)(2,1)S(1)}, bf16[4,8,32,128]{3,2,1,0:T(8,128)(2,1)S(1)}, u32[]{:S(2)}, u32[]{:S(2)}) %collective-permute-start) | collective-permute-done | bytes 262176 | tf_op jit(solution)/shard_map/ppermute | solution.py:362
  17.0 0.0 copy-start.1
  17.0 1.6 %collective-permute-start.4 = (bf16[4,8,32,128]{3,2,1,0:T(8,128)(2,1)S(1)}, bf16[4,8,32,128]{3,2,1,0:T(8,128)(2,1)S(1)}, u32[]{:S(2)}, u32[]{:S(2)}) collective-permute-start(bf16[4,8,32,128]{3,2,1,0:T(8,128)(2,1)S(1)} %choose.5), channel_id=1, source_target_pairs={{0,4},{2,6},{4,0},{6,2},{8,12},{10,14},{12,8},{14,10},{16,20},{18,... | collective-permute-start | bytes 786440 | tf_op jit(solution)/shard_map/ppermute | solution.py:374
  18.6 0.1 collective-permute-start.5
  18.6 0.0 copy-done.1
  18.6 0.7 %gains.1.refs_0_ = f32[64,128]{1,0:T(8,128)S(1)} custom-call(s32[64]{0:T(128)S(1)} %copy-done.1), custom_call_target="tpu_custom_call" | custom-call | flops 550000000 | tf_op jit(solution)/shard_map/gains/pallas_call | solution.py:142
  19.3 0.2 cross_far.1.refs_6_
  19.6 3.4 %collective-permute-done.2.far_ref.refs_3_ = bf16[4,8,32,128]{3,2,1,0:T(8,128)(2,1)S(1)} collective-permute-done((bf16[4,8,32,128]{3,2,1,0:T(8,128)(2,1)S(1)}, bf16[4,8,32,128]{3,2,1,0:T(8,128)(2,1)S(1)}, u32[]{:S(2)}, u32[]{:S(2)}) %collective-permute-start.2) | collective-permute-done | bytes 262176 | tf_op jit(solution)/shard_map/ppermute | solution.py:362
  23.0 1.5 %collective-permute-start.3 = (bf16[4,8,32,128]{3,2,1,0:T(8,128)(2,1)S(1)}, bf16[4,8,32,128]{3,2,1,0:T(8,128)(2,1)S(1)}, u32[]{:S(2)}, u32[]{:S(2)}) collective-permute-start(bf16[4,8,32,128]{3,2,1,0:T(8,128)(2,1)S(1)} %choose.4), channel_id=1, source_target_pairs={{0,4},{2,6},{4,0},{6,2},{8,12},{10,14},{12,8},{14,10},{16,20},{18,... | collective-permute-start | bytes 786440 | tf_op jit(solution)/shard_map/ppermute | solution.py:374
  24.5 0.1 collective-permute-start.7
  24.5 0.0 collective-permute-done.4.refs_4_
  24.5 0.5 %collective-permute-start.8 = (bf16[4,8,32,128]{3,2,1,0:T(8,128)(2,1)S(1)}, bf16[4,8,32,128]{3,2,1,0:T(8,128)(2,1)S(1)}, u32[]{:S(2)}, u32[]{:S(2)}) collective-permute-start(bf16[4,8,32,128]{3,2,1,0:T(8,128)(2,1)S(1)} %collective-permute-done.4.refs_4_), channel_id=1, source_target_pairs={{0,2},{2,0},{4,6},{6,4},{8,10},{10,8},{12,14},{14,12},{16,18},{18,... | collective-permute-start | bytes 786440 | tf_op jit(solution)/shard_map/ppermute | solution.py:377
  25.0 0.0 collective-permute-done.5.refs_5_
  25.0 0.8 %cross_most.1 = (f32[4,4,32,128]{3,2,1,0:T(8,128)S(1)}, f32[4,4,32,128]{3,2,1,0:T(8,128)S(1)}, f32[4,4,32,128]{3,2,1,0:T(8,128)S(1)}) custom-call(f32[64,128]{1,0:T(8,128)S(1)} %gains.1.refs_0_, bf16[4,8,32,128]{3,2,1,0:T(8,128)(2,1)S(1)} %get-tuple-element.27.refs_1_.own_ref, bf16[4,8,32,128]{3,2,1,0:T(8,128)(2,1)S(1)} %collective-permute-done.1.refs_2_.own_ref, ...), custom_call_target="tpu_custom_call" | custom-call | flops 1980000000 | tf_op jit(solution)/shard_map/cross_most/pallas_call | solution.py:312
  25.9 3.7 %collective-permute-done.3.refs_3_ = bf16[4,8,32,128]{3,2,1,0:T(8,128)(2,1)S(1)} collective-permute-done((bf16[4,8,32,128]{3,2,1,0:T(8,128)(2,1)S(1)}, bf16[4,8,32,128]{3,2,1,0:T(8,128)(2,1)S(1)}, u32[]{:S(2)}, u32[]{:S(2)}) %collective-permute-start.3) | collective-permute-done | bytes 262176 | tf_op jit(solution)/shard_map/ppermute | solution.py:374
  29.6 0.0 collective-permute-start.6
  29.6 0.0 collective-permute-done.7.refs_4_
  29.6 0.0 collective-permute-done.8.refs_5_
  29.6 0.9 %cross_next.1 = (f32[4,4,32,128]{3,2,1,0:T(8,128)S(1)}, f32[4,4,32,128]{3,2,1,0:T(8,128)S(1)}, f32[4,4,32,128]{3,2,1,0:T(8,128)S(1)}) custom-call(f32[64,128]{1,0:T(8,128)S(1)} %gains.1.refs_0_, bf16[4,8,32,128]{3,2,1,0:T(8,128)(2,1)S(1)} %get-tuple-element.27.refs_1_.own_ref, bf16[4,8,32,128]{3,2,1,0:T(8,128)(2,1)S(1)} %collective-permute-done.1.refs_2_.own_ref, ...), custom_call_target="tpu_custom_call" | custom-call | flops 1980000000 | tf_op jit(solution)/shard_map/cross_next/pallas_call | solution.py:312
  30.6 0.6 %collective-permute-done.6.refs_3_ = bf16[4,8,32,128]{3,2,1,0:T(8,128)(2,1)S(1)} collective-permute-done((bf16[4,8,32,128]{3,2,1,0:T(8,128)(2,1)S(1)}, bf16[4,8,32,128]{3,2,1,0:T(8,128)(2,1)S(1)}, u32[]{:S(2)}, u32[]{:S(2)}) %collective-permute-start.6) | collective-permute-done | bytes 262176 | tf_op jit(solution)/shard_map/ppermute | solution.py:389
  31.2 1.1 %cross_last.1 = f32[4,4,4,32,128]{4,3,2,1,0:T(8,128)} custom-call(f32[64,128]{1,0:T(8,128)S(1)} %gains.1.refs_0_, bf16[4,8,32,128]{3,2,1,0:T(8,128)(2,1)S(1)} %get-tuple-element.27.refs_1_.own_ref, bf16[4,8,32,128]{3,2,1,0:T(8,128)(2,1)S(1)} %collective-permute-done.1.refs_2_.own_ref, bf16[4,8,32,128]{3,2,1,0:T(8,128)(2,1)S(1)} %collective-permute-done.6.refs_3_, ...), custom_call_target="tpu_custom_call" | custom-call | flops 660000000 | tf_op jit(solution)/shard_map/cross_last/pallas_call | solution.py:312
  (4 shorter events, 0.1 us)
Async XLA Ops:
  0.0 1.2 %copy-start = (f32[4,8,8192]{2,1,0:T(8,128)S(1)}, f32[4,8,8192]{2,1,0:T(8,128)}, u32[]{:S(2)}) copy-start(f32[4,8,8192]{2,1,0:T(8,128)} %param.2) | copy-start | bytes 3145732
  4.2 9.3 %collective-permute-start.1 = (bf16[4,8,32,128]{3,2,1,0:T(8,128)(2,1)S(1)}, bf16[4,8,32,128]{3,2,1,0:T(8,128)(2,1)S(1)}, u32[]{:S(2)}, u32[]{:S(2)}) collective-permute-start(bf16[4,8,32,128]{3,2,1,0:T(8,128)(2,1)S(1)} %get-tuple-element.29), channel_id=1, source_target_pairs={{0,1},{1,0},{2,3},{3,2},{4,5},{5,4},{6,7},{7,6},{8,9},{9,8},{10,11... | collective-permute-start | bytes 786440 | tf_op jit(solution)/shard_map/ppermute | solution.py:361
  7.3 9.6 %collective-permute-start = (bf16[4,8,32,128]{3,2,1,0:T(8,128)(2,1)S(1)}, bf16[4,8,32,128]{3,2,1,0:T(8,128)(2,1)S(1)}, u32[]{:S(2)}, u32[]{:S(2)}) collective-permute-start(bf16[4,8,32,128]{3,2,1,0:T(8,128)(2,1)S(1)} %get-tuple-element.27.refs_1_.own_ref), channel_id=1, source_target_pairs={{8,0},{10,2},{12,4},{14,6},{16,8},{18,10},{20,12},{22,14},{24,16},... | collective-permute-start | bytes 786440 | tf_op jit(solution)/shard_map/ppermute | solution.py:362
  13.6 9.4 %collective-permute-start.2 = (bf16[4,8,32,128]{3,2,1,0:T(8,128)(2,1)S(1)}, bf16[4,8,32,128]{3,2,1,0:T(8,128)(2,1)S(1)}, u32[]{:S(2)}, u32[]{:S(2)}) collective-permute-start(bf16[4,8,32,128]{3,2,1,0:T(8,128)(2,1)S(1)} %collective-permute-done.1.refs_2_.own_ref), channel_id=1, source_target_pairs={{8,0},{10,2},{12,4},{14,6},{16,8},{18,10},{20,12},{22,14},{24,16},... | collective-permute-start | bytes 786440 | tf_op jit(solution)/shard_map/ppermute | solution.py:362
  17.0 1.7 %copy-start.1 = (s32[64]{0:T(128)S(1)}, s32[64]{0:T(128)}, u32[]{:S(2)}) copy-start(s32[64]{0:T(128)} %pos_ref) | copy-start | bytes 772
  17.0 7.6 %collective-permute-start.4 = (bf16[4,8,32,128]{3,2,1,0:T(8,128)(2,1)S(1)}, bf16[4,8,32,128]{3,2,1,0:T(8,128)(2,1)S(1)}, u32[]{:S(2)}, u32[]{:S(2)}) collective-permute-start(bf16[4,8,32,128]{3,2,1,0:T(8,128)(2,1)S(1)} %choose.5), channel_id=1, source_target_pairs={{0,4},{2,6},{4,0},{6,2},{8,12},{10,14},{12,8},{14,10},{16,20},{18,... | collective-permute-start | bytes 786440 | tf_op jit(solution)/shard_map/ppermute | solution.py:374
  18.6 6.5 %collective-permute-start.5 = (bf16[4,8,32,128]{3,2,1,0:T(8,128)(2,1)S(1)}, bf16[4,8,32,128]{3,2,1,0:T(8,128)(2,1)S(1)}, u32[]{:S(2)}, u32[]{:S(2)}) collective-permute-start(bf16[4,8,32,128]{3,2,1,0:T(8,128)(2,1)S(1)} %choose.6), channel_id=1, source_target_pairs={{0,2},{2,0},{4,6},{6,4},{8,10},{10,8},{12,14},{14,12},{16,18},{18,... | collective-permute-start | bytes 786440 | tf_op jit(solution)/shard_map/ppermute | solution.py:375
  23.0 6.6 %collective-permute-start.3 = (bf16[4,8,32,128]{3,2,1,0:T(8,128)(2,1)S(1)}, bf16[4,8,32,128]{3,2,1,0:T(8,128)(2,1)S(1)}, u32[]{:S(2)}, u32[]{:S(2)}) collective-permute-start(bf16[4,8,32,128]{3,2,1,0:T(8,128)(2,1)S(1)} %choose.4), channel_id=1, source_target_pairs={{0,4},{2,6},{4,0},{6,2},{8,12},{10,14},{12,8},{14,10},{16,20},{18,... | collective-permute-start | bytes 786440 | tf_op jit(solution)/shard_map/ppermute | solution.py:374
  24.5 5.2 %collective-permute-start.7 = (bf16[4,8,32,128]{3,2,1,0:T(8,128)(2,1)S(1)}, bf16[4,8,32,128]{3,2,1,0:T(8,128)(2,1)S(1)}, u32[]{:S(2)}, u32[]{:S(2)}) collective-permute-start(bf16[4,8,32,128]{3,2,1,0:T(8,128)(2,1)S(1)} %choose.7), channel_id=1, source_target_pairs={{0,2},{2,0},{4,6},{6,4},{8,10},{10,8},{12,14},{14,12},{16,18},{18,... | collective-permute-start | bytes 786440 | tf_op jit(solution)/shard_map/ppermute | solution.py:375
  24.5 5.1 %collective-permute-start.8 = (bf16[4,8,32,128]{3,2,1,0:T(8,128)(2,1)S(1)}, bf16[4,8,32,128]{3,2,1,0:T(8,128)(2,1)S(1)}, u32[]{:S(2)}, u32[]{:S(2)}) collective-permute-start(bf16[4,8,32,128]{3,2,1,0:T(8,128)(2,1)S(1)} %collective-permute-done.4.refs_4_), channel_id=1, source_target_pairs={{0,2},{2,0},{4,6},{6,4},{8,10},{10,8},{12,14},{14,12},{16,18},{18,... | collective-permute-start | bytes 786440 | tf_op jit(solution)/shard_map/ppermute | solution.py:377
  29.6 1.5 %collective-permute-start.6 = (bf16[4,8,32,128]{3,2,1,0:T(8,128)(2,1)S(1)}, bf16[4,8,32,128]{3,2,1,0:T(8,128)(2,1)S(1)}, u32[]{:S(2)}, u32[]{:S(2)}) collective-permute-start(bf16[4,8,32,128]{3,2,1,0:T(8,128)(2,1)S(1)} %collective-permute-done.3.refs_3_), channel_id=1, source_target_pairs={{0,2},{2,0},{4,6},{6,4},{8,10},{10,8},{12,14},{14,12},{16,18},{18,... | collective-permute-start | bytes 786440 | tf_op jit(solution)/shard_map/ppermute | solution.py:389

commit v5 on v4

--- a/solution.py
+++ b/solution.py
@@ -243,6 +243,14 @@
     return acc
 
 
+def channel(refs, index, chan):
+    for i in index if isinstance(index, tuple) else (index,):
+        if chan < refs[i].shape[0]:
+            break
+        chan -= refs[i].shape[0]
+    return refs[i].at[chan]
+
+
 def cross_kernel(layout, jobs, *refs):
     groups, at = {}, 0
     for name, count in layout:
@@ -276,7 +284,7 @@
             for c_start in range(0, chans, step):
                 c_list = range(c_start, min(c_start + step, chans))
                 ours = [[mine[piece].at[a] for a in a_list] for piece, _ in pieces]
-                theirs = [[groups[source][ref].at[c] for c in c_list] for _, ref in pieces]
+                theirs = [[channel(groups[source], ref, c) for c in c_list] for _, ref in pieces]
                 order = [(a, c, i) for a in a_list for c in c_list for i in range(2)]
                 if acc_in is None:
                     acc = tuple(jnp.zeros((bands, LANES), jnp.float32) for _ in order)
@@ -316,28 +324,30 @@
         out_shape=[whole] * ends + [sums] * acc_count,
         scratch_shapes=scratch * ends,
         compiler_params=PARAMS,
-        cost_estimate=cost(0.6 * sum(len(job[1]) for job in jobs)),
+        cost_estimate=cost({"cross_mid": 30.0}.get(name, 0.6)),
         name=name,
     )(*operands)
 
 
-def choose(bit, own, far):
+def choose(bit, own, far, count=None):
+    count = count or far.shape[0]
+
     def kernel(own_ref, far_ref, out_ref):
         yes = lax.rem(lax.div(lax.axis_index("chan"), bit), 2) == 1
 
         @pl.when(yes)
         def _():
-            out_ref[...] = own_ref[...]
+            out_ref[...] = own_ref[pl.ds(0, count)]
 
         @pl.when(jnp.logical_not(yes))
         def _():
-            out_ref[...] = far_ref[...]
+            out_ref[...] = far_ref[pl.ds(0, count)]
 
     return pl.pallas_call(
         kernel,
         in_specs=[VMEM] * 2,
         out_specs=VMEM,
-        out_shape=jax.ShapeDtypeStruct(far.shape, far.dtype),
+        out_shape=jax.ShapeDtypeStruct((count,) + far.shape[1:], far.dtype),
         compiler_params=PARAMS,
         cost_estimate=cost(0.1),
         name="choose",
@@ -370,36 +380,45 @@
     )
     far[last] = after(far[last], acc_far)
     mid, one, two = [], [], []
+    half = chans // 2
+    direct = lax.ppermute(mine[last][half:], "chan", [(b, b - 2) for b in range(2, blocks)])
     for s in range(parts):
-        mid.append(lax.ppermute(choose(2, mine[s], far[s]), "chan", swap2))
+        count = None if s < last else half
+        mid.append(lax.ppermute(choose(2, mine[s], far[s], count), "chan", swap2))
         one.append(lax.ppermute(choose(1, mine[s], far[s]), "chan", swap1))
         if s < last:
             two.append(lax.ppermute(mid[s], "chan", swap1))
-    done_far, acc_mid, acc_one = call(
+    done_far, acc_mid = call(
         "cross_most",
         [
             ("far", [(last, 0)], 0, True, 0),
             ("mid", [(s, s) for s in early], None, False, 1),
-            ("one", [(s, s) for s in early], None, False, 2),
         ],
-        sources={"far": far[last:], "mid": mid[:last], "one": one[:last]},
+        sources={"far": far[last:], "mid": mid[:last]},
         acc_in=[acc_far],
     )
+    direct = after(direct, acc_mid)
+    two_direct = lax.ppermute(direct, "chan", swap1)
     mid[last] = after(mid[last], acc_mid)
     two.append(lax.ppermute(mid[last], "chan", swap1))
-    done_mid, done_one, acc_two = call(
+    (done_mid,) = call(
+        "cross_mid", [("mid", [(last, (0, 1))], 0, True, 0)],
+        sources={"mid": [mid[last], direct]}, acc_in=[acc_mid],
+    )
+    one[last] = after(one[last], done_mid)
+    two[0] = after(two[0], done_mid)
+    done_one, acc_two = call(
         "cross_next",
         [
-            ("mid", [(last, 0)], 0, True, 0),
-            ("one", [(last, 0)], 1, True, 1),
-            ("two", [(s, s) for s in early], None, False, 2),
+            ("one", [(s, s) for s in range(parts)], None, True, 0),
+            ("two", [(s, s) for s in early], None, False, 1),
         ],
-        sources={"mid": mid[last:], "one": one[last:], "two": two[:last]},
-        acc_in=[acc_mid, acc_one],
+        sources={"one": one, "two": two[:last]},
     )
     two[last] = after(two[last], acc_two)
     (out,) = call(
-        "cross_last", [("two", [(last, 0)], 0, True, None)], sources={"two": two[last:]},
+        "cross_last", [("two", [(last, (0, 1))], 0, True, None)],
+        sources={"two": [two[last], two_direct]},
         acc_in=[acc_two], done=[done_far, done_mid, done_one],
     )
     bands = out.shape[3] // 2

time: 32.4 us -> 32.3 us (level)
    ppermute x1, waiting for transfers between devices: 0.58 us -> 0.01 us  [shards(): two.append(lax.ppermute(mid[last], 'chan', swap1))]
    ppermute x2, starting transfers between devices: 0.14 us -> 0.65 us  [shards(): one.append(lax.ppermute(choose(1, mine[s], far[s]), 'chan', swap1))]
    ppermute x1, starting transfers between devices: 0.49 us -> 0.08 us  [shards(): two.append(lax.ppermute(mid[s], 'chan', swap1))]
    ppermute x1, waiting for transfers between devices: 0.01 us -> 0.36 us  [shards(): two.append(lax.ppermute(mid[s], 'chan', swap1))]
    ppermute x2 -> x4, waiting for transfers between devices: 3.75 us -> 3.65 us  [the longest x2 3.21 us: shards(): mid.append(lax.ppermute(choose(2, mine[s], far[s], count), 'chan', swap2))]
    ppermute x2 -> x4, starting transfers between devices: 3.02 us -> 2.94 us  [the longest x2 1.64 us: shards(): mid.append(lax.ppermute(choose(2, mine[s], far[s], count), 'chan', swap2))]
    pallas_call x4 -> x5, Pallas kernels: 3.09 us -> 3.01 us  [cross_call(): pl.pallas_call(functools.partial(cross_kernel, layout, jobs), in_specs=[V...]
  transfers between devices with their start and end apart: 9 -> 11, of which waited for: 5 -> 7; matrix products, arithmetic and copies ran while one was open for 0% -> 0% of each run, Pallas kernels for 9% -> 8%
where the time goes in v5:
time: 32.3 us; the launch traced here: 32.1 us
  waiting for transfers between devices  14.7 us (46%)
  starting transfers between devices  9.26 us (29%)
  Pallas kernels  7.08 us (22%)
  local copies, waits for them, and re-layouts  0.94 us (3%)
    ppermute x2, waiting for transfers between devices, shards(): far = [lax.ppermute(own, 'chan', up) for own in mine]  5.63 us
    ppermute x1, waiting for transfers between devices, shards(): lax.ppermute(spectra[s], 'win', [(i, (i + s) % parts) for i in range(part...  5.02 us
    ppermute x2, waiting for transfers between devices, shards(): mid.append(lax.ppermute(choose(2, mine[s], far[s], count), 'chan', swap2))  3.21 us
    ppermute x1, starting transfers between devices, shards(): lax.ppermute(spectra[s], 'win', [(i, (i + s) % parts) for i in range(part...  3.03 us
    pallas_call x1, Pallas kernels, whitened_spectra(): pl.pallas_call(functools.partial(spectra_kernel, parts), in_specs=[VMEM]...  3.01 us
    pallas_call x5, Pallas kernels, cross_call(): pl.pallas_call(functools.partial(cross_kernel, layout, jobs), in_specs=[V...  3.01 us
    ppermute x2, starting transfers between devices, shards(): far = [lax.ppermute(own, 'chan', up) for own in mine]  2.56 us
    ppermute x2, starting transfers between devices, shards(): mid.append(lax.ppermute(choose(2, mine[s], far[s], count), 'chan', swap2))  1.64 us
  transfers between devices with their start and end apart: 11, of which 7 were waited for; matrix products, arithmetic and copies ran while one was open for 0% of the time, Pallas kernels for 8%

profile of v5, /device:TPU:0, one launch (start us, length us, event | category | flops | bytes accessed | tf_op | source)
XLA Modules:
  0.0 32.1 jit_solution(3939048081569166951)
XLA Ops:
  0.0 0.0 copy-start
  0.0 0.3 tables.1
  0.3 0.9 %copy-done = f32[4,8,8192]{2,1,0:T(8,128)S(1)} copy-done((f32[4,8,8192]{2,1,0:T(8,128)S(1)}, f32[4,8,8192]{2,1,0:T(8,128)}, u32[]{:S(2)}) %copy-start) | copy-done | bytes 1048600
  1.2 3.0 %spectra.1 = (bf16[4,8,32,128]{3,2,1,0:T(8,128)(2,1)S(1)}, bf16[4,8,32,128]{3,2,1,0:T(8,128)(2,1)S(1)}) custom-call(f32[4,64,8,128]{3,2,1,0:T(8,128)S(1)} %bitcast.8, f32[2,64,128]{2,1,0:T(8,128)S(1)} %get-tuple-element.23.refs_0_, bf16[512,256]{1,0:T(8,128)(2,1)S(1)} %get-tuple-element.24.refs_1_, bf16[512,128]{1,0:T(8,128)(2,1)S(1)} %get-tuple-element.25.refs_2_, ...), custom_call_target="tpu_custom_call" | custom-call | flops 4400000000 | tf_op jit(solution)/shard_map/spectra/pallas_call | solution.py:206
  4.2 3.0 %collective-permute-start.1 = (bf16[4,8,32,128]{3,2,1,0:T(8,128)(2,1)S(1)}, bf16[4,8,32,128]{3,2,1,0:T(8,128)(2,1)S(1)}, u32[]{:S(2)}, u32[]{:S(2)}) collective-permute-start(bf16[4,8,32,128]{3,2,1,0:T(8,128)(2,1)S(1)} %get-tuple-element.30), channel_id=1, source_target_pairs={{0,1},{1,0},{2,3},{3,2},{4,5},{5,4},{6,7},{7,6},{8,9},{9,8},{10,11... | collective-permute-start | bytes 786440 | tf_op jit(solution)/shard_map/ppermute | solution.py:371
  7.3 1.3 %collective-permute-start = (bf16[4,8,32,128]{3,2,1,0:T(8,128)(2,1)S(1)}, bf16[4,8,32,128]{3,2,1,0:T(8,128)(2,1)S(1)}, u32[]{:S(2)}, u32[]{:S(2)}) collective-permute-start(bf16[4,8,32,128]{3,2,1,0:T(8,128)(2,1)S(1)} %get-tuple-element.28.refs_1_.own_ref), channel_id=1, source_target_pairs={{8,0},{10,2},{12,4},{14,6},{16,8},{18,10},{20,12},{22,14},{24,16},... | collective-permute-start | bytes 786440 | tf_op jit(solution)/shard_map/ppermute | solution.py:372
  8.6 5.0 %collective-permute-done.1.refs_2_.own_ref = bf16[4,8,32,128]{3,2,1,0:T(8,128)(2,1)S(1)} collective-permute-done((bf16[4,8,32,128]{3,2,1,0:T(8,128)(2,1)S(1)}, bf16[4,8,32,128]{3,2,1,0:T(8,128)(2,1)S(1)}, u32[]{:S(2)}, u32[]{:S(2)}) %collective-permute-start.1) | collective-permute-done | bytes 262176 | tf_op jit(solution)/shard_map/ppermute | solution.py:371
  13.6 1.3 %collective-permute-start.2 = (bf16[4,8,32,128]{3,2,1,0:T(8,128)(2,1)S(1)}, bf16[4,8,32,128]{3,2,1,0:T(8,128)(2,1)S(1)}, u32[]{:S(2)}, u32[]{:S(2)}) collective-permute-start(bf16[4,8,32,128]{3,2,1,0:T(8,128)(2,1)S(1)} %collective-permute-done.1.refs_2_.own_ref), channel_id=1, source_target_pairs={{8,0},{10,2},{12,4},{14,6},{16,8},{18,10},{20,12},{22,14},{24,16},... | collective-permute-start | bytes 786440 | tf_op jit(solution)/shard_map/ppermute | solution.py:372
  14.9 2.1 %collective-permute-done.refs_3_.far_ref = bf16[4,8,32,128]{3,2,1,0:T(8,128)(2,1)S(1)} collective-permute-done((bf16[4,8,32,128]{3,2,1,0:T(8,128)(2,1)S(1)}, bf16[4,8,32,128]{3,2,1,0:T(8,128)(2,1)S(1)}, u32[]{:S(2)}, u32[]{:S(2)}) %collective-permute-start) | collective-permute-done | bytes 262176 | tf_op jit(solution)/shard_map/ppermute | solution.py:372
  17.0 0.0 copy-start.1
  17.0 1.6 %collective-permute-start.4 = (bf16[4,8,32,128]{3,2,1,0:T(8,128)(2,1)S(1)}, bf16[4,8,32,128]{3,2,1,0:T(8,128)(2,1)S(1)}, u32[]{:S(2)}, u32[]{:S(2)}) collective-permute-start(bf16[4,8,32,128]{3,2,1,0:T(8,128)(2,1)S(1)} %choose.5), channel_id=1, source_target_pairs={{0,4},{2,6},{4,0},{6,2},{8,12},{10,14},{12,8},{14,10},{16,20},{18,... | collective-permute-start | bytes 786440 | tf_op jit(solution)/shard_map/ppermute | solution.py:387
  18.5 1.3 %collective-permute-start.8 = (bf16[2,8,32,128]{3,2,1,0:T(8,128)(2,1)S(1)}, bf16[2,8,32,128]{3,2,1,0:T(8,128)(2,1)S(1)}, u32[]{:S(2)}, u32[]{:S(2)}) collective-permute-start(bf16[2,8,32,128]{3,2,1,0:T(8,128)(2,1)S(1)} %slice.4), channel_id=1, source_target_pairs={{4,0},{6,2},{8,4},{10,6},{12,8},{14,10},{16,12},{18,14},{20,16},{2... | collective-permute-start | bytes 393224 | tf_op jit(solution)/shard_map/ppermute | solution.py:384
  19.8 0.0 copy-done.1
  19.9 0.7 %gains.1.refs_0_ = f32[64,128]{1,0:T(8,128)S(1)} custom-call(s32[64]{0:T(128)S(1)} %copy-done.1), custom_call_target="tpu_custom_call" | custom-call | flops 550000000 | tf_op jit(solution)/shard_map/gains/pallas_call | solution.py:142
  20.5 0.2 cross_far.1.refs_5_
  20.8 3.6 %collective-permute-done.2.far_ref.refs_3_ = bf16[4,8,32,128]{3,2,1,0:T(8,128)(2,1)S(1)} collective-permute-done((bf16[4,8,32,128]{3,2,1,0:T(8,128)(2,1)S(1)}, bf16[4,8,32,128]{3,2,1,0:T(8,128)(2,1)S(1)}, u32[]{:S(2)}, u32[]{:S(2)}) %collective-permute-start.2) | collective-permute-done | bytes 262176 | tf_op jit(solution)/shard_map/ppermute | solution.py:372
  24.4 0.1 collective-permute-start.3
  24.5 0.1 collective-permute-start.6
  24.6 2.5 %collective-permute-done.4.refs_4_ = bf16[4,8,32,128]{3,2,1,0:T(8,128)(2,1)S(1)} collective-permute-done((bf16[4,8,32,128]{3,2,1,0:T(8,128)(2,1)S(1)}, bf16[4,8,32,128]{3,2,1,0:T(8,128)(2,1)S(1)}, u32[]{:S(2)}, u32[]{:S(2)}) %collective-permute-start.4) | collective-permute-done | bytes 262176 | tf_op jit(solution)/shard_map/ppermute | solution.py:387
  27.1 0.6 %cross_most.1 = (f32[4,4,32,128]{3,2,1,0:T(8,128)S(1)}, f32[4,4,32,128]{3,2,1,0:T(8,128)S(1)}) custom-call(f32[64,128]{1,0:T(8,128)S(1)} %gains.1.refs_0_, bf16[4,8,32,128]{3,2,1,0:T(8,128)(2,1)S(1)} %get-tuple-element.28.refs_1_.own_ref, bf16[4,8,32,128]{3,2,1,0:T(8,128)(2,1)S(1)} %collective-permute-done.1.refs_2_.own_ref, ...), custom_call_target="tpu_custom_call" | custom-call | flops 660000000 | tf_op jit(solution)/shard_map/cross_most/pallas_call | solution.py:320
  27.7 0.4 %collective-permute-done.8.refs_4_ = bf16[2,8,32,128]{3,2,1,0:T(8,128)(2,1)S(1)} collective-permute-done((bf16[2,8,32,128]{3,2,1,0:T(8,128)(2,1)S(1)}, bf16[2,8,32,128]{3,2,1,0:T(8,128)(2,1)S(1)}, u32[]{:S(2)}, u32[]{:S(2)}) %collective-permute-start.8) | collective-permute-done | bytes 131104 | tf_op jit(solution)/shard_map/ppermute | solution.py:384
  28.1 0.0 collective-permute-start.10
  28.1 0.6 %collective-permute-start.7 = (bf16[4,8,32,128]{3,2,1,0:T(8,128)(2,1)S(1)}, bf16[4,8,32,128]{3,2,1,0:T(8,128)(2,1)S(1)}, u32[]{:S(2)}, u32[]{:S(2)}) collective-permute-start(bf16[4,8,32,128]{3,2,1,0:T(8,128)(2,1)S(1)} %choose.7), channel_id=1, source_target_pairs={{0,2},{2,0},{4,6},{6,4},{8,10},{10,8},{12,14},{14,12},{16,18},{18,... | collective-permute-start | bytes 786440 | tf_op jit(solution)/shard_map/ppermute | solution.py:388
  28.7 0.1 collective-permute-start.9
  28.8 0.7 %collective-permute-done.3.refs_3_ = bf16[2,8,32,128]{3,2,1,0:T(8,128)(2,1)S(1)} collective-permute-done((bf16[2,8,32,128]{3,2,1,0:T(8,128)(2,1)S(1)}, bf16[2,8,32,128]{3,2,1,0:T(8,128)(2,1)S(1)}, u32[]{:S(2)}, u32[]{:S(2)}) %collective-permute-start.3) | collective-permute-done | bytes 131104 | tf_op jit(solution)/shard_map/ppermute | solution.py:387
  29.5 0.0 collective-permute-start.5
  29.5 0.4 %cross_mid.1.refs_7_ = f32[4,4,32,128]{3,2,1,0:T(8,128)S(1)} custom-call(f32[64,128]{1,0:T(8,128)S(1)} %gains.1.refs_0_, bf16[4,8,32,128]{3,2,1,0:T(8,128)(2,1)S(1)} %get-tuple-element.28.refs_1_.own_ref, bf16[4,8,32,128]{3,2,1,0:T(8,128)(2,1)S(1)} %collective-permute-done.1.refs_2_.own_ref, bf16[2,8,32,128]{3,2,1,0:T(8,128)(2,1)S(1)} %collective-permute-done.3.refs_3_, ...), custom_call_target="tpu_custom_call" | custom-call | flops 32999999488 | tf_op jit(solution)/shard_map/cross_mid/pallas_call | solution.py:320
  29.9 0.4 %collective-permute-done.9.refs_5_ = bf16[4,8,32,128]{3,2,1,0:T(8,128)(2,1)S(1)} collective-permute-done((bf16[4,8,32,128]{3,2,1,0:T(8,128)(2,1)S(1)}, bf16[4,8,32,128]{3,2,1,0:T(8,128)(2,1)S(1)}, u32[]{:S(2)}, u32[]{:S(2)}) %collective-permute-start.9) | collective-permute-done | bytes 262176 | tf_op jit(solution)/shard_map/ppermute | solution.py:390
  30.2 0.0 collective-permute-done.7.refs_4_
  30.2 0.0 collective-permute-done.6.refs_3_
  30.2 0.7 %cross_next.1 = (f32[4,4,32,128]{3,2,1,0:T(8,128)S(1)}, f32[4,4,32,128]{3,2,1,0:T(8,128)S(1)}) custom-call(f32[64,128]{1,0:T(8,128)S(1)} %gains.1.refs_0_, bf16[4,8,32,128]{3,2,1,0:T(8,128)(2,1)S(1)} %get-tuple-element.28.refs_1_.own_ref, bf16[4,8,32,128]{3,2,1,0:T(8,128)(2,1)S(1)} %collective-permute-done.1.refs_2_.own_ref, ...), custom_call_target="tpu_custom_call" | custom-call | flops 660000000 | tf_op jit(solution)/shard_map/cross_next/pallas_call | solution.py:320
  31.0 0.0 collective-permute-done.5.refs_3_
  31.0 0.0 collective-permute-done.10.refs_4_
  31.0 1.1 %cross_last.1 = f32[4,4,4,32,128]{4,3,2,1,0:T(8,128)} custom-call(f32[64,128]{1,0:T(8,128)S(1)} %gains.1.refs_0_, bf16[4,8,32,128]{3,2,1,0:T(8,128)(2,1)S(1)} %get-tuple-element.28.refs_1_.own_ref, bf16[4,8,32,128]{3,2,1,0:T(8,128)(2,1)S(1)} %collective-permute-done.1.refs_2_.own_ref, bf16[2,8,32,128]{3,2,1,0:T(8,128)(2,1)S(1)} %collective-permute-done.5.refs_3_, ...), custom_call_target="tpu_custom_call" | custom-call | flops 660000000 | tf_op jit(solution)/shard_map/cross_last/pallas_call | solution.py:320
  (5 shorter events, 0.1 us)
Async XLA Ops:
  0.0 1.2 %copy-start = (f32[4,8,8192]{2,1,0:T(8,128)S(1)}, f32[4,8,8192]{2,1,0:T(8,128)}, u32[]{:S(2)}) copy-start(f32[4,8,8192]{2,1,0:T(8,128)} %param.2) | copy-start | bytes 3145732
  4.2 9.3 %collective-permute-start.1 = (bf16[4,8,32,128]{3,2,1,0:T(8,128)(2,1)S(1)}, bf16[4,8,32,128]{3,2,1,0:T(8,128)(2,1)S(1)}, u32[]{:S(2)}, u32[]{:S(2)}) collective-permute-start(bf16[4,8,32,128]{3,2,1,0:T(8,128)(2,1)S(1)} %get-tuple-element.30), channel_id=1, source_target_pairs={{0,1},{1,0},{2,3},{3,2},{4,5},{5,4},{6,7},{7,6},{8,9},{9,8},{10,11... | collective-permute-start | bytes 786440 | tf_op jit(solution)/shard_map/ppermute | solution.py:371
  7.3 9.6 %collective-permute-start = (bf16[4,8,32,128]{3,2,1,0:T(8,128)(2,1)S(1)}, bf16[4,8,32,128]{3,2,1,0:T(8,128)(2,1)S(1)}, u32[]{:S(2)}, u32[]{:S(2)}) collective-permute-start(bf16[4,8,32,128]{3,2,1,0:T(8,128)(2,1)S(1)} %get-tuple-element.28.refs_1_.own_ref), channel_id=1, source_target_pairs={{8,0},{10,2},{12,4},{14,6},{16,8},{18,10},{20,12},{22,14},{24,16},... | collective-permute-start | bytes 786440 | tf_op jit(solution)/shard_map/ppermute | solution.py:372
  13.6 10.8 %collective-permute-start.2 = (bf16[4,8,32,128]{3,2,1,0:T(8,128)(2,1)S(1)}, bf16[4,8,32,128]{3,2,1,0:T(8,128)(2,1)S(1)}, u32[]{:S(2)}, u32[]{:S(2)}) collective-permute-start(bf16[4,8,32,128]{3,2,1,0:T(8,128)(2,1)S(1)} %collective-permute-done.1.refs_2_.own_ref), channel_id=1, source_target_pairs={{8,0},{10,2},{12,4},{14,6},{16,8},{18,10},{20,12},{22,14},{24,16},... | collective-permute-start | bytes 786440 | tf_op jit(solution)/shard_map/ppermute | solution.py:372
  17.0 2.9 %copy-start.1 = (s32[64]{0:T(128)S(1)}, s32[64]{0:T(128)}, u32[]{:S(2)}) copy-start(s32[64]{0:T(128)} %pos_ref) | copy-start | bytes 772
  17.0 10.1 %collective-permute-start.4 = (bf16[4,8,32,128]{3,2,1,0:T(8,128)(2,1)S(1)}, bf16[4,8,32,128]{3,2,1,0:T(8,128)(2,1)S(1)}, u32[]{:S(2)}, u32[]{:S(2)}) collective-permute-start(bf16[4,8,32,128]{3,2,1,0:T(8,128)(2,1)S(1)} %choose.5), channel_id=1, source_target_pairs={{0,4},{2,6},{4,0},{6,2},{8,12},{10,14},{12,8},{14,10},{16,20},{18,... | collective-permute-start | bytes 786440 | tf_op jit(solution)/shard_map/ppermute | solution.py:387
  18.5 9.6 %collective-permute-start.8 = (bf16[2,8,32,128]{3,2,1,0:T(8,128)(2,1)S(1)}, bf16[2,8,32,128]{3,2,1,0:T(8,128)(2,1)S(1)}, u32[]{:S(2)}, u32[]{:S(2)}) collective-permute-start(bf16[2,8,32,128]{3,2,1,0:T(8,128)(2,1)S(1)} %slice.4), channel_id=1, source_target_pairs={{4,0},{6,2},{8,4},{10,6},{12,8},{14,10},{16,12},{18,14},{20,16},{2... | collective-permute-start | bytes 393224 | tf_op jit(solution)/shard_map/ppermute | solution.py:384
  24.4 5.1 %collective-permute-start.3 = (bf16[2,8,32,128]{3,2,1,0:T(8,128)(2,1)S(1)}, bf16[2,8,32,128]{3,2,1,0:T(8,128)(2,1)S(1)}, u32[]{:S(2)}, u32[]{:S(2)}) collective-permute-start(bf16[2,8,32,128]{3,2,1,0:T(8,128)(2,1)S(1)} %choose.4), channel_id=1, source_target_pairs={{0,4},{2,6},{4,0},{6,2},{8,12},{10,14},{12,8},{14,10},{16,20},{18,... | collective-permute-start | bytes 393224 | tf_op jit(solution)/shard_map/ppermute | solution.py:387
  24.5 5.7 %collective-permute-start.6 = (bf16[4,8,32,128]{3,2,1,0:T(8,128)(2,1)S(1)}, bf16[4,8,32,128]{3,2,1,0:T(8,128)(2,1)S(1)}, u32[]{:S(2)}, u32[]{:S(2)}) collective-permute-start(bf16[4,8,32,128]{3,2,1,0:T(8,128)(2,1)S(1)} %choose.6), channel_id=1, source_target_pairs={{0,2},{2,0},{4,6},{6,4},{8,10},{10,8},{12,14},{14,12},{16,18},{18,... | collective-permute-start | bytes 786440 | tf_op jit(solution)/shard_map/ppermute | solution.py:388
  28.1 2.9 %collective-permute-start.10 = (bf16[2,8,32,128]{3,2,1,0:T(8,128)(2,1)S(1)}, bf16[2,8,32,128]{3,2,1,0:T(8,128)(2,1)S(1)}, u32[]{:S(2)}, u32[]{:S(2)}) collective-permute-start(bf16[2,8,32,128]{3,2,1,0:T(8,128)(2,1)S(1)} %collective-permute-done.8.refs_4_), channel_id=1, source_target_pairs={{0,2},{2,0},{4,6},{6,4},{8,10},{10,8},{12,14},{14,12},{16,18},{18,... | collective-permute-start | bytes 393224 | tf_op jit(solution)/shard_map/ppermute | solution.py:401
  28.1 2.1 %collective-permute-start.7 = (bf16[4,8,32,128]{3,2,1,0:T(8,128)(2,1)S(1)}, bf16[4,8,32,128]{3,2,1,0:T(8,128)(2,1)S(1)}, u32[]{:S(2)}, u32[]{:S(2)}) collective-permute-start(bf16[4,8,32,128]{3,2,1,0:T(8,128)(2,1)S(1)} %choose.7), channel_id=1, source_target_pairs={{0,2},{2,0},{4,6},{6,4},{8,10},{10,8},{12,14},{14,12},{16,18},{18,... | collective-permute-start | bytes 786440 | tf_op jit(solution)/shard_map/ppermute | solution.py:388
  28.7 1.5 %collective-permute-start.9 = (bf16[4,8,32,128]{3,2,1,0:T(8,128)(2,1)S(1)}, bf16[4,8,32,128]{3,2,1,0:T(8,128)(2,1)S(1)}, u32[]{:S(2)}, u32[]{:S(2)}) collective-permute-start(bf16[4,8,32,128]{3,2,1,0:T(8,128)(2,1)S(1)} %collective-permute-done.4.refs_4_), channel_id=1, source_target_pairs={{0,2},{2,0},{4,6},{6,4},{8,10},{10,8},{12,14},{14,12},{16,18},{18,... | collective-permute-start | bytes 786440 | tf_op jit(solution)/shard_map/ppermute | solution.py:390
  29.5 1.5 %collective-permute-start.5 = (bf16[2,8,32,128]{3,2,1,0:T(8,128)(2,1)S(1)}, bf16[2,8,32,128]{3,2,1,0:T(8,128)(2,1)S(1)}, u32[]{:S(2)}, u32[]{:S(2)}) collective-permute-start(bf16[2,8,32,128]{3,2,1,0:T(8,128)(2,1)S(1)} %collective-permute-done.3.refs_3_), channel_id=1, source_target_pairs={{0,2},{2,0},{4,6},{6,4},{8,10},{10,8},{12,14},{14,12},{16,18},{18,... | collective-permute-start | bytes 393224 | tf_op jit(solution)/shard_map/ppermute | solution.py:403

commit v6 on v5

--- a/solution.py
+++ b/solution.py
@@ -243,14 +243,6 @@
     return acc
 
 
-def channel(refs, index, chan):
-    for i in index if isinstance(index, tuple) else (index,):
-        if chan < refs[i].shape[0]:
-            break
-        chan -= refs[i].shape[0]
-    return refs[i].at[chan]
-
-
 def cross_kernel(layout, jobs, *refs):
     groups, at = {}, 0
     for name, count in layout:
@@ -284,7 +276,7 @@
             for c_start in range(0, chans, step):
                 c_list = range(c_start, min(c_start + step, chans))
                 ours = [[mine[piece].at[a] for a in a_list] for piece, _ in pieces]
-                theirs = [[channel(groups[source], ref, c) for c in c_list] for _, ref in pieces]
+                theirs = [[groups[source][ref].at[c] for c in c_list] for _, ref in pieces]
                 order = [(a, c, i) for a in a_list for c in c_list for i in range(2)]
                 if acc_in is None:
                     acc = tuple(jnp.zeros((bands, LANES), jnp.float32) for _ in order)
@@ -354,6 +346,25 @@
     )(own, far)
 
 
+def join(estimate, *arrays):
+    def kernel(*refs):
+        start = 0
+        for ref in refs[:-1]:
+            refs[-1][pl.ds(start, ref.shape[0])] = ref[...]
+            start += ref.shape[0]
+
+    shape = (sum(array.shape[0] for array in arrays),) + arrays[0].shape[1:]
+    return pl.pallas_call(
+        kernel,
+        in_specs=[VMEM] * len(arrays),
+        out_specs=VMEM,
+        out_shape=jax.ShapeDtypeStruct(shape, arrays[0].dtype),
+        compiler_params=PARAMS,
+        cost_estimate=cost(estimate),
+        name="join",
+    )(*arrays)
+
+
 def after(value, *others):
     return lax.optimization_barrier((value, *others))[0]
 
@@ -397,13 +408,12 @@
         sources={"far": far[last:], "mid": mid[:last]},
         acc_in=[acc_far],
     )
-    direct = after(direct, acc_mid)
-    two_direct = lax.ppermute(direct, "chan", swap1)
-    mid[last] = after(mid[last], acc_mid)
+    direct = join(0.1, after(direct, acc_mid))
+    mid[last] = join(0.1, after(mid[last], direct), direct)
     two.append(lax.ppermute(mid[last], "chan", swap1))
     (done_mid,) = call(
-        "cross_mid", [("mid", [(last, (0, 1))], 0, True, 0)],
-        sources={"mid": [mid[last], direct]}, acc_in=[acc_mid],
+        "cross_mid", [("mid", [(last, 0)], 0, True, 0)],
+        sources={"mid": mid[last:]}, acc_in=[acc_mid],
     )
     one[last] = after(one[last], done_mid)
     two[0] = after(two[0], done_mid)
@@ -417,8 +427,7 @@
     )
     two[last] = after(two[last], acc_two)
     (out,) = call(
-        "cross_last", [("two", [(last, (0, 1))], 0, True, None)],
-        sources={"two": [two[last], two_direct]},
+        "cross_last", [("two", [(last, 0)], 0, True, None)], sources={"two": two[last:]},
         acc_in=[acc_two], done=[done_far, done_mid, done_one],
     )
     bands = out.shape[3] // 2

time: 32.3 us -> 32.4 us (level)
    ppermute x2, starting transfers between devices: 0.65 us -> 0.14 us  [shards(): one.append(lax.ppermute(choose(1, mine[s], far[s]), 'chan', swap1))]
    ppermute x1, starting transfers between devices: 0.08 us -> 0.5 us  [shards(): two.append(lax.ppermute(mid[s], 'chan', swap1))]
  transfers between devices with their start and end apart: 11 -> 10, of which waited for: 7 -> 8; matrix products, arithmetic and copies ran while one was open for 0% -> 0% of each run, Pallas kernels for 8% -> 8%
where the time goes in v6:
time: 32.4 us; the launch traced here: 32.2 us
  waiting for transfers between devices  14.8 us (46%)
  starting transfers between devices  9.24 us (29%)
  Pallas kernels  7.11 us (22%)
  local copies, waits for them, and re-layouts  0.94 us (3%)
    ppermute x2, waiting for transfers between devices, shards(): far = [lax.ppermute(own, 'chan', up) for own in mine]  5.63 us
    ppermute x1, waiting for transfers between devices, shards(): lax.ppermute(spectra[s], 'win', [(i, (i + s) % parts) for i in range(part...  5.02 us
    ppermute x2, waiting for transfers between devices, shards(): mid.append(lax.ppermute(choose(2, mine[s], far[s], count), 'chan', swap2))  3.28 us
    ppermute x1, starting transfers between devices, shards(): lax.ppermute(spectra[s], 'win', [(i, (i + s) % parts) for i in range(part...  3.03 us
    pallas_call x1, Pallas kernels, whitened_spectra(): pl.pallas_call(functools.partial(spectra_kernel, parts), in_specs=[VMEM]...  3.01 us
    pallas_call x5, Pallas kernels, cross_call(): pl.pallas_call(functools.partial(cross_kernel, layout, jobs), in_specs=[V...  3.01 us
    ppermute x2, starting transfers between devices, shards(): far = [lax.ppermute(own, 'chan', up) for own in mine]  2.56 us
    ppermute x2, starting transfers between devices, shards(): mid.append(lax.ppermute(choose(2, mine[s], far[s], count), 'chan', swap2))  1.64 us
  transfers between devices with their start and end apart: 10, of which 8 were waited for; matrix products, arithmetic and copies ran while one was open for 0% of the time, Pallas kernels for 8%

profile of v6, /device:TPU:0, one launch (start us, length us, event | category | flops | bytes accessed | tf_op | source)
XLA Modules:
  0.0 32.2 jit_solution(4442576330315693057)
XLA Ops:
  0.0 0.0 copy-start
  0.0 0.3 tables.1
  0.3 0.9 %copy-done = f32[4,8,8192]{2,1,0:T(8,128)S(1)} copy-done((f32[4,8,8192]{2,1,0:T(8,128)S(1)}, f32[4,8,8192]{2,1,0:T(8,128)}, u32[]{:S(2)}) %copy-start) | copy-done | bytes 1048600
  1.2 3.0 %spectra.1 = (bf16[4,8,32,128]{3,2,1,0:T(8,128)(2,1)S(1)}, bf16[4,8,32,128]{3,2,1,0:T(8,128)(2,1)S(1)}) custom-call(f32[4,64,8,128]{3,2,1,0:T(8,128)S(1)} %bitcast.8, f32[2,64,128]{2,1,0:T(8,128)S(1)} %get-tuple-element.23.refs_0_, bf16[512,256]{1,0:T(8,128)(2,1)S(1)} %get-tuple-element.24.refs_1_, bf16[512,128]{1,0:T(8,128)(2,1)S(1)} %get-tuple-element.25.refs_2_, ...), custom_call_target="tpu_custom_call" | custom-call | flops 4400000000 | tf_op jit(solution)/shard_map/spectra/pallas_call | solution.py:206
  4.2 3.0 %collective-permute-start.1 = (bf16[4,8,32,128]{3,2,1,0:T(8,128)(2,1)S(1)}, bf16[4,8,32,128]{3,2,1,0:T(8,128)(2,1)S(1)}, u32[]{:S(2)}, u32[]{:S(2)}) collective-permute-start(bf16[4,8,32,128]{3,2,1,0:T(8,128)(2,1)S(1)} %get-tuple-element.30), channel_id=1, source_target_pairs={{0,1},{1,0},{2,3},{3,2},{4,5},{5,4},{6,7},{7,6},{8,9},{9,8},{10,11... | collective-permute-start | bytes 786440 | tf_op jit(solution)/shard_map/ppermute | solution.py:382
  7.3 1.3 %collective-permute-start = (bf16[4,8,32,128]{3,2,1,0:T(8,128)(2,1)S(1)}, bf16[4,8,32,128]{3,2,1,0:T(8,128)(2,1)S(1)}, u32[]{:S(2)}, u32[]{:S(2)}) collective-permute-start(bf16[4,8,32,128]{3,2,1,0:T(8,128)(2,1)S(1)} %get-tuple-element.28.refs_1_.own_ref), channel_id=1, source_target_pairs={{8,0},{10,2},{12,4},{14,6},{16,8},{18,10},{20,12},{22,14},{24,16},... | collective-permute-start | bytes 786440 | tf_op jit(solution)/shard_map/ppermute | solution.py:383
  8.6 5.0 %collective-permute-done.1.refs_2_.own_ref = bf16[4,8,32,128]{3,2,1,0:T(8,128)(2,1)S(1)} collective-permute-done((bf16[4,8,32,128]{3,2,1,0:T(8,128)(2,1)S(1)}, bf16[4,8,32,128]{3,2,1,0:T(8,128)(2,1)S(1)}, u32[]{:S(2)}, u32[]{:S(2)}) %collective-permute-start.1) | collective-permute-done | bytes 262176 | tf_op jit(solution)/shard_map/ppermute | solution.py:382
  13.6 1.3 %collective-permute-start.2 = (bf16[4,8,32,128]{3,2,1,0:T(8,128)(2,1)S(1)}, bf16[4,8,32,128]{3,2,1,0:T(8,128)(2,1)S(1)}, u32[]{:S(2)}, u32[]{:S(2)}) collective-permute-start(bf16[4,8,32,128]{3,2,1,0:T(8,128)(2,1)S(1)} %collective-permute-done.1.refs_2_.own_ref), channel_id=1, source_target_pairs={{8,0},{10,2},{12,4},{14,6},{16,8},{18,10},{20,12},{22,14},{24,16},... | collective-permute-start | bytes 786440 | tf_op jit(solution)/shard_map/ppermute | solution.py:383
  14.9 2.1 %collective-permute-done.refs_3_.far_ref = bf16[4,8,32,128]{3,2,1,0:T(8,128)(2,1)S(1)} collective-permute-done((bf16[4,8,32,128]{3,2,1,0:T(8,128)(2,1)S(1)}, bf16[4,8,32,128]{3,2,1,0:T(8,128)(2,1)S(1)}, u32[]{:S(2)}, u32[]{:S(2)}) %collective-permute-start) | collective-permute-done | bytes 262176 | tf_op jit(solution)/shard_map/ppermute | solution.py:383
  17.0 0.0 copy-start.1
  17.0 1.6 %collective-permute-start.5 = (bf16[4,8,32,128]{3,2,1,0:T(8,128)(2,1)S(1)}, bf16[4,8,32,128]{3,2,1,0:T(8,128)(2,1)S(1)}, u32[]{:S(2)}, u32[]{:S(2)}) collective-permute-start(bf16[4,8,32,128]{3,2,1,0:T(8,128)(2,1)S(1)} %choose.5), channel_id=1, source_target_pairs={{0,4},{2,6},{4,0},{6,2},{8,12},{10,14},{12,8},{14,10},{16,20},{18,... | collective-permute-start | bytes 786440 | tf_op jit(solution)/shard_map/ppermute | solution.py:398
  18.5 1.3 %collective-permute-start.4 = (bf16[2,8,32,128]{3,2,1,0:T(8,128)(2,1)S(1)}, bf16[2,8,32,128]{3,2,1,0:T(8,128)(2,1)S(1)}, u32[]{:S(2)}, u32[]{:S(2)}) collective-permute-start(bf16[2,8,32,128]{3,2,1,0:T(8,128)(2,1)S(1)} %slice.4), channel_id=1, source_target_pairs={{4,0},{6,2},{8,4},{10,6},{12,8},{14,10},{16,12},{18,14},{20,16},{2... | collective-permute-start | bytes 393224 | tf_op jit(solution)/shard_map/ppermute | solution.py:395
  19.8 0.0 copy-done.1
  19.9 0.7 %gains.1.refs_0_ = f32[64,128]{1,0:T(8,128)S(1)} custom-call(s32[64]{0:T(128)S(1)} %copy-done.1), custom_call_target="tpu_custom_call" | custom-call | flops 550000000 | tf_op jit(solution)/shard_map/gains/pallas_call | solution.py:142
  20.5 0.2 cross_far.1.refs_5_
  20.8 3.6 %collective-permute-done.2.far_ref.refs_3_ = bf16[4,8,32,128]{3,2,1,0:T(8,128)(2,1)S(1)} collective-permute-done((bf16[4,8,32,128]{3,2,1,0:T(8,128)(2,1)S(1)}, bf16[4,8,32,128]{3,2,1,0:T(8,128)(2,1)S(1)}, u32[]{:S(2)}, u32[]{:S(2)}) %collective-permute-start.2) | collective-permute-done | bytes 262176 | tf_op jit(solution)/shard_map/ppermute | solution.py:383
  24.4 0.1 collective-permute-start.3
  24.5 0.1 collective-permute-start.7
  24.6 2.5 %collective-permute-done.5.refs_4_ = bf16[4,8,32,128]{3,2,1,0:T(8,128)(2,1)S(1)} collective-permute-done((bf16[4,8,32,128]{3,2,1,0:T(8,128)(2,1)S(1)}, bf16[4,8,32,128]{3,2,1,0:T(8,128)(2,1)S(1)}, u32[]{:S(2)}, u32[]{:S(2)}) %collective-permute-start.5) | collective-permute-done | bytes 262176 | tf_op jit(solution)/shard_map/ppermute | solution.py:398
  27.1 0.6 %cross_most.1 = (f32[4,4,32,128]{3,2,1,0:T(8,128)S(1)}, f32[4,4,32,128]{3,2,1,0:T(8,128)S(1)}) custom-call(f32[64,128]{1,0:T(8,128)S(1)} %gains.1.refs_0_, bf16[4,8,32,128]{3,2,1,0:T(8,128)(2,1)S(1)} %get-tuple-element.28.refs_1_.own_ref, bf16[4,8,32,128]{3,2,1,0:T(8,128)(2,1)S(1)} %collective-permute-done.1.refs_2_.own_ref, ...), custom_call_target="tpu_custom_call" | custom-call | flops 660000000 | tf_op jit(solution)/shard_map/cross_most/pallas_call | solution.py:312
  27.7 0.4 %collective-permute-done.4.refs_0_ = bf16[2,8,32,128]{3,2,1,0:T(8,128)(2,1)S(1)} collective-permute-done((bf16[2,8,32,128]{3,2,1,0:T(8,128)(2,1)S(1)}, bf16[2,8,32,128]{3,2,1,0:T(8,128)(2,1)S(1)}, u32[]{:S(2)}, u32[]{:S(2)}) %collective-permute-start.4) | collective-permute-done | bytes 131104 | tf_op jit(solution)/shard_map/ppermute | solution.py:395
  28.1 0.1 collective-permute-start.8
  28.2 0.5 %collective-permute-start.9 = (bf16[4,8,32,128]{3,2,1,0:T(8,128)(2,1)S(1)}, bf16[4,8,32,128]{3,2,1,0:T(8,128)(2,1)S(1)}, u32[]{:S(2)}, u32[]{:S(2)}) collective-permute-start(bf16[4,8,32,128]{3,2,1,0:T(8,128)(2,1)S(1)} %collective-permute-done.5.refs_4_), channel_id=1, source_target_pairs={{0,2},{2,0},{4,6},{6,4},{8,10},{10,8},{12,14},{14,12},{16,18},{18,... | collective-permute-start | bytes 786440 | tf_op jit(solution)/shard_map/ppermute | solution.py:401
  28.7 0.8 %collective-permute-done.3.refs_0_ = bf16[2,8,32,128]{3,2,1,0:T(8,128)(2,1)S(1)} collective-permute-done((bf16[2,8,32,128]{3,2,1,0:T(8,128)(2,1)S(1)}, bf16[2,8,32,128]{3,2,1,0:T(8,128)(2,1)S(1)}, u32[]{:S(2)}, u32[]{:S(2)}) %collective-permute-start.3) | collective-permute-done | bytes 131104 | tf_op jit(solution)/shard_map/ppermute | solution.py:398
  29.5 0.1 collective-permute-start.6
  29.6 0.4 %cross_mid.1.refs_6_ = f32[4,4,32,128]{3,2,1,0:T(8,128)S(1)} custom-call(f32[64,128]{1,0:T(8,128)S(1)} %gains.1.refs_0_, bf16[4,8,32,128]{3,2,1,0:T(8,128)(2,1)S(1)} %get-tuple-element.28.refs_1_.own_ref, bf16[4,8,32,128]{3,2,1,0:T(8,128)(2,1)S(1)} %collective-permute-done.1.refs_2_.own_ref, bf16[4,8,32,128]{3,2,1,0:T(8,128)(2,1)S(1)} %join.3.refs_3_, ...), custom_call_target="tpu_custom_call" | custom-call | flops 32999999488 | tf_op jit(solution)/shard_map/cross_mid/pallas_call | solution.py:312
  30.0 0.1 collective-permute-done.9.refs_5_
  30.1 0.0 collective-permute-done.8.refs_4_
  30.1 0.0 collective-permute-done.7.refs_3_
  30.1 0.7 %cross_next.1 = (f32[4,4,32,128]{3,2,1,0:T(8,128)S(1)}, f32[4,4,32,128]{3,2,1,0:T(8,128)S(1)}) custom-call(f32[64,128]{1,0:T(8,128)S(1)} %gains.1.refs_0_, bf16[4,8,32,128]{3,2,1,0:T(8,128)(2,1)S(1)} %get-tuple-element.28.refs_1_.own_ref, bf16[4,8,32,128]{3,2,1,0:T(8,128)(2,1)S(1)} %collective-permute-done.1.refs_2_.own_ref, ...), custom_call_target="tpu_custom_call" | custom-call | flops 660000000 | tf_op jit(solution)/shard_map/cross_next/pallas_call | solution.py:312
  30.8 0.3 collective-permute-done.6.refs_3_
  31.1 1.1 %cross_last.1 = f32[4,4,4,32,128]{4,3,2,1,0:T(8,128)} custom-call(f32[64,128]{1,0:T(8,128)S(1)} %gains.1.refs_0_, bf16[4,8,32,128]{3,2,1,0:T(8,128)(2,1)S(1)} %get-tuple-element.28.refs_1_.own_ref, bf16[4,8,32,128]{3,2,1,0:T(8,128)(2,1)S(1)} %collective-permute-done.1.refs_2_.own_ref, bf16[4,8,32,128]{3,2,1,0:T(8,128)(2,1)S(1)} %collective-permute-done.6.refs_3_, ...), custom_call_target="tpu_custom_call" | custom-call | flops 660000000 | tf_op jit(solution)/shard_map/cross_last/pallas_call | solution.py:312
  (7 shorter events, 0.1 us)
Async XLA Ops:
  0.0 1.2 %copy-start = (f32[4,8,8192]{2,1,0:T(8,128)S(1)}, f32[4,8,8192]{2,1,0:T(8,128)}, u32[]{:S(2)}) copy-start(f32[4,8,8192]{2,1,0:T(8,128)} %param.2) | copy-start | bytes 3145732
  4.2 9.3 %collective-permute-start.1 = (bf16[4,8,32,128]{3,2,1,0:T(8,128)(2,1)S(1)}, bf16[4,8,32,128]{3,2,1,0:T(8,128)(2,1)S(1)}, u32[]{:S(2)}, u32[]{:S(2)}) collective-permute-start(bf16[4,8,32,128]{3,2,1,0:T(8,128)(2,1)S(1)} %get-tuple-element.30), channel_id=1, source_target_pairs={{0,1},{1,0},{2,3},{3,2},{4,5},{5,4},{6,7},{7,6},{8,9},{9,8},{10,11... | collective-permute-start | bytes 786440 | tf_op jit(solution)/shard_map/ppermute | solution.py:382
  7.3 9.6 %collective-permute-start = (bf16[4,8,32,128]{3,2,1,0:T(8,128)(2,1)S(1)}, bf16[4,8,32,128]{3,2,1,0:T(8,128)(2,1)S(1)}, u32[]{:S(2)}, u32[]{:S(2)}) collective-permute-start(bf16[4,8,32,128]{3,2,1,0:T(8,128)(2,1)S(1)} %get-tuple-element.28.refs_1_.own_ref), channel_id=1, source_target_pairs={{8,0},{10,2},{12,4},{14,6},{16,8},{18,10},{20,12},{22,14},{24,16},... | collective-permute-start | bytes 786440 | tf_op jit(solution)/shard_map/ppermute | solution.py:383
  13.6 10.8 %collective-permute-start.2 = (bf16[4,8,32,128]{3,2,1,0:T(8,128)(2,1)S(1)}, bf16[4,8,32,128]{3,2,1,0:T(8,128)(2,1)S(1)}, u32[]{:S(2)}, u32[]{:S(2)}) collective-permute-start(bf16[4,8,32,128]{3,2,1,0:T(8,128)(2,1)S(1)} %collective-permute-done.1.refs_2_.own_ref), channel_id=1, source_target_pairs={{8,0},{10,2},{12,4},{14,6},{16,8},{18,10},{20,12},{22,14},{24,16},... | collective-permute-start | bytes 786440 | tf_op jit(solution)/shard_map/ppermute | solution.py:383
  17.0 2.9 %copy-start.1 = (s32[64]{0:T(128)S(1)}, s32[64]{0:T(128)}, u32[]{:S(2)}) copy-start(s32[64]{0:T(128)} %pos_ref) | copy-start | bytes 772
  17.0 10.1 %collective-permute-start.5 = (bf16[4,8,32,128]{3,2,1,0:T(8,128)(2,1)S(1)}, bf16[4,8,32,128]{3,2,1,0:T(8,128)(2,1)S(1)}, u32[]{:S(2)}, u32[]{:S(2)}) collective-permute-start(bf16[4,8,32,128]{3,2,1,0:T(8,128)(2,1)S(1)} %choose.5), channel_id=1, source_target_pairs={{0,4},{2,6},{4,0},{6,2},{8,12},{10,14},{12,8},{14,10},{16,20},{18,... | collective-permute-start | bytes 786440 | tf_op jit(solution)/shard_map/ppermute | solution.py:398
  18.5 9.6 %collective-permute-start.4 = (bf16[2,8,32,128]{3,2,1,0:T(8,128)(2,1)S(1)}, bf16[2,8,32,128]{3,2,1,0:T(8,128)(2,1)S(1)}, u32[]{:S(2)}, u32[]{:S(2)}) collective-permute-start(bf16[2,8,32,128]{3,2,1,0:T(8,128)(2,1)S(1)} %slice.4), channel_id=1, source_target_pairs={{4,0},{6,2},{8,4},{10,6},{12,8},{14,10},{16,12},{18,14},{20,16},{2... | collective-permute-start | bytes 393224 | tf_op jit(solution)/shard_map/ppermute | solution.py:395
  24.4 5.1 %collective-permute-start.3 = (bf16[2,8,32,128]{3,2,1,0:T(8,128)(2,1)S(1)}, bf16[2,8,32,128]{3,2,1,0:T(8,128)(2,1)S(1)}, u32[]{:S(2)}, u32[]{:S(2)}) collective-permute-start(bf16[2,8,32,128]{3,2,1,0:T(8,128)(2,1)S(1)} %choose.4), channel_id=1, source_target_pairs={{0,4},{2,6},{4,0},{6,2},{8,12},{10,14},{12,8},{14,10},{16,20},{18,... | collective-permute-start | bytes 393224 | tf_op jit(solution)/shard_map/ppermute | solution.py:398
  24.5 5.6 %collective-permute-start.7 = (bf16[4,8,32,128]{3,2,1,0:T(8,128)(2,1)S(1)}, bf16[4,8,32,128]{3,2,1,0:T(8,128)(2,1)S(1)}, u32[]{:S(2)}, u32[]{:S(2)}) collective-permute-start(bf16[4,8,32,128]{3,2,1,0:T(8,128)(2,1)S(1)} %choose.6), channel_id=1, source_target_pairs={{0,2},{2,0},{4,6},{6,4},{8,10},{10,8},{12,14},{14,12},{16,18},{18,... | collective-permute-start | bytes 786440 | tf_op jit(solution)/shard_map/ppermute | solution.py:399
  28.1 2.0 %collective-permute-start.8 = (bf16[4,8,32,128]{3,2,1,0:T(8,128)(2,1)S(1)}, bf16[4,8,32,128]{3,2,1,0:T(8,128)(2,1)S(1)}, u32[]{:S(2)}, u32[]{:S(2)}) collective-permute-start(bf16[4,8,32,128]{3,2,1,0:T(8,128)(2,1)S(1)} %choose.7), channel_id=1, source_target_pairs={{0,2},{2,0},{4,6},{6,4},{8,10},{10,8},{12,14},{14,12},{16,18},{18,... | collective-permute-start | bytes 786440 | tf_op jit(solution)/shard_map/ppermute | solution.py:399
  28.2 1.9 %collective-permute-start.9 = (bf16[4,8,32,128]{3,2,1,0:T(8,128)(2,1)S(1)}, bf16[4,8,32,128]{3,2,1,0:T(8,128)(2,1)S(1)}, u32[]{:S(2)}, u32[]{:S(2)}) collective-permute-start(bf16[4,8,32,128]{3,2,1,0:T(8,128)(2,1)S(1)} %collective-permute-done.5.refs_4_), channel_id=1, source_target_pairs={{0,2},{2,0},{4,6},{6,4},{8,10},{10,8},{12,14},{14,12},{16,18},{18,... | collective-permute-start | bytes 786440 | tf_op jit(solution)/shard_map/ppermute | solution.py:401
  29.5 1.6 %collective-permute-start.6 = (bf16[4,8,32,128]{3,2,1,0:T(8,128)(2,1)S(1)}, bf16[4,8,32,128]{3,2,1,0:T(8,128)(2,1)S(1)}, u32[]{:S(2)}, u32[]{:S(2)}) collective-permute-start(bf16[4,8,32,128]{3,2,1,0:T(8,128)(2,1)S(1)} %join.3.refs_3_), channel_id=1, source_target_pairs={{0,2},{2,0},{4,6},{6,4},{8,10},{10,8},{12,14},{14,12},{16,18},{18,... | collective-permute-start | bytes 786440 | tf_op jit(solution)/shard_map/ppermute | solution.py:413

commit v7 on v6

--- a/solution.py
+++ b/solution.py
@@ -391,7 +391,7 @@
     )
     far[last] = after(far[last], acc_far)
     mid, one, two = [], [], []
-    half = chans // 2
+    half = chans - chans // 4
     direct = lax.ppermute(mine[last][half:], "chan", [(b, b - 2) for b in range(2, blocks)])
     for s in range(parts):
         count = None if s < last else half

time: 32.4 us -> 34.6 us (1.068)
  starting transfers between devices: 9.24 us -> 10.8 us
  waiting for transfers between devices: 14.8 us -> 15.4 us
    ppermute x1, waiting for transfers between devices: 0.44 us -> 4.13 us  [shards(): lax.ppermute(mine[last][half:], 'chan', [(b, b - 2) for b in range(2, blo...]
    ppermute x2, waiting for transfers between devices: 3.28 us -> 0.01 us  [shards(): mid.append(lax.ppermute(choose(2, mine[s], far[s], count), 'chan', swap2))]
    ppermute x2, starting transfers between devices: 1.64 us -> 3.02 us  [shards(): mid.append(lax.ppermute(choose(2, mine[s], far[s], count), 'chan', swap2))]
    ppermute x1, waiting for transfers between devices: 0.12 us -> 0.85 us  [shards(): two.append(lax.ppermute(mid[s], 'chan', swap1))]
  transfers between devices with their start and end apart: 10 -> 10, of which waited for: 8 -> 5; matrix products, arithmetic and copies ran while one was open for 0% -> 0% of each run, Pallas kernels for 8% -> 8%
where the time goes in v7:
time: 34.6 us; the launch traced here: 34.4 us
  waiting for transfers between devices  15.4 us (45%)
  starting transfers between devices  10.8 us (31%)
  Pallas kernels  7.11 us (21%)
  local copies, waits for them, and re-layouts  0.93 us (3%)
    ppermute x2, waiting for transfers between devices, shards(): far = [lax.ppermute(own, 'chan', up) for own in mine]  5.55 us
    ppermute x1, waiting for transfers between devices, shards(): lax.ppermute(spectra[s], 'win', [(i, (i + s) % parts) for i in range(part...  4.89 us
    ppermute x1, waiting for transfers between devices, shards(): lax.ppermute(mine[last][half:], 'chan', [(b, b - 2) for b in range(2, blo...  4.13 us
    ppermute x1, starting transfers between devices, shards(): lax.ppermute(spectra[s], 'win', [(i, (i + s) % parts) for i in range(part...  3.03 us
    ppermute x2, starting transfers between devices, shards(): mid.append(lax.ppermute(choose(2, mine[s], far[s], count), 'chan', swap2))  3.02 us
    pallas_call x5, Pallas kernels, cross_call(): pl.pallas_call(functools.partial(cross_kernel, layout, jobs), in_specs=[V...  3.02 us
    pallas_call x1, Pallas kernels, whitened_spectra(): pl.pallas_call(functools.partial(spectra_kernel, parts), in_specs=[VMEM]...  3.01 us
    ppermute x2, starting transfers between devices, shards(): far = [lax.ppermute(own, 'chan', up) for own in mine]  2.69 us
  transfers between devices with their start and end apart: 10, of which 5 were waited for; matrix products, arithmetic and copies ran while one was open for 0% of the time, Pallas kernels for 8%

profile of v7, /device:TPU:0, one launch (start us, length us, event | category | flops | bytes accessed | tf_op | source)
XLA Modules:
  0.0 34.4 jit_solution(124099125392164097)
XLA Ops:
  0.0 0.0 copy-start
  0.0 0.3 tables.1
  0.3 0.9 %copy-done = f32[4,8,8192]{2,1,0:T(8,128)S(1)} copy-done((f32[4,8,8192]{2,1,0:T(8,128)S(1)}, f32[4,8,8192]{2,1,0:T(8,128)}, u32[]{:S(2)}) %copy-start) | copy-done | bytes 1048600
  1.2 3.0 %spectra.1 = (bf16[4,8,32,128]{3,2,1,0:T(8,128)(2,1)S(1)}, bf16[4,8,32,128]{3,2,1,0:T(8,128)(2,1)S(1)}) custom-call(f32[4,64,8,128]{3,2,1,0:T(8,128)S(1)} %bitcast.8, f32[2,64,128]{2,1,0:T(8,128)S(1)} %get-tuple-element.23.refs_0_, bf16[512,256]{1,0:T(8,128)(2,1)S(1)} %get-tuple-element.24.refs_1_, bf16[512,128]{1,0:T(8,128)(2,1)S(1)} %get-tuple-element.25.refs_2_, ...), custom_call_target="tpu_custom_call" | custom-call | flops 4400000000 | tf_op jit(solution)/shard_map/spectra/pallas_call | solution.py:206
  4.2 3.0 %collective-permute-start.1 = (bf16[4,8,32,128]{3,2,1,0:T(8,128)(2,1)S(1)}, bf16[4,8,32,128]{3,2,1,0:T(8,128)(2,1)S(1)}, u32[]{:S(2)}, u32[]{:S(2)}) collective-permute-start(bf16[4,8,32,128]{3,2,1,0:T(8,128)(2,1)S(1)} %get-tuple-element.30), channel_id=1, source_target_pairs={{0,1},{1,0},{2,3},{3,2},{4,5},{5,4},{6,7},{7,6},{8,9},{9,8},{10,11... | collective-permute-start | bytes 786440 | tf_op jit(solution)/shard_map/ppermute | solution.py:382
  7.3 0.0 copy-start.1
  7.3 1.4 %collective-permute-start = (bf16[4,8,32,128]{3,2,1,0:T(8,128)(2,1)S(1)}, bf16[4,8,32,128]{3,2,1,0:T(8,128)(2,1)S(1)}, u32[]{:S(2)}, u32[]{:S(2)}) collective-permute-start(bf16[4,8,32,128]{3,2,1,0:T(8,128)(2,1)S(1)} %get-tuple-element.28.refs_1_.own_ref), channel_id=1, source_target_pairs={{8,0},{10,2},{12,4},{14,6},{16,8},{18,10},{20,12},{22,14},{24,16},... | collective-permute-start | bytes 786440 | tf_op jit(solution)/shard_map/ppermute | solution.py:383
  8.7 4.9 %collective-permute-done.1.refs_2_.own_ref = bf16[4,8,32,128]{3,2,1,0:T(8,128)(2,1)S(1)} collective-permute-done((bf16[4,8,32,128]{3,2,1,0:T(8,128)(2,1)S(1)}, bf16[4,8,32,128]{3,2,1,0:T(8,128)(2,1)S(1)}, u32[]{:S(2)}, u32[]{:S(2)}) %collective-permute-start.1) | collective-permute-done | bytes 262176 | tf_op jit(solution)/shard_map/ppermute | solution.py:382
  13.6 1.3 %collective-permute-start.2 = (bf16[4,8,32,128]{3,2,1,0:T(8,128)(2,1)S(1)}, bf16[4,8,32,128]{3,2,1,0:T(8,128)(2,1)S(1)}, u32[]{:S(2)}, u32[]{:S(2)}) collective-permute-start(bf16[4,8,32,128]{3,2,1,0:T(8,128)(2,1)S(1)} %collective-permute-done.1.refs_2_.own_ref), channel_id=1, source_target_pairs={{8,0},{10,2},{12,4},{14,6},{16,8},{18,10},{20,12},{22,14},{24,16},... | collective-permute-start | bytes 786440 | tf_op jit(solution)/shard_map/ppermute | solution.py:383
  14.9 2.2 %collective-permute-done.refs_3_.far_ref = bf16[4,8,32,128]{3,2,1,0:T(8,128)(2,1)S(1)} collective-permute-done((bf16[4,8,32,128]{3,2,1,0:T(8,128)(2,1)S(1)}, bf16[4,8,32,128]{3,2,1,0:T(8,128)(2,1)S(1)}, u32[]{:S(2)}, u32[]{:S(2)}) %collective-permute-start) | collective-permute-done | bytes 262176 | tf_op jit(solution)/shard_map/ppermute | solution.py:383
  17.1 1.6 %collective-permute-start.5 = (bf16[4,8,32,128]{3,2,1,0:T(8,128)(2,1)S(1)}, bf16[4,8,32,128]{3,2,1,0:T(8,128)(2,1)S(1)}, u32[]{:S(2)}, u32[]{:S(2)}) collective-permute-start(bf16[4,8,32,128]{3,2,1,0:T(8,128)(2,1)S(1)} %choose.5), channel_id=1, source_target_pairs={{0,4},{2,6},{4,0},{6,2},{8,12},{10,14},{12,8},{14,10},{16,20},{18,... | collective-permute-start | bytes 786440 | tf_op jit(solution)/shard_map/ppermute | solution.py:398
  18.7 0.0 copy-done.1
  18.7 0.7 %gains.1.refs_0_ = f32[64,128]{1,0:T(8,128)S(1)} custom-call(s32[64]{0:T(128)S(1)} %copy-done.1), custom_call_target="tpu_custom_call" | custom-call | flops 550000000 | tf_op jit(solution)/shard_map/gains/pallas_call | solution.py:142
  19.3 0.2 cross_far.1.refs_5_
  19.6 3.4 %collective-permute-done.2.far_ref.refs_3_ = bf16[4,8,32,128]{3,2,1,0:T(8,128)(2,1)S(1)} collective-permute-done((bf16[4,8,32,128]{3,2,1,0:T(8,128)(2,1)S(1)}, bf16[4,8,32,128]{3,2,1,0:T(8,128)(2,1)S(1)}, u32[]{:S(2)}, u32[]{:S(2)}) %collective-permute-start.2) | collective-permute-done | bytes 262176 | tf_op jit(solution)/shard_map/ppermute | solution.py:383
  23.0 1.5 %collective-permute-start.3 = (bf16[3,8,32,128]{3,2,1,0:T(8,128)(2,1)S(1)}, bf16[3,8,32,128]{3,2,1,0:T(8,128)(2,1)S(1)}, u32[]{:S(2)}, u32[]{:S(2)}) collective-permute-start(bf16[3,8,32,128]{3,2,1,0:T(8,128)(2,1)S(1)} %choose.4), channel_id=1, source_target_pairs={{0,4},{2,6},{4,0},{6,2},{8,12},{10,14},{12,8},{14,10},{16,20},{18,... | collective-permute-start | bytes 589832 | tf_op jit(solution)/shard_map/ppermute | solution.py:398
  24.4 1.3 %collective-permute-start.4 = (bf16[1,8,32,128]{3,2,1,0:T(8,128)(2,1)S(1)}, bf16[1,8,32,128]{3,2,1,0:T(8,128)(2,1)S(1)}, u32[]{:S(2)}, u32[]{:S(2)}) collective-permute-start(bf16[1,8,32,128]{3,2,1,0:T(8,128)(2,1)S(1)} %slice.4), channel_id=1, source_target_pairs={{4,0},{6,2},{8,4},{10,6},{12,8},{14,10},{16,12},{18,14},{20,16},{2... | collective-permute-start | bytes 196616 | tf_op jit(solution)/shard_map/ppermute | solution.py:395
  25.8 0.1 collective-permute-start.7
  25.8 0.0 collective-permute-done.5.refs_4_
  25.9 0.6 %cross_most.1 = (f32[4,4,32,128]{3,2,1,0:T(8,128)S(1)}, f32[4,4,32,128]{3,2,1,0:T(8,128)S(1)}) custom-call(f32[64,128]{1,0:T(8,128)S(1)} %gains.1.refs_0_, bf16[4,8,32,128]{3,2,1,0:T(8,128)(2,1)S(1)} %get-tuple-element.28.refs_1_.own_ref, bf16[4,8,32,128]{3,2,1,0:T(8,128)(2,1)S(1)} %collective-permute-done.1.refs_2_.own_ref, ...), custom_call_target="tpu_custom_call" | custom-call | flops 660000000 | tf_op jit(solution)/shard_map/cross_most/pallas_call | solution.py:312
  26.5 4.1 %collective-permute-done.4.refs_0_ = bf16[1,8,32,128]{3,2,1,0:T(8,128)(2,1)S(1)} collective-permute-done((bf16[1,8,32,128]{3,2,1,0:T(8,128)(2,1)S(1)}, bf16[1,8,32,128]{3,2,1,0:T(8,128)(2,1)S(1)}, u32[]{:S(2)}, u32[]{:S(2)}) %collective-permute-start.4) | collective-permute-done | bytes 65568 | tf_op jit(solution)/shard_map/ppermute | solution.py:395
  30.6 0.1 collective-permute-start.8
  30.7 0.5 %collective-permute-start.9 = (bf16[4,8,32,128]{3,2,1,0:T(8,128)(2,1)S(1)}, bf16[4,8,32,128]{3,2,1,0:T(8,128)(2,1)S(1)}, u32[]{:S(2)}, u32[]{:S(2)}) collective-permute-start(bf16[4,8,32,128]{3,2,1,0:T(8,128)(2,1)S(1)} %collective-permute-done.5.refs_4_), channel_id=1, source_target_pairs={{0,2},{2,0},{4,6},{6,4},{8,10},{10,8},{12,14},{14,12},{16,18},{18,... | collective-permute-start | bytes 786440 | tf_op jit(solution)/shard_map/ppermute | solution.py:401
  31.2 0.0 collective-permute-done.3.refs_0_
  31.2 0.1 collective-permute-start.6
  31.4 0.4 %cross_mid.1.refs_6_ = f32[4,4,32,128]{3,2,1,0:T(8,128)S(1)} custom-call(f32[64,128]{1,0:T(8,128)S(1)} %gains.1.refs_0_, bf16[4,8,32,128]{3,2,1,0:T(8,128)(2,1)S(1)} %get-tuple-element.28.refs_1_.own_ref, bf16[4,8,32,128]{3,2,1,0:T(8,128)(2,1)S(1)} %collective-permute-done.1.refs_2_.own_ref, bf16[4,8,32,128]{3,2,1,0:T(8,128)(2,1)S(1)} %join.3.refs_3_, ...), custom_call_target="tpu_custom_call" | custom-call | flops 32999999488 | tf_op jit(solution)/shard_map/cross_mid/pallas_call | solution.py:312
  31.7 0.8 %collective-permute-done.9.refs_5_ = bf16[4,8,32,128]{3,2,1,0:T(8,128)(2,1)S(1)} collective-permute-done((bf16[4,8,32,128]{3,2,1,0:T(8,128)(2,1)S(1)}, bf16[4,8,32,128]{3,2,1,0:T(8,128)(2,1)S(1)}, u32[]{:S(2)}, u32[]{:S(2)}) %collective-permute-start.9) | collective-permute-done | bytes 262176 | tf_op jit(solution)/shard_map/ppermute | solution.py:401
  32.6 0.0 collective-permute-done.8.refs_4_
  32.6 0.0 collective-permute-done.7.refs_3_
  32.6 0.7 %cross_next.1 = (f32[4,4,32,128]{3,2,1,0:T(8,128)S(1)}, f32[4,4,32,128]{3,2,1,0:T(8,128)S(1)}) custom-call(f32[64,128]{1,0:T(8,128)S(1)} %gains.1.refs_0_, bf16[4,8,32,128]{3,2,1,0:T(8,128)(2,1)S(1)} %get-tuple-element.28.refs_1_.own_ref, bf16[4,8,32,128]{3,2,1,0:T(8,128)(2,1)S(1)} %collective-permute-done.1.refs_2_.own_ref, ...), custom_call_target="tpu_custom_call" | custom-call | flops 660000000 | tf_op jit(solution)/shard_map/cross_next/pallas_call | solution.py:312
  33.3 0.0 collective-permute-done.6.refs_3_
  33.3 1.1 %cross_last.1 = f32[4,4,4,32,128]{4,3,2,1,0:T(8,128)} custom-call(f32[64,128]{1,0:T(8,128)S(1)} %gains.1.refs_0_, bf16[4,8,32,128]{3,2,1,0:T(8,128)(2,1)S(1)} %get-tuple-element.28.refs_1_.own_ref, bf16[4,8,32,128]{3,2,1,0:T(8,128)(2,1)S(1)} %collective-permute-done.1.refs_2_.own_ref, bf16[4,8,32,128]{3,2,1,0:T(8,128)(2,1)S(1)} %collective-permute-done.6.refs_3_, ...), custom_call_target="tpu_custom_call" | custom-call | flops 660000000 | tf_op jit(solution)/shard_map/cross_last/pallas_call | solution.py:312
  (7 shorter events, 0.1 us)
Async XLA Ops:
  0.0 1.2 %copy-start = (f32[4,8,8192]{2,1,0:T(8,128)S(1)}, f32[4,8,8192]{2,1,0:T(8,128)}, u32[]{:S(2)}) copy-start(f32[4,8,8192]{2,1,0:T(8,128)} %param.2) | copy-start | bytes 3145732
  4.2 9.3 %collective-permute-start.1 = (bf16[4,8,32,128]{3,2,1,0:T(8,128)(2,1)S(1)}, bf16[4,8,32,128]{3,2,1,0:T(8,128)(2,1)S(1)}, u32[]{:S(2)}, u32[]{:S(2)}) collective-permute-start(bf16[4,8,32,128]{3,2,1,0:T(8,128)(2,1)S(1)} %get-tuple-element.30), channel_id=1, source_target_pairs={{0,1},{1,0},{2,3},{3,2},{4,5},{5,4},{6,7},{7,6},{8,9},{9,8},{10,11... | collective-permute-start | bytes 786440 | tf_op jit(solution)/shard_map/ppermute | solution.py:382
  7.3 11.4 %copy-start.1 = (s32[64]{0:T(128)S(1)}, s32[64]{0:T(128)}, u32[]{:S(2)}) copy-start(s32[64]{0:T(128)} %pos_ref) | copy-start | bytes 772
  7.3 9.8 %collective-permute-start = (bf16[4,8,32,128]{3,2,1,0:T(8,128)(2,1)S(1)}, bf16[4,8,32,128]{3,2,1,0:T(8,128)(2,1)S(1)}, u32[]{:S(2)}, u32[]{:S(2)}) collective-permute-start(bf16[4,8,32,128]{3,2,1,0:T(8,128)(2,1)S(1)} %get-tuple-element.28.refs_1_.own_ref), channel_id=1, source_target_pairs={{8,0},{10,2},{12,4},{14,6},{16,8},{18,10},{20,12},{22,14},{24,16},... | collective-permute-start | bytes 786440 | tf_op jit(solution)/shard_map/ppermute | solution.py:383
  13.6 9.4 %collective-permute-start.2 = (bf16[4,8,32,128]{3,2,1,0:T(8,128)(2,1)S(1)}, bf16[4,8,32,128]{3,2,1,0:T(8,128)(2,1)S(1)}, u32[]{:S(2)}, u32[]{:S(2)}) collective-permute-start(bf16[4,8,32,128]{3,2,1,0:T(8,128)(2,1)S(1)} %collective-permute-done.1.refs_2_.own_ref), channel_id=1, source_target_pairs={{8,0},{10,2},{12,4},{14,6},{16,8},{18,10},{20,12},{22,14},{24,16},... | collective-permute-start | bytes 786440 | tf_op jit(solution)/shard_map/ppermute | solution.py:383
  17.1 8.8 %collective-permute-start.5 = (bf16[4,8,32,128]{3,2,1,0:T(8,128)(2,1)S(1)}, bf16[4,8,32,128]{3,2,1,0:T(8,128)(2,1)S(1)}, u32[]{:S(2)}, u32[]{:S(2)}) collective-permute-start(bf16[4,8,32,128]{3,2,1,0:T(8,128)(2,1)S(1)} %choose.5), channel_id=1, source_target_pairs={{0,4},{2,6},{4,0},{6,2},{8,12},{10,14},{12,8},{14,10},{16,20},{18,... | collective-permute-start | bytes 786440 | tf_op jit(solution)/shard_map/ppermute | solution.py:398
  23.0 8.2 %collective-permute-start.3 = (bf16[3,8,32,128]{3,2,1,0:T(8,128)(2,1)S(1)}, bf16[3,8,32,128]{3,2,1,0:T(8,128)(2,1)S(1)}, u32[]{:S(2)}, u32[]{:S(2)}) collective-permute-start(bf16[3,8,32,128]{3,2,1,0:T(8,128)(2,1)S(1)} %choose.4), channel_id=1, source_target_pairs={{0,4},{2,6},{4,0},{6,2},{8,12},{10,14},{12,8},{14,10},{16,20},{18,... | collective-permute-start | bytes 589832 | tf_op jit(solution)/shard_map/ppermute | solution.py:398
  24.4 6.1 %collective-permute-start.4 = (bf16[1,8,32,128]{3,2,1,0:T(8,128)(2,1)S(1)}, bf16[1,8,32,128]{3,2,1,0:T(8,128)(2,1)S(1)}, u32[]{:S(2)}, u32[]{:S(2)}) collective-permute-start(bf16[1,8,32,128]{3,2,1,0:T(8,128)(2,1)S(1)} %slice.4), channel_id=1, source_target_pairs={{4,0},{6,2},{8,4},{10,6},{12,8},{14,10},{16,12},{18,14},{20,16},{2... | collective-permute-start | bytes 196616 | tf_op jit(solution)/shard_map/ppermute | solution.py:395
  25.8 6.8 %collective-permute-start.7 = (bf16[4,8,32,128]{3,2,1,0:T(8,128)(2,1)S(1)}, bf16[4,8,32,128]{3,2,1,0:T(8,128)(2,1)S(1)}, u32[]{:S(2)}, u32[]{:S(2)}) collective-permute-start(bf16[4,8,32,128]{3,2,1,0:T(8,128)(2,1)S(1)} %choose.6), channel_id=1, source_target_pairs={{0,2},{2,0},{4,6},{6,4},{8,10},{10,8},{12,14},{14,12},{16,18},{18,... | collective-permute-start | bytes 786440 | tf_op jit(solution)/shard_map/ppermute | solution.py:399
  30.6 2.0 %collective-permute-start.8 = (bf16[4,8,32,128]{3,2,1,0:T(8,128)(2,1)S(1)}, bf16[4,8,32,128]{3,2,1,0:T(8,128)(2,1)S(1)}, u32[]{:S(2)}, u32[]{:S(2)}) collective-permute-start(bf16[4,8,32,128]{3,2,1,0:T(8,128)(2,1)S(1)} %choose.7), channel_id=1, source_target_pairs={{0,2},{2,0},{4,6},{6,4},{8,10},{10,8},{12,14},{14,12},{16,18},{18,... | collective-permute-start | bytes 786440 | tf_op jit(solution)/shard_map/ppermute | solution.py:399
  30.7 1.9 %collective-permute-start.9 = (bf16[4,8,32,128]{3,2,1,0:T(8,128)(2,1)S(1)}, bf16[4,8,32,128]{3,2,1,0:T(8,128)(2,1)S(1)}, u32[]{:S(2)}, u32[]{:S(2)}) collective-permute-start(bf16[4,8,32,128]{3,2,1,0:T(8,128)(2,1)S(1)} %collective-permute-done.5.refs_4_), channel_id=1, source_target_pairs={{0,2},{2,0},{4,6},{6,4},{8,10},{10,8},{12,14},{14,12},{16,18},{18,... | collective-permute-start | bytes 786440 | tf_op jit(solution)/shard_map/ppermute | solution.py:401
  31.2 2.1 %collective-permute-start.6 = (bf16[4,8,32,128]{3,2,1,0:T(8,128)(2,1)S(1)}, bf16[4,8,32,128]{3,2,1,0:T(8,128)(2,1)S(1)}, u32[]{:S(2)}, u32[]{:S(2)}) collective-permute-start(bf16[4,8,32,128]{3,2,1,0:T(8,128)(2,1)S(1)} %join.3.refs_3_), channel_id=1, source_target_pairs={{0,2},{2,0},{4,6},{6,4},{8,10},{10,8},{12,14},{14,12},{16,18},{18,... | collective-permute-start | bytes 786440 | tf_op jit(solution)/shard_map/ppermute | solution.py:413

commit v8 on v6

--- a/solution.py
+++ b/solution.py
@@ -408,7 +408,7 @@
         sources={"far": far[last:], "mid": mid[:last]},
         acc_in=[acc_far],
     )
-    direct = join(0.1, after(direct, acc_mid))
+    direct = join(5.0, after(direct, acc_mid))
     mid[last] = join(0.1, after(mid[last], direct), direct)
     two.append(lax.ppermute(mid[last], "chan", swap1))
     (done_mid,) = call(

time: 32.4 us -> 32.4 us (level)
    ppermute x1, waiting for transfers between devices: 0.44 us -> 1 us  [shards(): lax.ppermute(mine[last][half:], 'chan', [(b, b - 2) for b in range(2, blo...]
    ppermute x2, waiting for transfers between devices: 3.28 us -> 2.8 us  [shards(): mid.append(lax.ppermute(choose(2, mine[s], far[s], count), 'chan', swap2))]
  transfers between devices with their start and end apart: 10 -> 10, of which waited for: 8 -> 8; matrix products, arithmetic and copies ran while one was open for 0% -> 0% of each run, Pallas kernels for 8% -> 9%
where the time goes in v8:
time: 32.4 us; the launch traced here: 32.2 us
  waiting for transfers between devices  14.7 us (45%)
  starting transfers between devices  9.24 us (29%)
  Pallas kernels  7.13 us (22%)
  local copies, waits for them, and re-layouts  0.94 us (3%)
    ppermute x2, waiting for transfers between devices, shards(): far = [lax.ppermute(own, 'chan', up) for own in mine]  5.5 us
    ppermute x1, waiting for transfers between devices, shards(): lax.ppermute(spectra[s], 'win', [(i, (i + s) % parts) for i in range(part...  5.02 us
    ppermute x1, starting transfers between devices, shards(): lax.ppermute(spectra[s], 'win', [(i, (i + s) % parts) for i in range(part...  3.03 us
    pallas_call x1, Pallas kernels, whitened_spectra(): pl.pallas_call(functools.partial(spectra_kernel, parts), in_specs=[VMEM]...  3.01 us
    pallas_call x5, Pallas kernels, cross_call(): pl.pallas_call(functools.partial(cross_kernel, layout, jobs), in_specs=[V...  3.01 us
    ppermute x2, waiting for transfers between devices, shards(): mid.append(lax.ppermute(choose(2, mine[s], far[s], count), 'chan', swap2))  2.8 us
    ppermute x2, starting transfers between devices, shards(): far = [lax.ppermute(own, 'chan', up) for own in mine]  2.56 us
    ppermute x2, starting transfers between devices, shards(): mid.append(lax.ppermute(choose(2, mine[s], far[s], count), 'chan', swap2))  1.64 us
  transfers between devices with their start and end apart: 10, of which 8 were waited for; matrix products, arithmetic and copies ran while one was open for 0% of the time, Pallas kernels for 9%

profile of v8, /device:TPU:0, one launch (start us, length us, event | category | flops | bytes accessed | tf_op | source)
XLA Modules:
  0.0 32.2 jit_solution(5071872463895356068)
XLA Ops:
  0.0 0.0 copy-start
  0.0 0.3 tables.1
  0.3 0.9 %copy-done = f32[4,8,8192]{2,1,0:T(8,128)S(1)} copy-done((f32[4,8,8192]{2,1,0:T(8,128)S(1)}, f32[4,8,8192]{2,1,0:T(8,128)}, u32[]{:S(2)}) %copy-start) | copy-done | bytes 1048600
  1.2 3.0 %spectra.1 = (bf16[4,8,32,128]{3,2,1,0:T(8,128)(2,1)S(1)}, bf16[4,8,32,128]{3,2,1,0:T(8,128)(2,1)S(1)}) custom-call(f32[4,64,8,128]{3,2,1,0:T(8,128)S(1)} %bitcast.8, f32[2,64,128]{2,1,0:T(8,128)S(1)} %get-tuple-element.23.refs_0_, bf16[512,256]{1,0:T(8,128)(2,1)S(1)} %get-tuple-element.24.refs_1_, bf16[512,128]{1,0:T(8,128)(2,1)S(1)} %get-tuple-element.25.refs_2_, ...), custom_call_target="tpu_custom_call" | custom-call | flops 4400000000 | tf_op jit(solution)/shard_map/spectra/pallas_call | solution.py:206
  4.2 3.0 %collective-permute-start.1 = (bf16[4,8,32,128]{3,2,1,0:T(8,128)(2,1)S(1)}, bf16[4,8,32,128]{3,2,1,0:T(8,128)(2,1)S(1)}, u32[]{:S(2)}, u32[]{:S(2)}) collective-permute-start(bf16[4,8,32,128]{3,2,1,0:T(8,128)(2,1)S(1)} %get-tuple-element.30), channel_id=1, source_target_pairs={{0,1},{1,0},{2,3},{3,2},{4,5},{5,4},{6,7},{7,6},{8,9},{9,8},{10,11... | collective-permute-start | bytes 786440 | tf_op jit(solution)/shard_map/ppermute | solution.py:382
  7.3 1.3 %collective-permute-start = (bf16[4,8,32,128]{3,2,1,0:T(8,128)(2,1)S(1)}, bf16[4,8,32,128]{3,2,1,0:T(8,128)(2,1)S(1)}, u32[]{:S(2)}, u32[]{:S(2)}) collective-permute-start(bf16[4,8,32,128]{3,2,1,0:T(8,128)(2,1)S(1)} %get-tuple-element.28.refs_1_.own_ref), channel_id=1, source_target_pairs={{8,0},{10,2},{12,4},{14,6},{16,8},{18,10},{20,12},{22,14},{24,16},... | collective-permute-start | bytes 786440 | tf_op jit(solution)/shard_map/ppermute | solution.py:383
  8.6 5.0 %collective-permute-done.1.refs_2_.own_ref = bf16[4,8,32,128]{3,2,1,0:T(8,128)(2,1)S(1)} collective-permute-done((bf16[4,8,32,128]{3,2,1,0:T(8,128)(2,1)S(1)}, bf16[4,8,32,128]{3,2,1,0:T(8,128)(2,1)S(1)}, u32[]{:S(2)}, u32[]{:S(2)}) %collective-permute-start.1) | collective-permute-done | bytes 262176 | tf_op jit(solution)/shard_map/ppermute | solution.py:382
  13.6 1.3 %collective-permute-start.2 = (bf16[4,8,32,128]{3,2,1,0:T(8,128)(2,1)S(1)}, bf16[4,8,32,128]{3,2,1,0:T(8,128)(2,1)S(1)}, u32[]{:S(2)}, u32[]{:S(2)}) collective-permute-start(bf16[4,8,32,128]{3,2,1,0:T(8,128)(2,1)S(1)} %collective-permute-done.1.refs_2_.own_ref), channel_id=1, source_target_pairs={{8,0},{10,2},{12,4},{14,6},{16,8},{18,10},{20,12},{22,14},{24,16},... | collective-permute-start | bytes 786440 | tf_op jit(solution)/shard_map/ppermute | solution.py:383
  14.9 2.1 %collective-permute-done.refs_3_.far_ref = bf16[4,8,32,128]{3,2,1,0:T(8,128)(2,1)S(1)} collective-permute-done((bf16[4,8,32,128]{3,2,1,0:T(8,128)(2,1)S(1)}, bf16[4,8,32,128]{3,2,1,0:T(8,128)(2,1)S(1)}, u32[]{:S(2)}, u32[]{:S(2)}) %collective-permute-start) | collective-permute-done | bytes 262176 | tf_op jit(solution)/shard_map/ppermute | solution.py:383
  17.0 1.6 %collective-permute-start.5 = (bf16[4,8,32,128]{3,2,1,0:T(8,128)(2,1)S(1)}, bf16[4,8,32,128]{3,2,1,0:T(8,128)(2,1)S(1)}, u32[]{:S(2)}, u32[]{:S(2)}) collective-permute-start(bf16[4,8,32,128]{3,2,1,0:T(8,128)(2,1)S(1)} %choose.5), channel_id=1, source_target_pairs={{0,4},{2,6},{4,0},{6,2},{8,12},{10,14},{12,8},{14,10},{16,20},{18,... | collective-permute-start | bytes 786440 | tf_op jit(solution)/shard_map/ppermute | solution.py:398
  18.5 0.0 copy-start.1
  18.5 1.3 %collective-permute-start.4 = (bf16[2,8,32,128]{3,2,1,0:T(8,128)(2,1)S(1)}, bf16[2,8,32,128]{3,2,1,0:T(8,128)(2,1)S(1)}, u32[]{:S(2)}, u32[]{:S(2)}) collective-permute-start(bf16[2,8,32,128]{3,2,1,0:T(8,128)(2,1)S(1)} %slice.4), channel_id=1, source_target_pairs={{4,0},{6,2},{8,4},{10,6},{12,8},{14,10},{16,12},{18,14},{20,16},{2... | collective-permute-start | bytes 393224 | tf_op jit(solution)/shard_map/ppermute | solution.py:395
  19.9 0.1 collective-permute-start.7
  20.0 0.0 copy-done.1
  20.0 0.7 %gains.1.refs_0_ = f32[64,128]{1,0:T(8,128)S(1)} custom-call(s32[64]{0:T(128)S(1)} %copy-done.1), custom_call_target="tpu_custom_call" | custom-call | flops 550000000 | tf_op jit(solution)/shard_map/gains/pallas_call | solution.py:142
  20.7 0.2 cross_far.1.refs_5_
  20.9 3.4 %collective-permute-done.2.far_ref.refs_3_ = bf16[4,8,32,128]{3,2,1,0:T(8,128)(2,1)S(1)} collective-permute-done((bf16[4,8,32,128]{3,2,1,0:T(8,128)(2,1)S(1)}, bf16[4,8,32,128]{3,2,1,0:T(8,128)(2,1)S(1)}, u32[]{:S(2)}, u32[]{:S(2)}) %collective-permute-start.2) | collective-permute-done | bytes 262176 | tf_op jit(solution)/shard_map/ppermute | solution.py:383
  24.4 0.1 collective-permute-start.3
  24.5 2.0 %collective-permute-done.5.refs_4_ = bf16[4,8,32,128]{3,2,1,0:T(8,128)(2,1)S(1)} collective-permute-done((bf16[4,8,32,128]{3,2,1,0:T(8,128)(2,1)S(1)}, bf16[4,8,32,128]{3,2,1,0:T(8,128)(2,1)S(1)}, u32[]{:S(2)}, u32[]{:S(2)}) %collective-permute-start.5) | collective-permute-done | bytes 262176 | tf_op jit(solution)/shard_map/ppermute | solution.py:398
  26.5 0.6 %cross_most.1 = (f32[4,4,32,128]{3,2,1,0:T(8,128)S(1)}, f32[4,4,32,128]{3,2,1,0:T(8,128)S(1)}) custom-call(f32[64,128]{1,0:T(8,128)S(1)} %gains.1.refs_0_, bf16[4,8,32,128]{3,2,1,0:T(8,128)(2,1)S(1)} %get-tuple-element.28.refs_1_.own_ref, bf16[4,8,32,128]{3,2,1,0:T(8,128)(2,1)S(1)} %collective-permute-done.1.refs_2_.own_ref, ...), custom_call_target="tpu_custom_call" | custom-call | flops 660000000 | tf_op jit(solution)/shard_map/cross_most/pallas_call | solution.py:312
  27.1 1.0 %collective-permute-done.4.refs_0_ = bf16[2,8,32,128]{3,2,1,0:T(8,128)(2,1)S(1)} collective-permute-done((bf16[2,8,32,128]{3,2,1,0:T(8,128)(2,1)S(1)}, bf16[2,8,32,128]{3,2,1,0:T(8,128)(2,1)S(1)}, u32[]{:S(2)}, u32[]{:S(2)}) %collective-permute-start.4) | collective-permute-done | bytes 131104 | tf_op jit(solution)/shard_map/ppermute | solution.py:395
  28.1 0.1 collective-permute-start.8
  28.2 0.5 %collective-permute-start.9 = (bf16[4,8,32,128]{3,2,1,0:T(8,128)(2,1)S(1)}, bf16[4,8,32,128]{3,2,1,0:T(8,128)(2,1)S(1)}, u32[]{:S(2)}, u32[]{:S(2)}) collective-permute-start(bf16[4,8,32,128]{3,2,1,0:T(8,128)(2,1)S(1)} %collective-permute-done.5.refs_4_), channel_id=1, source_target_pairs={{0,2},{2,0},{4,6},{6,4},{8,10},{10,8},{12,14},{14,12},{16,18},{18,... | collective-permute-start | bytes 786440 | tf_op jit(solution)/shard_map/ppermute | solution.py:401
  28.7 0.8 %collective-permute-done.3.refs_0_ = bf16[2,8,32,128]{3,2,1,0:T(8,128)(2,1)S(1)} collective-permute-done((bf16[2,8,32,128]{3,2,1,0:T(8,128)(2,1)S(1)}, bf16[2,8,32,128]{3,2,1,0:T(8,128)(2,1)S(1)}, u32[]{:S(2)}, u32[]{:S(2)}) %collective-permute-start.3) | collective-permute-done | bytes 131104 | tf_op jit(solution)/shard_map/ppermute | solution.py:398
  29.5 0.1 collective-permute-start.6
  29.6 0.4 %cross_mid.1.refs_6_ = f32[4,4,32,128]{3,2,1,0:T(8,128)S(1)} custom-call(f32[64,128]{1,0:T(8,128)S(1)} %gains.1.refs_0_, bf16[4,8,32,128]{3,2,1,0:T(8,128)(2,1)S(1)} %get-tuple-element.28.refs_1_.own_ref, bf16[4,8,32,128]{3,2,1,0:T(8,128)(2,1)S(1)} %collective-permute-done.1.refs_2_.own_ref, bf16[4,8,32,128]{3,2,1,0:T(8,128)(2,1)S(1)} %join.3.refs_3_, ...), custom_call_target="tpu_custom_call" | custom-call | flops 32999999488 | tf_op jit(solution)/shard_map/cross_mid/pallas_call | solution.py:312
  30.0 0.2 collective-permute-done.9.refs_5_
  30.1 0.0 collective-permute-done.8.refs_4_
  30.1 0.0 collective-permute-done.7.refs_3_
  30.1 0.7 %cross_next.1 = (f32[4,4,32,128]{3,2,1,0:T(8,128)S(1)}, f32[4,4,32,128]{3,2,1,0:T(8,128)S(1)}) custom-call(f32[64,128]{1,0:T(8,128)S(1)} %gains.1.refs_0_, bf16[4,8,32,128]{3,2,1,0:T(8,128)(2,1)S(1)} %get-tuple-element.28.refs_1_.own_ref, bf16[4,8,32,128]{3,2,1,0:T(8,128)(2,1)S(1)} %collective-permute-done.1.refs_2_.own_ref, ...), custom_call_target="tpu_custom_call" | custom-call | flops 660000000 | tf_op jit(solution)/shard_map/cross_next/pallas_call | solution.py:312
  30.9 0.2 collective-permute-done.6.refs_3_
  31.1 1.1 %cross_last.1 = f32[4,4,4,32,128]{4,3,2,1,0:T(8,128)} custom-call(f32[64,128]{1,0:T(8,128)S(1)} %gains.1.refs_0_, bf16[4,8,32,128]{3,2,1,0:T(8,128)(2,1)S(1)} %get-tuple-element.28.refs_1_.own_ref, bf16[4,8,32,128]{3,2,1,0:T(8,128)(2,1)S(1)} %collective-permute-done.1.refs_2_.own_ref, bf16[4,8,32,128]{3,2,1,0:T(8,128)(2,1)S(1)} %collective-permute-done.6.refs_3_, ...), custom_call_target="tpu_custom_call" | custom-call | flops 660000000 | tf_op jit(solution)/shard_map/cross_last/pallas_call | solution.py:312
  (7 shorter events, 0.1 us)
Async XLA Ops:
  0.0 1.2 %copy-start = (f32[4,8,8192]{2,1,0:T(8,128)S(1)}, f32[4,8,8192]{2,1,0:T(8,128)}, u32[]{:S(2)}) copy-start(f32[4,8,8192]{2,1,0:T(8,128)} %param.2) | copy-start | bytes 3145732
  4.2 9.3 %collective-permute-start.1 = (bf16[4,8,32,128]{3,2,1,0:T(8,128)(2,1)S(1)}, bf16[4,8,32,128]{3,2,1,0:T(8,128)(2,1)S(1)}, u32[]{:S(2)}, u32[]{:S(2)}) collective-permute-start(bf16[4,8,32,128]{3,2,1,0:T(8,128)(2,1)S(1)} %get-tuple-element.30), channel_id=1, source_target_pairs={{0,1},{1,0},{2,3},{3,2},{4,5},{5,4},{6,7},{7,6},{8,9},{9,8},{10,11... | collective-permute-start | bytes 786440 | tf_op jit(solution)/shard_map/ppermute | solution.py:382
  7.3 9.6 %collective-permute-start = (bf16[4,8,32,128]{3,2,1,0:T(8,128)(2,1)S(1)}, bf16[4,8,32,128]{3,2,1,0:T(8,128)(2,1)S(1)}, u32[]{:S(2)}, u32[]{:S(2)}) collective-permute-start(bf16[4,8,32,128]{3,2,1,0:T(8,128)(2,1)S(1)} %get-tuple-element.28.refs_1_.own_ref), channel_id=1, source_target_pairs={{8,0},{10,2},{12,4},{14,6},{16,8},{18,10},{20,12},{22,14},{24,16},... | collective-permute-start | bytes 786440 | tf_op jit(solution)/shard_map/ppermute | solution.py:383
  13.6 10.8 %collective-permute-start.2 = (bf16[4,8,32,128]{3,2,1,0:T(8,128)(2,1)S(1)}, bf16[4,8,32,128]{3,2,1,0:T(8,128)(2,1)S(1)}, u32[]{:S(2)}, u32[]{:S(2)}) collective-permute-start(bf16[4,8,32,128]{3,2,1,0:T(8,128)(2,1)S(1)} %collective-permute-done.1.refs_2_.own_ref), channel_id=1, source_target_pairs={{8,0},{10,2},{12,4},{14,6},{16,8},{18,10},{20,12},{22,14},{24,16},... | collective-permute-start | bytes 786440 | tf_op jit(solution)/shard_map/ppermute | solution.py:383
  17.0 9.5 %collective-permute-start.5 = (bf16[4,8,32,128]{3,2,1,0:T(8,128)(2,1)S(1)}, bf16[4,8,32,128]{3,2,1,0:T(8,128)(2,1)S(1)}, u32[]{:S(2)}, u32[]{:S(2)}) collective-permute-start(bf16[4,8,32,128]{3,2,1,0:T(8,128)(2,1)S(1)} %choose.5), channel_id=1, source_target_pairs={{0,4},{2,6},{4,0},{6,2},{8,12},{10,14},{12,8},{14,10},{16,20},{18,... | collective-permute-start | bytes 786440 | tf_op jit(solution)/shard_map/ppermute | solution.py:398
  18.5 1.4 %copy-start.1 = (s32[64]{0:T(128)S(1)}, s32[64]{0:T(128)}, u32[]{:S(2)}) copy-start(s32[64]{0:T(128)} %pos_ref) | copy-start | bytes 772
  18.5 9.5 %collective-permute-start.4 = (bf16[2,8,32,128]{3,2,1,0:T(8,128)(2,1)S(1)}, bf16[2,8,32,128]{3,2,1,0:T(8,128)(2,1)S(1)}, u32[]{:S(2)}, u32[]{:S(2)}) collective-permute-start(bf16[2,8,32,128]{3,2,1,0:T(8,128)(2,1)S(1)} %slice.4), channel_id=1, source_target_pairs={{4,0},{6,2},{8,4},{10,6},{12,8},{14,10},{16,12},{18,14},{20,16},{2... | collective-permute-start | bytes 393224 | tf_op jit(solution)/shard_map/ppermute | solution.py:395
  19.9 10.2 %collective-permute-start.7 = (bf16[4,8,32,128]{3,2,1,0:T(8,128)(2,1)S(1)}, bf16[4,8,32,128]{3,2,1,0:T(8,128)(2,1)S(1)}, u32[]{:S(2)}, u32[]{:S(2)}) collective-permute-start(bf16[4,8,32,128]{3,2,1,0:T(8,128)(2,1)S(1)} %choose.6), channel_id=1, source_target_pairs={{0,2},{2,0},{4,6},{6,4},{8,10},{10,8},{12,14},{14,12},{16,18},{18,... | collective-permute-start | bytes 786440 | tf_op jit(solution)/shard_map/ppermute | solution.py:399
  24.4 5.1 %collective-permute-start.3 = (bf16[2,8,32,128]{3,2,1,0:T(8,128)(2,1)S(1)}, bf16[2,8,32,128]{3,2,1,0:T(8,128)(2,1)S(1)}, u32[]{:S(2)}, u32[]{:S(2)}) collective-permute-start(bf16[2,8,32,128]{3,2,1,0:T(8,128)(2,1)S(1)} %choose.4), channel_id=1, source_target_pairs={{0,4},{2,6},{4,0},{6,2},{8,12},{10,14},{12,8},{14,10},{16,20},{18,... | collective-permute-start | bytes 393224 | tf_op jit(solution)/shard_map/ppermute | solution.py:398
  28.1 2.0 %collective-permute-start.8 = (bf16[4,8,32,128]{3,2,1,0:T(8,128)(2,1)S(1)}, bf16[4,8,32,128]{3,2,1,0:T(8,128)(2,1)S(1)}, u32[]{:S(2)}, u32[]{:S(2)}) collective-permute-start(bf16[4,8,32,128]{3,2,1,0:T(8,128)(2,1)S(1)} %choose.7), channel_id=1, source_target_pairs={{0,2},{2,0},{4,6},{6,4},{8,10},{10,8},{12,14},{14,12},{16,18},{18,... | collective-permute-start | bytes 786440 | tf_op jit(solution)/shard_map/ppermute | solution.py:399
  28.2 1.9 %collective-permute-start.9 = (bf16[4,8,32,128]{3,2,1,0:T(8,128)(2,1)S(1)}, bf16[4,8,32,128]{3,2,1,0:T(8,128)(2,1)S(1)}, u32[]{:S(2)}, u32[]{:S(2)}) collective-permute-start(bf16[4,8,32,128]{3,2,1,0:T(8,128)(2,1)S(1)} %collective-permute-done.5.refs_4_), channel_id=1, source_target_pairs={{0,2},{2,0},{4,6},{6,4},{8,10},{10,8},{12,14},{14,12},{16,18},{18,... | collective-permute-start | bytes 786440 | tf_op jit(solution)/shard_map/ppermute | solution.py:401
  29.5 1.6 %collective-permute-start.6 = (bf16[4,8,32,128]{3,2,1,0:T(8,128)(2,1)S(1)}, bf16[4,8,32,128]{3,2,1,0:T(8,128)(2,1)S(1)}, u32[]{:S(2)}, u32[]{:S(2)}) collective-permute-start(bf16[4,8,32,128]{3,2,1,0:T(8,128)(2,1)S(1)} %join.3.refs_3_), channel_id=1, source_target_pairs={{0,2},{2,0},{4,6},{6,4},{8,10},{10,8},{12,14},{14,12},{16,18},{18,... | collective-permute-start | bytes 786440 | tf_op jit(solution)/shard_map/ppermute | solution.py:413

commit v9 on v5

--- a/solution.py
+++ b/solution.py
@@ -78,6 +78,7 @@
     side = jnp.dot(
         jnp.concatenate([hi, lo], axis=1), side_ref[...], preferred_element_type=jnp.float32
     )
+    yield
     spec = (main[:, :LANES] + main[:, LANES:] + side).reshape(first, wins, LANES)
     total = jnp.dot(
         jnp.concatenate(split3(jnp.sum(spec * spec, axis=0)), axis=1),
@@ -93,6 +94,7 @@
     spread = lax.dot_general(
         pick_ref[...], white, (((1,), (1,)), ((), ())), preferred_element_type=jnp.float32
     )
+    yield
     left = lax.broadcasted_iota(jnp.int32, (bands, LANES), 1) < first
     for pair in range(wins // 2):
         tile = spread[:, pair * LANES : (pair + 1) * LANES].reshape(parts, 2, 2, bands, LANES)
@@ -179,9 +181,14 @@
 def spectra_kernel(parts, x_ref, *refs):
     tables, outs, t_ref = refs[:5], refs[5:-1], refs[-1]
     chans, first = x_ref.shape[:2]
-    for chan in range(chans):
-        x = [x_ref[chan, p] for p in range(first)]
-        spectra_channel(parts, chan, x, tables, t_ref, outs)
+    stages = 3
+    works = []
+    for turn in range(chans + stages - 1):
+        if turn < chans:
+            x = [x_ref[turn, p] for p in range(first)]
+            works.append(spectra_channel(parts, turn, x, tables, t_ref, outs))
+        for work in reversed(works[max(0, turn - stages + 1) :]):
+            next(work, None)
 
 
 def whitened_spectra(records, parts):

time: 32.3 us -> 31.8 us (0.985)
  Pallas kernels: 7.08 us -> 6.59 us
    pallas_call x1, Pallas kernels: 3.01 us -> 2.52 us  [whitened_spectra(): pl.pallas_call(functools.partial(spectra_kernel, parts), in_specs=[VMEM]...]
  transfers between devices with their start and end apart: 11 -> 11, of which waited for: 7 -> 7; matrix products, arithmetic and copies ran while one was open for 0% -> 0% of each run, Pallas kernels for 8% -> 9%
where the time goes in v9:
time: 31.8 us; the launch traced here: 31.6 us
  waiting for transfers between devices  14.7 us (46%)
  starting transfers between devices  9.25 us (29%)
  Pallas kernels  6.59 us (21%)
  local copies, waits for them, and re-layouts  0.94 us (3%)
    ppermute x2, waiting for transfers between devices, shards(): far = [lax.ppermute(own, 'chan', up) for own in mine]  5.63 us
    ppermute x1, waiting for transfers between devices, shards(): lax.ppermute(spectra[s], 'win', [(i, (i + s) % parts) for i in range(part...  5.01 us
    ppermute x2, waiting for transfers between devices, shards(): mid.append(lax.ppermute(choose(2, mine[s], far[s], count), 'chan', swap2))  3.17 us
    ppermute x1, starting transfers between devices, shards(): lax.ppermute(spectra[s], 'win', [(i, (i + s) % parts) for i in range(part...  3.03 us
    pallas_call x5, Pallas kernels, cross_call(): pl.pallas_call(functools.partial(cross_kernel, layout, jobs), in_specs=[V...  3.01 us
    ppermute x2, starting transfers between devices, shards(): far = [lax.ppermute(own, 'chan', up) for own in mine]  2.56 us
    pallas_call x1, Pallas kernels, whitened_spectra(): pl.pallas_call(functools.partial(spectra_kernel, parts), in_specs=[VMEM]...  2.52 us
    ppermute x2, starting transfers between devices, shards(): mid.append(lax.ppermute(choose(2, mine[s], far[s], count), 'chan', swap2))  1.63 us
  transfers between devices with their start and end apart: 11, of which 7 were waited for; matrix products, arithmetic and copies ran while one was open for 0% of the time, Pallas kernels for 9%

profile of v9, /device:TPU:0, one launch (start us, length us, event | category | flops | bytes accessed | tf_op | source)
XLA Modules:
  0.0 31.6 jit_solution(8026087903220398760)
XLA Ops:
  0.0 0.0 copy-start
  0.0 0.3 tables.1
  0.3 0.9 %copy-done = f32[4,8,8192]{2,1,0:T(8,128)S(1)} copy-done((f32[4,8,8192]{2,1,0:T(8,128)S(1)}, f32[4,8,8192]{2,1,0:T(8,128)}, u32[]{:S(2)}) %copy-start) | copy-done | bytes 1048600
  1.2 2.5 %spectra.1 = (bf16[4,8,32,128]{3,2,1,0:T(8,128)(2,1)S(1)}, bf16[4,8,32,128]{3,2,1,0:T(8,128)(2,1)S(1)}) custom-call(f32[4,64,8,128]{3,2,1,0:T(8,128)S(1)} %bitcast.8, f32[2,64,128]{2,1,0:T(8,128)S(1)} %get-tuple-element.23.refs_0_, bf16[512,256]{1,0:T(8,128)(2,1)S(1)} %get-tuple-element.24.refs_1_, bf16[512,128]{1,0:T(8,128)(2,1)S(1)} %get-tuple-element.25.refs_2_, ...), custom_call_target="tpu_custom_call" | custom-call | flops 4400000000 | tf_op jit(solution)/shard_map/spectra/pallas_call | solution.py:213
  3.8 3.0 %collective-permute-start.1 = (bf16[4,8,32,128]{3,2,1,0:T(8,128)(2,1)S(1)}, bf16[4,8,32,128]{3,2,1,0:T(8,128)(2,1)S(1)}, u32[]{:S(2)}, u32[]{:S(2)}) collective-permute-start(bf16[4,8,32,128]{3,2,1,0:T(8,128)(2,1)S(1)} %get-tuple-element.30), channel_id=1, source_target_pairs={{0,1},{1,0},{2,3},{3,2},{4,5},{5,4},{6,7},{7,6},{8,9},{9,8},{10,11... | collective-permute-start | bytes 786440 | tf_op jit(solution)/shard_map/ppermute | solution.py:378
  6.8 1.3 %collective-permute-start = (bf16[4,8,32,128]{3,2,1,0:T(8,128)(2,1)S(1)}, bf16[4,8,32,128]{3,2,1,0:T(8,128)(2,1)S(1)}, u32[]{:S(2)}, u32[]{:S(2)}) collective-permute-start(bf16[4,8,32,128]{3,2,1,0:T(8,128)(2,1)S(1)} %get-tuple-element.28.refs_1_.own_ref), channel_id=1, source_target_pairs={{8,0},{10,2},{12,4},{14,6},{16,8},{18,10},{20,12},{22,14},{24,16},... | collective-permute-start | bytes 786440 | tf_op jit(solution)/shard_map/ppermute | solution.py:379
  8.1 5.0 %collective-permute-done.1.refs_2_.own_ref = bf16[4,8,32,128]{3,2,1,0:T(8,128)(2,1)S(1)} collective-permute-done((bf16[4,8,32,128]{3,2,1,0:T(8,128)(2,1)S(1)}, bf16[4,8,32,128]{3,2,1,0:T(8,128)(2,1)S(1)}, u32[]{:S(2)}, u32[]{:S(2)}) %collective-permute-start.1) | collective-permute-done | bytes 262176 | tf_op jit(solution)/shard_map/ppermute | solution.py:378
  13.1 1.3 %collective-permute-start.2 = (bf16[4,8,32,128]{3,2,1,0:T(8,128)(2,1)S(1)}, bf16[4,8,32,128]{3,2,1,0:T(8,128)(2,1)S(1)}, u32[]{:S(2)}, u32[]{:S(2)}) collective-permute-start(bf16[4,8,32,128]{3,2,1,0:T(8,128)(2,1)S(1)} %collective-permute-done.1.refs_2_.own_ref), channel_id=1, source_target_pairs={{8,0},{10,2},{12,4},{14,6},{16,8},{18,10},{20,12},{22,14},{24,16},... | collective-permute-start | bytes 786440 | tf_op jit(solution)/shard_map/ppermute | solution.py:379
  14.4 2.1 %collective-permute-done.refs_3_.far_ref = bf16[4,8,32,128]{3,2,1,0:T(8,128)(2,1)S(1)} collective-permute-done((bf16[4,8,32,128]{3,2,1,0:T(8,128)(2,1)S(1)}, bf16[4,8,32,128]{3,2,1,0:T(8,128)(2,1)S(1)}, u32[]{:S(2)}, u32[]{:S(2)}) %collective-permute-start) | collective-permute-done | bytes 262176 | tf_op jit(solution)/shard_map/ppermute | solution.py:379
  16.4 0.0 copy-start.1
  16.5 1.6 %collective-permute-start.4 = (bf16[4,8,32,128]{3,2,1,0:T(8,128)(2,1)S(1)}, bf16[4,8,32,128]{3,2,1,0:T(8,128)(2,1)S(1)}, u32[]{:S(2)}, u32[]{:S(2)}) collective-permute-start(bf16[4,8,32,128]{3,2,1,0:T(8,128)(2,1)S(1)} %choose.5), channel_id=1, source_target_pairs={{0,4},{2,6},{4,0},{6,2},{8,12},{10,14},{12,8},{14,10},{16,20},{18,... | collective-permute-start | bytes 786440 | tf_op jit(solution)/shard_map/ppermute | solution.py:394
  18.0 1.3 %collective-permute-start.8 = (bf16[2,8,32,128]{3,2,1,0:T(8,128)(2,1)S(1)}, bf16[2,8,32,128]{3,2,1,0:T(8,128)(2,1)S(1)}, u32[]{:S(2)}, u32[]{:S(2)}) collective-permute-start(bf16[2,8,32,128]{3,2,1,0:T(8,128)(2,1)S(1)} %slice.4), channel_id=1, source_target_pairs={{4,0},{6,2},{8,4},{10,6},{12,8},{14,10},{16,12},{18,14},{20,16},{2... | collective-permute-start | bytes 393224 | tf_op jit(solution)/shard_map/ppermute | solution.py:391
  19.3 0.0 copy-done.1
  19.3 0.7 %gains.1.refs_0_ = f32[64,128]{1,0:T(8,128)S(1)} custom-call(s32[64]{0:T(128)S(1)} %copy-done.1), custom_call_target="tpu_custom_call" | custom-call | flops 550000000 | tf_op jit(solution)/shard_map/gains/pallas_call | solution.py:144
  20.0 0.2 cross_far.1.refs_5_
  20.3 3.6 %collective-permute-done.2.far_ref.refs_3_ = bf16[4,8,32,128]{3,2,1,0:T(8,128)(2,1)S(1)} collective-permute-done((bf16[4,8,32,128]{3,2,1,0:T(8,128)(2,1)S(1)}, bf16[4,8,32,128]{3,2,1,0:T(8,128)(2,1)S(1)}, u32[]{:S(2)}, u32[]{:S(2)}) %collective-permute-start.2) | collective-permute-done | bytes 262176 | tf_op jit(solution)/shard_map/ppermute | solution.py:379
  23.9 0.1 collective-permute-start.3
  24.0 0.1 collective-permute-start.6
  24.1 2.5 %collective-permute-done.4.refs_4_ = bf16[4,8,32,128]{3,2,1,0:T(8,128)(2,1)S(1)} collective-permute-done((bf16[4,8,32,128]{3,2,1,0:T(8,128)(2,1)S(1)}, bf16[4,8,32,128]{3,2,1,0:T(8,128)(2,1)S(1)}, u32[]{:S(2)}, u32[]{:S(2)}) %collective-permute-start.4) | collective-permute-done | bytes 262176 | tf_op jit(solution)/shard_map/ppermute | solution.py:394
  26.5 0.6 %cross_most.1 = (f32[4,4,32,128]{3,2,1,0:T(8,128)S(1)}, f32[4,4,32,128]{3,2,1,0:T(8,128)S(1)}) custom-call(f32[64,128]{1,0:T(8,128)S(1)} %gains.1.refs_0_, bf16[4,8,32,128]{3,2,1,0:T(8,128)(2,1)S(1)} %get-tuple-element.28.refs_1_.own_ref, bf16[4,8,32,128]{3,2,1,0:T(8,128)(2,1)S(1)} %collective-permute-done.1.refs_2_.own_ref, ...), custom_call_target="tpu_custom_call" | custom-call | flops 660000000 | tf_op jit(solution)/shard_map/cross_most/pallas_call | solution.py:327
  27.1 0.5 %collective-permute-done.8.refs_4_ = bf16[2,8,32,128]{3,2,1,0:T(8,128)(2,1)S(1)} collective-permute-done((bf16[2,8,32,128]{3,2,1,0:T(8,128)(2,1)S(1)}, bf16[2,8,32,128]{3,2,1,0:T(8,128)(2,1)S(1)}, u32[]{:S(2)}, u32[]{:S(2)}) %collective-permute-start.8) | collective-permute-done | bytes 131104 | tf_op jit(solution)/shard_map/ppermute | solution.py:391
  27.6 0.0 collective-permute-start.10
  27.6 0.6 %collective-permute-start.7 = (bf16[4,8,32,128]{3,2,1,0:T(8,128)(2,1)S(1)}, bf16[4,8,32,128]{3,2,1,0:T(8,128)(2,1)S(1)}, u32[]{:S(2)}, u32[]{:S(2)}) collective-permute-start(bf16[4,8,32,128]{3,2,1,0:T(8,128)(2,1)S(1)} %choose.7), channel_id=1, source_target_pairs={{0,2},{2,0},{4,6},{6,4},{8,10},{10,8},{12,14},{14,12},{16,18},{18,... | collective-permute-start | bytes 786440 | tf_op jit(solution)/shard_map/ppermute | solution.py:395
  28.2 0.1 collective-permute-start.9
  28.3 0.7 %collective-permute-done.3.refs_3_ = bf16[2,8,32,128]{3,2,1,0:T(8,128)(2,1)S(1)} collective-permute-done((bf16[2,8,32,128]{3,2,1,0:T(8,128)(2,1)S(1)}, bf16[2,8,32,128]{3,2,1,0:T(8,128)(2,1)S(1)}, u32[]{:S(2)}, u32[]{:S(2)}) %collective-permute-start.3) | collective-permute-done | bytes 131104 | tf_op jit(solution)/shard_map/ppermute | solution.py:394
  29.0 0.0 collective-permute-start.5
  29.0 0.4 %cross_mid.1.refs_7_ = f32[4,4,32,128]{3,2,1,0:T(8,128)S(1)} custom-call(f32[64,128]{1,0:T(8,128)S(1)} %gains.1.refs_0_, bf16[4,8,32,128]{3,2,1,0:T(8,128)(2,1)S(1)} %get-tuple-element.28.refs_1_.own_ref, bf16[4,8,32,128]{3,2,1,0:T(8,128)(2,1)S(1)} %collective-permute-done.1.refs_2_.own_ref, bf16[2,8,32,128]{3,2,1,0:T(8,128)(2,1)S(1)} %collective-permute-done.3.refs_3_, ...), custom_call_target="tpu_custom_call" | custom-call | flops 32999999488 | tf_op jit(solution)/shard_map/cross_mid/pallas_call | solution.py:327
  29.4 0.4 %collective-permute-done.9.refs_5_ = bf16[4,8,32,128]{3,2,1,0:T(8,128)(2,1)S(1)} collective-permute-done((bf16[4,8,32,128]{3,2,1,0:T(8,128)(2,1)S(1)}, bf16[4,8,32,128]{3,2,1,0:T(8,128)(2,1)S(1)}, u32[]{:S(2)}, u32[]{:S(2)}) %collective-permute-start.9) | collective-permute-done | bytes 262176 | tf_op jit(solution)/shard_map/ppermute | solution.py:397
  29.7 0.0 collective-permute-done.7.refs_4_
  29.7 0.0 collective-permute-done.6.refs_3_
  29.7 0.7 %cross_next.1 = (f32[4,4,32,128]{3,2,1,0:T(8,128)S(1)}, f32[4,4,32,128]{3,2,1,0:T(8,128)S(1)}) custom-call(f32[64,128]{1,0:T(8,128)S(1)} %gains.1.refs_0_, bf16[4,8,32,128]{3,2,1,0:T(8,128)(2,1)S(1)} %get-tuple-element.28.refs_1_.own_ref, bf16[4,8,32,128]{3,2,1,0:T(8,128)(2,1)S(1)} %collective-permute-done.1.refs_2_.own_ref, ...), custom_call_target="tpu_custom_call" | custom-call | flops 660000000 | tf_op jit(solution)/shard_map/cross_next/pallas_call | solution.py:327
  30.5 0.0 collective-permute-done.5.refs_3_
  30.5 0.0 collective-permute-done.10.refs_4_
  30.5 1.1 %cross_last.1 = f32[4,4,4,32,128]{4,3,2,1,0:T(8,128)} custom-call(f32[64,128]{1,0:T(8,128)S(1)} %gains.1.refs_0_, bf16[4,8,32,128]{3,2,1,0:T(8,128)(2,1)S(1)} %get-tuple-element.28.refs_1_.own_ref, bf16[4,8,32,128]{3,2,1,0:T(8,128)(2,1)S(1)} %collective-permute-done.1.refs_2_.own_ref, bf16[2,8,32,128]{3,2,1,0:T(8,128)(2,1)S(1)} %collective-permute-done.5.refs_3_, ...), custom_call_target="tpu_custom_call" | custom-call | flops 660000000 | tf_op jit(solution)/shard_map/cross_last/pallas_call | solution.py:327
  (5 shorter events, 0.1 us)
Async XLA Ops:
  0.0 1.2 %copy-start = (f32[4,8,8192]{2,1,0:T(8,128)S(1)}, f32[4,8,8192]{2,1,0:T(8,128)}, u32[]{:S(2)}) copy-start(f32[4,8,8192]{2,1,0:T(8,128)} %param.2) | copy-start | bytes 3145732
  3.8 9.3 %collective-permute-start.1 = (bf16[4,8,32,128]{3,2,1,0:T(8,128)(2,1)S(1)}, bf16[4,8,32,128]{3,2,1,0:T(8,128)(2,1)S(1)}, u32[]{:S(2)}, u32[]{:S(2)}) collective-permute-start(bf16[4,8,32,128]{3,2,1,0:T(8,128)(2,1)S(1)} %get-tuple-element.30), channel_id=1, source_target_pairs={{0,1},{1,0},{2,3},{3,2},{4,5},{5,4},{6,7},{7,6},{8,9},{9,8},{10,11... | collective-permute-start | bytes 786440 | tf_op jit(solution)/shard_map/ppermute | solution.py:378
  6.8 9.6 %collective-permute-start = (bf16[4,8,32,128]{3,2,1,0:T(8,128)(2,1)S(1)}, bf16[4,8,32,128]{3,2,1,0:T(8,128)(2,1)S(1)}, u32[]{:S(2)}, u32[]{:S(2)}) collective-permute-start(bf16[4,8,32,128]{3,2,1,0:T(8,128)(2,1)S(1)} %get-tuple-element.28.refs_1_.own_ref), channel_id=1, source_target_pairs={{8,0},{10,2},{12,4},{14,6},{16,8},{18,10},{20,12},{22,14},{24,16},... | collective-permute-start | bytes 786440 | tf_op jit(solution)/shard_map/ppermute | solution.py:379
  13.1 10.8 %collective-permute-start.2 = (bf16[4,8,32,128]{3,2,1,0:T(8,128)(2,1)S(1)}, bf16[4,8,32,128]{3,2,1,0:T(8,128)(2,1)S(1)}, u32[]{:S(2)}, u32[]{:S(2)}) collective-permute-start(bf16[4,8,32,128]{3,2,1,0:T(8,128)(2,1)S(1)} %collective-permute-done.1.refs_2_.own_ref), channel_id=1, source_target_pairs={{8,0},{10,2},{12,4},{14,6},{16,8},{18,10},{20,12},{22,14},{24,16},... | collective-permute-start | bytes 786440 | tf_op jit(solution)/shard_map/ppermute | solution.py:379
  16.4 2.9 %copy-start.1 = (s32[64]{0:T(128)S(1)}, s32[64]{0:T(128)}, u32[]{:S(2)}) copy-start(s32[64]{0:T(128)} %pos_ref) | copy-start | bytes 772
  16.5 10.1 %collective-permute-start.4 = (bf16[4,8,32,128]{3,2,1,0:T(8,128)(2,1)S(1)}, bf16[4,8,32,128]{3,2,1,0:T(8,128)(2,1)S(1)}, u32[]{:S(2)}, u32[]{:S(2)}) collective-permute-start(bf16[4,8,32,128]{3,2,1,0:T(8,128)(2,1)S(1)} %choose.5), channel_id=1, source_target_pairs={{0,4},{2,6},{4,0},{6,2},{8,12},{10,14},{12,8},{14,10},{16,20},{18,... | collective-permute-start | bytes 786440 | tf_op jit(solution)/shard_map/ppermute | solution.py:394
  18.0 9.6 %collective-permute-start.8 = (bf16[2,8,32,128]{3,2,1,0:T(8,128)(2,1)S(1)}, bf16[2,8,32,128]{3,2,1,0:T(8,128)(2,1)S(1)}, u32[]{:S(2)}, u32[]{:S(2)}) collective-permute-start(bf16[2,8,32,128]{3,2,1,0:T(8,128)(2,1)S(1)} %slice.4), channel_id=1, source_target_pairs={{4,0},{6,2},{8,4},{10,6},{12,8},{14,10},{16,12},{18,14},{20,16},{2... | collective-permute-start | bytes 393224 | tf_op jit(solution)/shard_map/ppermute | solution.py:391
  23.9 5.1 %collective-permute-start.3 = (bf16[2,8,32,128]{3,2,1,0:T(8,128)(2,1)S(1)}, bf16[2,8,32,128]{3,2,1,0:T(8,128)(2,1)S(1)}, u32[]{:S(2)}, u32[]{:S(2)}) collective-permute-start(bf16[2,8,32,128]{3,2,1,0:T(8,128)(2,1)S(1)} %choose.4), channel_id=1, source_target_pairs={{0,4},{2,6},{4,0},{6,2},{8,12},{10,14},{12,8},{14,10},{16,20},{18,... | collective-permute-start | bytes 393224 | tf_op jit(solution)/shard_map/ppermute | solution.py:394
  24.0 5.7 %collective-permute-start.6 = (bf16[4,8,32,128]{3,2,1,0:T(8,128)(2,1)S(1)}, bf16[4,8,32,128]{3,2,1,0:T(8,128)(2,1)S(1)}, u32[]{:S(2)}, u32[]{:S(2)}) collective-permute-start(bf16[4,8,32,128]{3,2,1,0:T(8,128)(2,1)S(1)} %choose.6), channel_id=1, source_target_pairs={{0,2},{2,0},{4,6},{6,4},{8,10},{10,8},{12,14},{14,12},{16,18},{18,... | collective-permute-start | bytes 786440 | tf_op jit(solution)/shard_map/ppermute | solution.py:395
  27.6 2.9 %collective-permute-start.10 = (bf16[2,8,32,128]{3,2,1,0:T(8,128)(2,1)S(1)}, bf16[2,8,32,128]{3,2,1,0:T(8,128)(2,1)S(1)}, u32[]{:S(2)}, u32[]{:S(2)}) collective-permute-start(bf16[2,8,32,128]{3,2,1,0:T(8,128)(2,1)S(1)} %collective-permute-done.8.refs_4_), channel_id=1, source_target_pairs={{0,2},{2,0},{4,6},{6,4},{8,10},{10,8},{12,14},{14,12},{16,18},{18,... | collective-permute-start | bytes 393224 | tf_op jit(solution)/shard_map/ppermute | solution.py:408
  27.6 2.1 %collective-permute-start.7 = (bf16[4,8,32,128]{3,2,1,0:T(8,128)(2,1)S(1)}, bf16[4,8,32,128]{3,2,1,0:T(8,128)(2,1)S(1)}, u32[]{:S(2)}, u32[]{:S(2)}) collective-permute-start(bf16[4,8,32,128]{3,2,1,0:T(8,128)(2,1)S(1)} %choose.7), channel_id=1, source_target_pairs={{0,2},{2,0},{4,6},{6,4},{8,10},{10,8},{12,14},{14,12},{16,18},{18,... | collective-permute-start | bytes 786440 | tf_op jit(solution)/shard_map/ppermute | solution.py:395
  28.2 1.5 %collective-permute-start.9 = (bf16[4,8,32,128]{3,2,1,0:T(8,128)(2,1)S(1)}, bf16[4,8,32,128]{3,2,1,0:T(8,128)(2,1)S(1)}, u32[]{:S(2)}, u32[]{:S(2)}) collective-permute-start(bf16[4,8,32,128]{3,2,1,0:T(8,128)(2,1)S(1)} %collective-permute-done.4.refs_4_), channel_id=1, source_target_pairs={{0,2},{2,0},{4,6},{6,4},{8,10},{10,8},{12,14},{14,12},{16,18},{18,... | collective-permute-start | bytes 786440 | tf_op jit(solution)/shard_map/ppermute | solution.py:397
  29.0 1.5 %collective-permute-start.5 = (bf16[2,8,32,128]{3,2,1,0:T(8,128)(2,1)S(1)}, bf16[2,8,32,128]{3,2,1,0:T(8,128)(2,1)S(1)}, u32[]{:S(2)}, u32[]{:S(2)}) collective-permute-start(bf16[2,8,32,128]{3,2,1,0:T(8,128)(2,1)S(1)} %collective-permute-done.3.refs_3_), channel_id=1, source_target_pairs={{0,2},{2,0},{4,6},{6,4},{8,10},{10,8},{12,14},{14,12},{16,18},{18,... | collective-permute-start | bytes 393224 | tf_op jit(solution)/shard_map/ppermute | solution.py:410

commit v10 on v9

--- a/solution.py
+++ b/solution.py
@@ -72,6 +72,7 @@
             row = [re * cos - im * sin, -(im * cos + re * sin)]
         rows.append(jnp.concatenate(row, axis=1))
     hi, mid, lo = split3(jnp.concatenate(rows, axis=0))
+    yield
     main = jnp.dot(
         jnp.concatenate([hi, mid], axis=1), main_ref[...], preferred_element_type=jnp.float32
     )
@@ -181,7 +182,7 @@
 def spectra_kernel(parts, x_ref, *refs):
     tables, outs, t_ref = refs[:5], refs[5:-1], refs[-1]
     chans, first = x_ref.shape[:2]
-    stages = 3
+    stages = 4
     works = []
     for turn in range(chans + stages - 1):
         if turn < chans:

time: 31.8 us -> 31.8 us (level)
  transfers between devices with their start and end apart: 11 -> 11, of which waited for: 7 -> 7; matrix products, arithmetic and copies ran while one was open for 0% -> 0% of each run, Pallas kernels for 9% -> 8%
where the time goes in v10:
time: 31.8 us; the launch traced here: 31.6 us
  waiting for transfers between devices  14.7 us (46%)
  starting transfers between devices  9.26 us (29%)
  Pallas kernels  6.59 us (21%)
  local copies, waits for them, and re-layouts  0.94 us (3%)
    ppermute x2, waiting for transfers between devices, shards(): far = [lax.ppermute(own, 'chan', up) for own in mine]  5.63 us
    ppermute x1, waiting for transfers between devices, shards(): lax.ppermute(spectra[s], 'win', [(i, (i + s) % parts) for i in range(part...  5.01 us
    ppermute x2, waiting for transfers between devices, shards(): mid.append(lax.ppermute(choose(2, mine[s], far[s], count), 'chan', swap2))  3.16 us
    ppermute x1, starting transfers between devices, shards(): lax.ppermute(spectra[s], 'win', [(i, (i + s) % parts) for i in range(part...  3.03 us
    pallas_call x5, Pallas kernels, cross_call(): pl.pallas_call(functools.partial(cross_kernel, layout, jobs), in_specs=[V...  3.01 us
    ppermute x2, starting transfers between devices, shards(): far = [lax.ppermute(own, 'chan', up) for own in mine]  2.56 us
    pallas_call x1, Pallas kernels, whitened_spectra(): pl.pallas_call(functools.partial(spectra_kernel, parts), in_specs=[VMEM]...  2.52 us
    ppermute x2, starting transfers between devices, shards(): mid.append(lax.ppermute(choose(2, mine[s], far[s], count), 'chan', swap2))  1.64 us
  transfers between devices with their start and end apart: 11, of which 7 were waited for; matrix products, arithmetic and copies ran while one was open for 0% of the time, Pallas kernels for 8%

profile of v10, /device:TPU:0, one launch (start us, length us, event | category | flops | bytes accessed | tf_op | source)
XLA Modules:
  0.0 31.6 jit_solution(12508915768248842306)
XLA Ops:
  0.0 0.0 copy-start
  0.0 0.3 tables.1
  0.3 0.9 %copy-done = f32[4,8,8192]{2,1,0:T(8,128)S(1)} copy-done((f32[4,8,8192]{2,1,0:T(8,128)S(1)}, f32[4,8,8192]{2,1,0:T(8,128)}, u32[]{:S(2)}) %copy-start) | copy-done | bytes 1048600
  1.2 2.5 %spectra.1 = (bf16[4,8,32,128]{3,2,1,0:T(8,128)(2,1)S(1)}, bf16[4,8,32,128]{3,2,1,0:T(8,128)(2,1)S(1)}) custom-call(f32[4,64,8,128]{3,2,1,0:T(8,128)S(1)} %bitcast.8, f32[2,64,128]{2,1,0:T(8,128)S(1)} %get-tuple-element.23.refs_0_, bf16[512,256]{1,0:T(8,128)(2,1)S(1)} %get-tuple-element.24.refs_1_, bf16[512,128]{1,0:T(8,128)(2,1)S(1)} %get-tuple-element.25.refs_2_, ...), custom_call_target="tpu_custom_call" | custom-call | flops 4400000000 | tf_op jit(solution)/shard_map/spectra/pallas_call | solution.py:214
  3.8 3.0 %collective-permute-start.1 = (bf16[4,8,32,128]{3,2,1,0:T(8,128)(2,1)S(1)}, bf16[4,8,32,128]{3,2,1,0:T(8,128)(2,1)S(1)}, u32[]{:S(2)}, u32[]{:S(2)}) collective-permute-start(bf16[4,8,32,128]{3,2,1,0:T(8,128)(2,1)S(1)} %get-tuple-element.30), channel_id=1, source_target_pairs={{0,1},{1,0},{2,3},{3,2},{4,5},{5,4},{6,7},{7,6},{8,9},{9,8},{10,11... | collective-permute-start | bytes 786440 | tf_op jit(solution)/shard_map/ppermute | solution.py:379
  6.8 1.3 %collective-permute-start = (bf16[4,8,32,128]{3,2,1,0:T(8,128)(2,1)S(1)}, bf16[4,8,32,128]{3,2,1,0:T(8,128)(2,1)S(1)}, u32[]{:S(2)}, u32[]{:S(2)}) collective-permute-start(bf16[4,8,32,128]{3,2,1,0:T(8,128)(2,1)S(1)} %get-tuple-element.28.refs_1_.own_ref), channel_id=1, source_target_pairs={{8,0},{10,2},{12,4},{14,6},{16,8},{18,10},{20,12},{22,14},{24,16},... | collective-permute-start | bytes 786440 | tf_op jit(solution)/shard_map/ppermute | solution.py:380
  8.1 5.0 %collective-permute-done.1.refs_2_.own_ref = bf16[4,8,32,128]{3,2,1,0:T(8,128)(2,1)S(1)} collective-permute-done((bf16[4,8,32,128]{3,2,1,0:T(8,128)(2,1)S(1)}, bf16[4,8,32,128]{3,2,1,0:T(8,128)(2,1)S(1)}, u32[]{:S(2)}, u32[]{:S(2)}) %collective-permute-start.1) | collective-permute-done | bytes 262176 | tf_op jit(solution)/shard_map/ppermute | solution.py:379
  13.1 1.3 %collective-permute-start.2 = (bf16[4,8,32,128]{3,2,1,0:T(8,128)(2,1)S(1)}, bf16[4,8,32,128]{3,2,1,0:T(8,128)(2,1)S(1)}, u32[]{:S(2)}, u32[]{:S(2)}) collective-permute-start(bf16[4,8,32,128]{3,2,1,0:T(8,128)(2,1)S(1)} %collective-permute-done.1.refs_2_.own_ref), channel_id=1, source_target_pairs={{8,0},{10,2},{12,4},{14,6},{16,8},{18,10},{20,12},{22,14},{24,16},... | collective-permute-start | bytes 786440 | tf_op jit(solution)/shard_map/ppermute | solution.py:380
  14.4 2.1 %collective-permute-done.refs_3_.far_ref = bf16[4,8,32,128]{3,2,1,0:T(8,128)(2,1)S(1)} collective-permute-done((bf16[4,8,32,128]{3,2,1,0:T(8,128)(2,1)S(1)}, bf16[4,8,32,128]{3,2,1,0:T(8,128)(2,1)S(1)}, u32[]{:S(2)}, u32[]{:S(2)}) %collective-permute-start) | collective-permute-done | bytes 262176 | tf_op jit(solution)/shard_map/ppermute | solution.py:380
  16.4 0.0 copy-start.1
  16.5 1.6 %collective-permute-start.4 = (bf16[4,8,32,128]{3,2,1,0:T(8,128)(2,1)S(1)}, bf16[4,8,32,128]{3,2,1,0:T(8,128)(2,1)S(1)}, u32[]{:S(2)}, u32[]{:S(2)}) collective-permute-start(bf16[4,8,32,128]{3,2,1,0:T(8,128)(2,1)S(1)} %choose.5), channel_id=1, source_target_pairs={{0,4},{2,6},{4,0},{6,2},{8,12},{10,14},{12,8},{14,10},{16,20},{18,... | collective-permute-start | bytes 786440 | tf_op jit(solution)/shard_map/ppermute | solution.py:395
  18.0 1.3 %collective-permute-start.8 = (bf16[2,8,32,128]{3,2,1,0:T(8,128)(2,1)S(1)}, bf16[2,8,32,128]{3,2,1,0:T(8,128)(2,1)S(1)}, u32[]{:S(2)}, u32[]{:S(2)}) collective-permute-start(bf16[2,8,32,128]{3,2,1,0:T(8,128)(2,1)S(1)} %slice.4), channel_id=1, source_target_pairs={{4,0},{6,2},{8,4},{10,6},{12,8},{14,10},{16,12},{18,14},{20,16},{2... | collective-permute-start | bytes 393224 | tf_op jit(solution)/shard_map/ppermute | solution.py:392
  19.3 0.0 copy-done.1
  19.3 0.7 %gains.1.refs_0_ = f32[64,128]{1,0:T(8,128)S(1)} custom-call(s32[64]{0:T(128)S(1)} %copy-done.1), custom_call_target="tpu_custom_call" | custom-call | flops 550000000 | tf_op jit(solution)/shard_map/gains/pallas_call | solution.py:145
  20.0 0.2 cross_far.1.refs_5_
  20.3 3.6 %collective-permute-done.2.far_ref.refs_3_ = bf16[4,8,32,128]{3,2,1,0:T(8,128)(2,1)S(1)} collective-permute-done((bf16[4,8,32,128]{3,2,1,0:T(8,128)(2,1)S(1)}, bf16[4,8,32,128]{3,2,1,0:T(8,128)(2,1)S(1)}, u32[]{:S(2)}, u32[]{:S(2)}) %collective-permute-start.2) | collective-permute-done | bytes 262176 | tf_op jit(solution)/shard_map/ppermute | solution.py:380
  23.9 0.1 collective-permute-start.3
  24.0 0.1 collective-permute-start.6
  24.1 2.4 %collective-permute-done.4.refs_4_ = bf16[4,8,32,128]{3,2,1,0:T(8,128)(2,1)S(1)} collective-permute-done((bf16[4,8,32,128]{3,2,1,0:T(8,128)(2,1)S(1)}, bf16[4,8,32,128]{3,2,1,0:T(8,128)(2,1)S(1)}, u32[]{:S(2)}, u32[]{:S(2)}) %collective-permute-start.4) | collective-permute-done | bytes 262176 | tf_op jit(solution)/shard_map/ppermute | solution.py:395
  26.5 0.6 %cross_most.1 = (f32[4,4,32,128]{3,2,1,0:T(8,128)S(1)}, f32[4,4,32,128]{3,2,1,0:T(8,128)S(1)}) custom-call(f32[64,128]{1,0:T(8,128)S(1)} %gains.1.refs_0_, bf16[4,8,32,128]{3,2,1,0:T(8,128)(2,1)S(1)} %get-tuple-element.28.refs_1_.own_ref, bf16[4,8,32,128]{3,2,1,0:T(8,128)(2,1)S(1)} %collective-permute-done.1.refs_2_.own_ref, ...), custom_call_target="tpu_custom_call" | custom-call | flops 660000000 | tf_op jit(solution)/shard_map/cross_most/pallas_call | solution.py:328
  27.1 0.5 %collective-permute-done.8.refs_4_ = bf16[2,8,32,128]{3,2,1,0:T(8,128)(2,1)S(1)} collective-permute-done((bf16[2,8,32,128]{3,2,1,0:T(8,128)(2,1)S(1)}, bf16[2,8,32,128]{3,2,1,0:T(8,128)(2,1)S(1)}, u32[]{:S(2)}, u32[]{:S(2)}) %collective-permute-start.8) | collective-permute-done | bytes 131104 | tf_op jit(solution)/shard_map/ppermute | solution.py:392
  27.6 0.0 collective-permute-start.10
  27.6 0.6 %collective-permute-start.7 = (bf16[4,8,32,128]{3,2,1,0:T(8,128)(2,1)S(1)}, bf16[4,8,32,128]{3,2,1,0:T(8,128)(2,1)S(1)}, u32[]{:S(2)}, u32[]{:S(2)}) collective-permute-start(bf16[4,8,32,128]{3,2,1,0:T(8,128)(2,1)S(1)} %choose.7), channel_id=1, source_target_pairs={{0,2},{2,0},{4,6},{6,4},{8,10},{10,8},{12,14},{14,12},{16,18},{18,... | collective-permute-start | bytes 786440 | tf_op jit(solution)/shard_map/ppermute | solution.py:396
  28.2 0.1 collective-permute-start.9
  28.3 0.7 %collective-permute-done.3.refs_3_ = bf16[2,8,32,128]{3,2,1,0:T(8,128)(2,1)S(1)} collective-permute-done((bf16[2,8,32,128]{3,2,1,0:T(8,128)(2,1)S(1)}, bf16[2,8,32,128]{3,2,1,0:T(8,128)(2,1)S(1)}, u32[]{:S(2)}, u32[]{:S(2)}) %collective-permute-start.3) | collective-permute-done | bytes 131104 | tf_op jit(solution)/shard_map/ppermute | solution.py:395
  29.0 0.0 collective-permute-start.5
  29.0 0.4 %cross_mid.1.refs_7_ = f32[4,4,32,128]{3,2,1,0:T(8,128)S(1)} custom-call(f32[64,128]{1,0:T(8,128)S(1)} %gains.1.refs_0_, bf16[4,8,32,128]{3,2,1,0:T(8,128)(2,1)S(1)} %get-tuple-element.28.refs_1_.own_ref, bf16[4,8,32,128]{3,2,1,0:T(8,128)(2,1)S(1)} %collective-permute-done.1.refs_2_.own_ref, bf16[2,8,32,128]{3,2,1,0:T(8,128)(2,1)S(1)} %collective-permute-done.3.refs_3_, ...), custom_call_target="tpu_custom_call" | custom-call | flops 32999999488 | tf_op jit(solution)/shard_map/cross_mid/pallas_call | solution.py:328
  29.4 0.4 %collective-permute-done.9.refs_5_ = bf16[4,8,32,128]{3,2,1,0:T(8,128)(2,1)S(1)} collective-permute-done((bf16[4,8,32,128]{3,2,1,0:T(8,128)(2,1)S(1)}, bf16[4,8,32,128]{3,2,1,0:T(8,128)(2,1)S(1)}, u32[]{:S(2)}, u32[]{:S(2)}) %collective-permute-start.9) | collective-permute-done | bytes 262176 | tf_op jit(solution)/shard_map/ppermute | solution.py:398
  29.7 0.0 collective-permute-done.7.refs_4_
  29.7 0.0 collective-permute-done.6.refs_3_
  29.7 0.7 %cross_next.1 = (f32[4,4,32,128]{3,2,1,0:T(8,128)S(1)}, f32[4,4,32,128]{3,2,1,0:T(8,128)S(1)}) custom-call(f32[64,128]{1,0:T(8,128)S(1)} %gains.1.refs_0_, bf16[4,8,32,128]{3,2,1,0:T(8,128)(2,1)S(1)} %get-tuple-element.28.refs_1_.own_ref, bf16[4,8,32,128]{3,2,1,0:T(8,128)(2,1)S(1)} %collective-permute-done.1.refs_2_.own_ref, ...), custom_call_target="tpu_custom_call" | custom-call | flops 660000000 | tf_op jit(solution)/shard_map/cross_next/pallas_call | solution.py:328
  30.5 0.0 collective-permute-done.5.refs_3_
  30.5 0.0 collective-permute-done.10.refs_4_
  30.5 1.1 %cross_last.1 = f32[4,4,4,32,128]{4,3,2,1,0:T(8,128)} custom-call(f32[64,128]{1,0:T(8,128)S(1)} %gains.1.refs_0_, bf16[4,8,32,128]{3,2,1,0:T(8,128)(2,1)S(1)} %get-tuple-element.28.refs_1_.own_ref, bf16[4,8,32,128]{3,2,1,0:T(8,128)(2,1)S(1)} %collective-permute-done.1.refs_2_.own_ref, bf16[2,8,32,128]{3,2,1,0:T(8,128)(2,1)S(1)} %collective-permute-done.5.refs_3_, ...), custom_call_target="tpu_custom_call" | custom-call | flops 660000000 | tf_op jit(solution)/shard_map/cross_last/pallas_call | solution.py:328
  (5 shorter events, 0.1 us)
Async XLA Ops:
  0.0 1.2 %copy-start = (f32[4,8,8192]{2,1,0:T(8,128)S(1)}, f32[4,8,8192]{2,1,0:T(8,128)}, u32[]{:S(2)}) copy-start(f32[4,8,8192]{2,1,0:T(8,128)} %param.2) | copy-start | bytes 3145732
  3.8 9.3 %collective-permute-start.1 = (bf16[4,8,32,128]{3,2,1,0:T(8,128)(2,1)S(1)}, bf16[4,8,32,128]{3,2,1,0:T(8,128)(2,1)S(1)}, u32[]{:S(2)}, u32[]{:S(2)}) collective-permute-start(bf16[4,8,32,128]{3,2,1,0:T(8,128)(2,1)S(1)} %get-tuple-element.30), channel_id=1, source_target_pairs={{0,1},{1,0},{2,3},{3,2},{4,5},{5,4},{6,7},{7,6},{8,9},{9,8},{10,11... | collective-permute-start | bytes 786440 | tf_op jit(solution)/shard_map/ppermute | solution.py:379
  6.8 9.6 %collective-permute-start = (bf16[4,8,32,128]{3,2,1,0:T(8,128)(2,1)S(1)}, bf16[4,8,32,128]{3,2,1,0:T(8,128)(2,1)S(1)}, u32[]{:S(2)}, u32[]{:S(2)}) collective-permute-start(bf16[4,8,32,128]{3,2,1,0:T(8,128)(2,1)S(1)} %get-tuple-element.28.refs_1_.own_ref), channel_id=1, source_target_pairs={{8,0},{10,2},{12,4},{14,6},{16,8},{18,10},{20,12},{22,14},{24,16},... | collective-permute-start | bytes 786440 | tf_op jit(solution)/shard_map/ppermute | solution.py:380
  13.1 10.8 %collective-permute-start.2 = (bf16[4,8,32,128]{3,2,1,0:T(8,128)(2,1)S(1)}, bf16[4,8,32,128]{3,2,1,0:T(8,128)(2,1)S(1)}, u32[]{:S(2)}, u32[]{:S(2)}) collective-permute-start(bf16[4,8,32,128]{3,2,1,0:T(8,128)(2,1)S(1)} %collective-permute-done.1.refs_2_.own_ref), channel_id=1, source_target_pairs={{8,0},{10,2},{12,4},{14,6},{16,8},{18,10},{20,12},{22,14},{24,16},... | collective-permute-start | bytes 786440 | tf_op jit(solution)/shard_map/ppermute | solution.py:380
  16.4 2.9 %copy-start.1 = (s32[64]{0:T(128)S(1)}, s32[64]{0:T(128)}, u32[]{:S(2)}) copy-start(s32[64]{0:T(128)} %pos_ref) | copy-start | bytes 772
  16.5 10.0 %collective-permute-start.4 = (bf16[4,8,32,128]{3,2,1,0:T(8,128)(2,1)S(1)}, bf16[4,8,32,128]{3,2,1,0:T(8,128)(2,1)S(1)}, u32[]{:S(2)}, u32[]{:S(2)}) collective-permute-start(bf16[4,8,32,128]{3,2,1,0:T(8,128)(2,1)S(1)} %choose.5), channel_id=1, source_target_pairs={{0,4},{2,6},{4,0},{6,2},{8,12},{10,14},{12,8},{14,10},{16,20},{18,... | collective-permute-start | bytes 786440 | tf_op jit(solution)/shard_map/ppermute | solution.py:395
  18.0 9.6 %collective-permute-start.8 = (bf16[2,8,32,128]{3,2,1,0:T(8,128)(2,1)S(1)}, bf16[2,8,32,128]{3,2,1,0:T(8,128)(2,1)S(1)}, u32[]{:S(2)}, u32[]{:S(2)}) collective-permute-start(bf16[2,8,32,128]{3,2,1,0:T(8,128)(2,1)S(1)} %slice.4), channel_id=1, source_target_pairs={{4,0},{6,2},{8,4},{10,6},{12,8},{14,10},{16,12},{18,14},{20,16},{2... | collective-permute-start | bytes 393224 | tf_op jit(solution)/shard_map/ppermute | solution.py:392
  23.9 5.1 %collective-permute-start.3 = (bf16[2,8,32,128]{3,2,1,0:T(8,128)(2,1)S(1)}, bf16[2,8,32,128]{3,2,1,0:T(8,128)(2,1)S(1)}, u32[]{:S(2)}, u32[]{:S(2)}) collective-permute-start(bf16[2,8,32,128]{3,2,1,0:T(8,128)(2,1)S(1)} %choose.4), channel_id=1, source_target_pairs={{0,4},{2,6},{4,0},{6,2},{8,12},{10,14},{12,8},{14,10},{16,20},{18,... | collective-permute-start | bytes 393224 | tf_op jit(solution)/shard_map/ppermute | solution.py:395
  24.0 5.7 %collective-permute-start.6 = (bf16[4,8,32,128]{3,2,1,0:T(8,128)(2,1)S(1)}, bf16[4,8,32,128]{3,2,1,0:T(8,128)(2,1)S(1)}, u32[]{:S(2)}, u32[]{:S(2)}) collective-permute-start(bf16[4,8,32,128]{3,2,1,0:T(8,128)(2,1)S(1)} %choose.6), channel_id=1, source_target_pairs={{0,2},{2,0},{4,6},{6,4},{8,10},{10,8},{12,14},{14,12},{16,18},{18,... | collective-permute-start | bytes 786440 | tf_op jit(solution)/shard_map/ppermute | solution.py:396
  27.6 2.9 %collective-permute-start.10 = (bf16[2,8,32,128]{3,2,1,0:T(8,128)(2,1)S(1)}, bf16[2,8,32,128]{3,2,1,0:T(8,128)(2,1)S(1)}, u32[]{:S(2)}, u32[]{:S(2)}) collective-permute-start(bf16[2,8,32,128]{3,2,1,0:T(8,128)(2,1)S(1)} %collective-permute-done.8.refs_4_), channel_id=1, source_target_pairs={{0,2},{2,0},{4,6},{6,4},{8,10},{10,8},{12,14},{14,12},{16,18},{18,... | collective-permute-start | bytes 393224 | tf_op jit(solution)/shard_map/ppermute | solution.py:409
  27.6 2.1 %collective-permute-start.7 = (bf16[4,8,32,128]{3,2,1,0:T(8,128)(2,1)S(1)}, bf16[4,8,32,128]{3,2,1,0:T(8,128)(2,1)S(1)}, u32[]{:S(2)}, u32[]{:S(2)}) collective-permute-start(bf16[4,8,32,128]{3,2,1,0:T(8,128)(2,1)S(1)} %choose.7), channel_id=1, source_target_pairs={{0,2},{2,0},{4,6},{6,4},{8,10},{10,8},{12,14},{14,12},{16,18},{18,... | collective-permute-start | bytes 786440 | tf_op jit(solution)/shard_map/ppermute | solution.py:396
  28.2 1.5 %collective-permute-start.9 = (bf16[4,8,32,128]{3,2,1,0:T(8,128)(2,1)S(1)}, bf16[4,8,32,128]{3,2,1,0:T(8,128)(2,1)S(1)}, u32[]{:S(2)}, u32[]{:S(2)}) collective-permute-start(bf16[4,8,32,128]{3,2,1,0:T(8,128)(2,1)S(1)} %collective-permute-done.4.refs_4_), channel_id=1, source_target_pairs={{0,2},{2,0},{4,6},{6,4},{8,10},{10,8},{12,14},{14,12},{16,18},{18,... | collective-permute-start | bytes 786440 | tf_op jit(solution)/shard_map/ppermute | solution.py:398
  29.0 1.5 %collective-permute-start.5 = (bf16[2,8,32,128]{3,2,1,0:T(8,128)(2,1)S(1)}, bf16[2,8,32,128]{3,2,1,0:T(8,128)(2,1)S(1)}, u32[]{:S(2)}, u32[]{:S(2)}) collective-permute-start(bf16[2,8,32,128]{3,2,1,0:T(8,128)(2,1)S(1)} %collective-permute-done.3.refs_3_), channel_id=1, source_target_pairs={{0,2},{2,0},{4,6},{6,4},{8,10},{10,8},{12,14},{14,12},{16,18},{18,... | collective-permute-start | bytes 393224 | tf_op jit(solution)/shard_map/ppermute | solution.py:411
